TPU v7x, 128 devices: a whole 4x4x4 slice. The times are simulated.
128 devices in a mesh: blk: 16 (over z, x_hi, core), grp: 8 (over x_lo, y).
Axes of the slice: x: 4 (x_hi: 2, x_lo: 2; x = x_hi * 2 + x_lo), y: 4, z: 4, core: 2. Of those that a mesh axis runs over, the one named last changes fastest.
Arguments:
- queries: bfloat16 [4096, 3584], P(('blk', 'grp')), may hold values from -8 to 8
- stored_documents: bfloat16 [16384, 3584], P('blk'), may hold values from -8 to 8
- positive: int32 [4096], P(('blk', 'grp')), may hold values from 0 to 16383, as said below
- last_hidden: bfloat16 [256, 3584], P(('blk', 'grp')), may hold values from -150 to 150
- norm_gain: float32 [3584], replicated, may hold values from 0.1 to 1.9
- gate_weight: bfloat16 [3584, 18944], P('grp', 'blk'), may hold values from -0.09375 to 0.09375
- up_weight: bfloat16 [3584, 18944], P('grp', 'blk'), may hold values from -0.09375 to 0.09375
- down_weight: bfloat16 [18944, 3584], P('blk', 'grp'), may hold values from -0.046875 to 0.046875
Outputs:
- losses: float32 [4096], P(('blk', 'grp'))
- passage_grads: float32 [16384, 3584], P(('blk', 'grp'))
- hidden_grads: float32 [256, 3584], P(('blk', 'grp'))
Inputs may be any that keep to these rules, and one draw needn't show every extreme that they name: No two queries share a positive passage.
All inputs are finite; a program needn't handle non-finite values.
Results may differ from a plain program's by a relative error of at most 0.019.
Values may be sent and summed in bfloat16 or wider, within the bound.
No kernel may reach another device: no remote copies, remote signals or barrier semaphores. Data moves between devices by JAX's collectives and lax.ppermute only.
A program may use at most 128 MiB of HBM per device.

v0:
```python
import jax
import jax.numpy as jnp
from jax import lax
from jax.sharding import PartitionSpec as P

sharpness_scale = 20.0
epsilon = 1e-06
contract_last = (((1,), (1,)), ((), ()))
contract_first = (((0,), (0,)), ((), ()))


def row_norm(hidden):
    hidden_f = hidden.astype(jnp.float32)
    inv_rms = lax.rsqrt(jnp.mean(hidden_f * hidden_f, axis=1, keepdims=True) + epsilon)
    return (hidden_f, inv_rms)


def swiglu_grads(act_grad, gate_value, up_value):
    gate_sigmoid = jax.nn.sigmoid(gate_value)
    up_grad = (act_grad * gate_value * gate_sigmoid).astype(jnp.bfloat16)
    gate_grad = (
        act_grad * up_value * gate_sigmoid * (1.0 + gate_value * (1.0 - gate_sigmoid))
    ).astype(jnp.bfloat16)
    return (up_grad, gate_grad)


def shards(
    queries, stored_documents, positive, last_hidden, norm_gain, gate_weight, up_weight, down_weight
):
    blk_pos = lax.axis_index("blk")
    shard_rows = stored_documents.shape[0]
    own_rows = queries.shape[0]
    first_col = blk_pos * shard_rows
    col_queries, col_pos = (
        lax.all_gather(queries, "blk", axis=0, tiled=True),
        lax.all_gather(positive, "blk", axis=0, tiled=True),
    )
    similarity_scores = sharpness_scale * lax.dot_general(
        col_queries, stored_documents, contract_last, preferred_element_type=jnp.float32
    )
    local_pos = col_pos - first_col
    slot_ids = lax.broadcasted_iota(jnp.int32, (1, shard_rows), 1)
    is_positive = slot_ids == local_pos[:, None]
    highest = jnp.max(similarity_scores, axis=1)
    summed = jnp.sum(jnp.exp(similarity_scores - highest[:, None]), axis=1)
    hit_logit = jnp.sum(jnp.where(is_positive, similarity_scores, 0.0), axis=1)
    row_top = lax.pmax(highest, "blk")
    row_total, pos_logit = lax.psum((summed * jnp.exp(highest - row_top), hit_logit), "blk")
    log_total = row_top + jnp.log(row_total)
    layer_parameters = (
        jnp.exp(similarity_scores - log_total[:, None]) - is_positive.astype(jnp.float32)
    ).astype(jnp.bfloat16)
    losses = lax.dynamic_slice_in_dim(log_total - pos_logit, blk_pos * own_rows, own_rows)
    query_grads = lax.psum_scatter(
        (
            sharpness_scale
            * jnp.dot(layer_parameters, stored_documents, preferred_element_type=jnp.float32)
        ).astype(jnp.bfloat16),
        "blk",
        scatter_dimension=0,
        tiled=True,
    ).astype(jnp.float32)
    passage_grads = lax.psum_scatter(
        (
            sharpness_scale
            * lax.dot_general(
                layer_parameters, col_queries, contract_first, preferred_element_type=jnp.float32
            )
        ).astype(jnp.bfloat16),
        "grp",
        scatter_dimension=0,
        tiled=True,
    ).astype(jnp.float32)
    sub_count = last_hidden.shape[0]
    cotangent = query_grads[:sub_count].astype(jnp.bfloat16)
    full_gate, full_up, full_down = (
        lax.all_gather(gate_weight, "grp", axis=0, tiled=True),
        lax.all_gather(up_weight, "grp", axis=0, tiled=True),
        lax.all_gather(down_weight, "grp", axis=1, tiled=True),
    )
    col_hidden, col_cotangent = (
        lax.all_gather(last_hidden, "blk", axis=0, tiled=True),
        lax.all_gather(cotangent, "blk", axis=0, tiled=True),
    )
    hidden_f, inv_rms = row_norm(col_hidden)
    normed = (hidden_f * inv_rms * norm_gain).astype(jnp.bfloat16)
    gate_value = jnp.dot(normed, full_gate, preferred_element_type=jnp.float32)
    up_value = jnp.dot(normed, full_up, preferred_element_type=jnp.float32)
    act_grad = lax.dot_general(
        col_cotangent, full_down, contract_last, preferred_element_type=jnp.float32
    )
    up_grad, gate_grad = swiglu_grads(act_grad, gate_value, up_value)
    from_gate = lax.dot_general(
        gate_grad, full_gate, contract_last, preferred_element_type=jnp.float32
    )
    from_up = lax.dot_general(up_grad, full_up, contract_last, preferred_element_type=jnp.float32)
    normed_grad = lax.psum_scatter(
        (from_gate + from_up).astype(jnp.bfloat16), "blk", scatter_dimension=0, tiled=True
    ).astype(jnp.float32)
    hidden_f, inv_rms = row_norm(last_hidden)
    scaled = normed_grad * norm_gain
    hidden_grads = (
        cotangent.astype(jnp.float32)
        + inv_rms * scaled
        - hidden_f
        * inv_rms
        * inv_rms
        * inv_rms
        * jnp.mean(hidden_f * scaled, axis=1, keepdims=True)
    )
    return (losses, passage_grads, hidden_grads)


def solution(mesh):
    return jax.shard_map(
        shards,
        mesh=mesh,
        in_specs=(
            P(("blk", "grp"), None),
            P("blk", None),
            P(("blk", "grp")),
            P(("blk", "grp"), None),
            P(),
            P("grp", "blk"),
            P("grp", "blk"),
            P("blk", "grp"),
        ),
        out_specs=(P(("blk", "grp")), P(("blk", "grp"), None), P(("blk", "grp"), None)),
        check_vma=False,
    )
```

profile of v0, /device:TPU:1, one launch (start us, length us, event | category | flops | bytes accessed | tf_op | source)
XLA Modules:
  0.0 672.5 jit_solution(18433338961616382478)
XLA Ops:
  8.0 0.7 all-gather.7.cloned.1.call-update
  8.8 1.3 fusion.20
  10.8 0.9 dynamic-update-slice
  11.6 13.5 %all-reduce = s32[512]{0:T(512)S(1)} all-reduce(s32[512]{0:T(512)S(1)} %dynamic-update-slice), channel_id=1, replica_groups=mesh['blk'=16,'grp'=8] {'blk'}, use_global_device_ids=true, to_apply=%add | all-reduce | flops 512 | bytes 4096
  25.2 42.9 %all-gather.7.cloned.1.call-done = bf16[512,3584]{1,0:T(8,128)(2,1)} async-done(((bf16[32,3584]{1,0:T(8,128)(2,1)}), bf16[512,3584]{1,0:T(8,128)(2,1)}) %all-gather.7.cloned.1.call-update) | async-done | bytes 3670032 | tf_op jit(solution)/shard_map/all_gather | solution.py:35
  68.0 7.5 %multiply_reduce_fusion = (f32[512]{0:T(512)S(1)}, f32[512,1024]{1,0:T(8,128)S(1)}) fusion(bf16[512,3584]{1,0:T(8,128)(2,1)} %all-gather.7.cloned.1.call-done, bf16[1024,3584]{1,0:T(8,128)(2,1)} %param.9), kind=kOutput, calls=%fused_computation.12 | convolution fusion | flops 3759144448 | bytes 13109248 | tf_op jit(solution)/shard_map/dot_general | solution.py:38
  75.6 32.8 %pmax.7 = f32[512]{0:T(512)S(1)} all-reduce(f32[512]{0:T(512)S(1)} %get-tuple-element.13), channel_id=1, replica_groups=mesh['blk'=16,'grp'=8] {'blk'}, use_global_device_ids=true, to_apply=%region_1.0 | all-reduce | flops 512 | bytes 4096 | tf_op jit(solution)/shard_map/pmax | solution.py:47
  108.3 0.9 select_reduce_fusion
  109.2 34.8 %all-reduce.2 = (f32[512]{0:T(512)S(1)}, f32[512]{0:T(512)S(1)}) all-reduce(f32[512]{0:T(512)S(1)} %exponential_multiply_fusion, f32[512]{0:T(512)S(1)} %get-tuple-element.3), channel_id=1, replica_groups=mesh['blk'=16,'grp'=8] {'blk'}, use_global_device_ids=true, to_apply=%region_3.4 | all-reduce | flops 1024 | bytes 8192 | tf_op jit(solution)/shard_map/psum | solution.py:48
  144.0 8.9 %multiply_convert_fusion.1 = bf16[512,3584]{1,0:T(8,128)(2,1)} fusion(bf16[1024,3584]{1,0:T(8,128)(2,1)} %param.9, f32[512,1024]{1,0:T(8,128)S(1)} %get-tuple-element.14, f32[512]{0:T(512)S(1)} %get-tuple-element.10, s32[512]{0:T(512)S(1)} %broadcast_subtract_fusion), kind=kOutput, calls=%fused_computation.1 | convolution fusion | flops 3764912128 | bytes 13111296 | tf_op jit(solution)/shard_map/dot_general | solution.py:57
  153.0 0.5 all-gather.9.cloned.1.call-update
  153.6 0.5 all-gather.13.cloned.1.call-update
  154.2 0.5 all-gather.11.cloned.1.call-update
  154.8 21.3 %all-gather.1 = bf16[16,2,3584]{2,1,0:T(2,128)(2,1)S(1)} all-gather(bf16[1,2,3584]{2,1,0:T(2,128)(2,1)S(1)} %bitcast.15), channel_id=1, replica_groups=mesh['blk'=16,'grp'=8] {'blk'}, dimensions={0}, use_global_device_ids=true | all-gather | bytes 243712 | tf_op jit(solution)/shard_map/all_gather | solution.py:82
  176.2 0.1 multiply_reduce_fusion.1
  176.3 67.0 %reduce-scatter.5.cloned.1.call-done = bf16[32,3584]{1,0:T(8,128)(2,1)} async-done(((bf16[512,3584]{1,0:T(8,128)(2,1)}), bf16[32,3584]{1,0:T(8,128)(2,1)}) %reduce-scatter.5.cloned.1.call-update) | async-done | bytes 229392 | tf_op jit(solution)/shard_map/reduce_scatter | solution.py:54
  243.3 0.8 slice_bitcast_fusion
  244.1 23.2 %all-gather = bf16[16,2,3584]{2,1,0:T(2,128)(2,1)S(1)} all-gather(bf16[1,2,3584]{2,1,0:T(2,128)(2,1)S(1)} %slice_bitcast_fusion), channel_id=1, replica_groups=mesh['blk'=16,'grp'=8] {'blk'}, dimensions={0}, use_global_device_ids=true | all-gather | bytes 243712 | tf_op jit(solution)/shard_map/all_gather | solution.py:83
  267.3 0.1 reshape.34
  267.4 5.3 fusion.21
  272.7 93.3 %all-gather.13.cloned.1.call-done = bf16[3584,1184]{1,0:T(8,128)(2,1)} async-done(((bf16[448,1184]{1,0:T(8,128)(2,1)}), bf16[3584,1184]{1,0:T(8,128)(2,1)}) %all-gather.13.cloned.1.call-update) | async-done | bytes 8486928 | tf_op jit(solution)/shard_map/all_gather | solution.py:77
  366.0 5.3 fusion.18
  371.3 94.2 %all-gather.11.cloned.1.call-done = bf16[3584,1184]{1,0:T(8,128)(2,1)} async-done(((bf16[448,1184]{1,0:T(8,128)(2,1)}), bf16[3584,1184]{1,0:T(8,128)(2,1)}) %all-gather.11.cloned.1.call-update) | async-done | bytes 8486928 | tf_op jit(solution)/shard_map/all_gather | solution.py:78
  465.5 10.6 %fusion.4 = f32[32,3584]{1,0:T(8,128)S(1)} fusion(bf16[3584,1184]{1,0:T(8,128)(2,1)} %all-gather.13.cloned.1.call-done, f32[32,1184]{1,0:T(8,128)S(1)} %fusion.21, bf16[3584,1184]{1,0:T(8,128)(2,1)} %all-gather.11.cloned.1.call-done, f32[32,1184]{1,0:T(8,128)S(1)} %fusion.18, f32[32,3584]{1,0:T(8,128)S(1)} %reshape.37, f32[3584]{0:T(1024)S(1)} %copy-done, ...), kind=kOutput, calls=%fused_computation.13 | convolution fusion | flops 543885312 | bytes 18208896 | tf_op jit(solution)/shard_map/dot_general | solution.py:93
  476.1 7.0 %fusion = bf16[32,3584]{1,0:T(8,128)(2,1)} fusion(f32[32,3584]{1,0:T(8,128)S(1)} %fusion.4, bf16[3584,1184]{1,0:T(8,128)(2,1)} %all-gather.11.cloned.1.call-done, f32[32,1184]{1,0:T(8,128)S(1)} %fusion.21, f32[32,1184]{1,0:T(8,128)S(1)} %fusion.18), kind=kOutput, calls=%fused_computation.3 | convolution fusion | flops 272037888 | bytes 9478144 | tf_op jit(solution)/shard_map/dot_general | solution.py:96
  483.2 0.2 reduce-scatter.3.cloned.1.call-start
  483.4 8.4 %multiply_convert_fusion = bf16[1024,3584]{1,0:T(8,128)(2,1)} fusion(bf16[512,3584]{1,0:T(8,128)(2,1)} %all-gather.7.cloned.1.call-done, f32[512,1024]{1,0:T(8,128)S(1)} %get-tuple-element.14, f32[512]{0:T(512)S(1)} %get-tuple-element.10, s32[512]{0:T(512)S(1)} %broadcast_subtract_fusion), kind=kOutput, calls=%fused_computation | convolution fusion | flops 3768582144 | bytes 13111296 | tf_op jit(solution)/shard_map/dot_general | solution.py:66
  492.5 0.6 dynamic_slice.3
  493.1 166.8 %all-reduce.5.cloned.1.call-done = bf16[32,3584]{1,0:T(8,128)(2,1)} async-done(((bf16[32,3584]{1,0:T(8,128)(2,1)}), bf16[32,3584]{1,0:T(8,128)(2,1)}) %all-reduce.5.cloned.1.call-update) | async-done | bytes 229392
  659.9 1.0 fusion.10
  660.9 1.6 fusion.14
  662.5 2.6 convert_element_type.44
  (22 shorter events, 0.4 us)
Async XLA Ops:
  8.0 60.0 %all-gather.7.cloned.1.call-start = ((), (), s32[]{:S(2)}) async-start(), calls=%async_computation.2 | async-start | bytes 3899392 | tf_op jit(solution)/shard_map/all_gather | solution.py:35
  8.7 234.5 %reduce-scatter.5.cloned.1.call-start = ((), (), s32[]{:S(2)}) async-start(), calls=%async_computation.4 | async-start | bytes 3899392 | tf_op jit(solution)/shard_map/reduce_scatter | solution.py:54
  152.9 1.8 copy-start.1
  153.0 114.5 %all-gather.9.cloned.1.call-start = ((), (), s32[]{:S(2)}) async-start(), calls=%async_computation.5 | async-start | bytes 10321920 | tf_op jit(solution)/shard_map/all_gather | solution.py:79
  153.5 212.4 %all-gather.13.cloned.1.call-start = ((), (), s32[]{:S(2)}) async-start(), calls=%async_computation.7 | async-start | bytes 10321920 | tf_op jit(solution)/shard_map/all_gather | solution.py:77
  154.1 311.4 %all-gather.11.cloned.1.call-start = ((), (), s32[]{:S(2)}) async-start(), calls=%async_computation.6 | async-start | bytes 10321920 | tf_op jit(solution)/shard_map/all_gather | solution.py:78
  154.7 505.2 %all-reduce.5.cloned.1.call-start = ((), (), s32[]{:S(2)}) async-start(), calls=%async_computation.8 | async-start | bytes 458752
  267.4 98.6 %copy-start = (f32[3584]{0:T(1024)S(1)}, f32[3584]{0:T(1024)}, u32[]{:S(2)}) copy-start(f32[3584]{0:T(1024)} %param.12) | copy-start | bytes 43012
  483.2 179.3 %reduce-scatter.3.cloned.1.call-start = ((), (), s32[]{:S(2)}) async-start(), calls=%async_computation.3 | async-start | bytes 8257536 | tf_op jit(solution)/shard_map/reduce_scatter | solution.py:63
Sparse Core Ops, SparseCore 0:
  11.3 56.6 all-gather.6
  153.1 90.1 reduce-scatter.4
  483.3 176.5 all-reduce.4
Sparse Core Ops, SparseCore 1:
  155.1 111.6 all-gather.8
  268.3 97.6 all-gather.12
  367.5 98.0 all-gather.10
  492.0 82.7 reduce-scatter.2
where the time goes:
time: 673 us; the launch traced here: 672 us
  waiting for transfers between devices  466 us (69%)
  blocking collectives  126 us (19%)
  matrix products  53.1 us (8%)
  between operations  16.8 us (2%)
    unnamed x8, waiting for transfers between devices  169 us
    all_gather x1, waiting for transfers between devices, shards(): lax.all_gather(up_weight, 'grp', axis=0, tiled=True)  94.2 us
    all_gather x1, waiting for transfers between devices, shards(): lax.all_gather(gate_weight, 'grp', axis=0, tiled=True)  93.3 us
    reduce_scatter x1, waiting for transfers between devices, shards(): lax.psum_scatter((sharpness_scale * jnp.dot(layer_parameters, stored_docu...  67 us
    all_gather x1, waiting for transfers between devices, shards(): lax.all_gather(queries, 'blk', axis=0, tiled=True)  42.9 us
    psum x1, blocking collectives, shards(): lax.psum((summed * jnp.exp(highest - row_top), hit_logit), 'blk')  34.8 us
    pmax x1, blocking collectives, shards(): row_top = lax.pmax(highest, 'blk')  32.8 us
    all_gather x1, blocking collectives, shards(): lax.all_gather(cotangent, 'blk', axis=0, tiled=True)  23.2 us
  transfers between devices with their start and end apart: 7, of which 5 were waited for; matrix products, arithmetic and copies ran while one was open for 4% of the time, Pallas kernels for 0%

commit v1 on v0

v1 whole, which is shorter than its diff:
```python
import functools

import jax
import jax.numpy as jnp
from jax import lax
from jax.experimental import pallas as pl
from jax.experimental.pallas import tpu as pltpu
from jax.sharding import PartitionSpec as P

sharpness_scale = 20.0
epsilon = 1e-06
contract_last = (((1,), (1,)), ((), ()))
Z, X, C = 4, 2, 2
N_BLK, N_GRP = 16, 8
POS_LANES = 128
POS_BASE = 128
BIG_VMEM = 56 * 1024 * 1024


def blk_shift(dz, dx, dc):
    pairs = []
    for s in range(N_BLK):
        z, x, c = s // (X * C), s // C % X, s % C
        pairs.append((s, ((z + dz) % Z * X + (x + dx) % X) * C + (c + dc) % C))
    return pairs


def whole(shape):
    return pl.BlockSpec(shape, lambda *_: (0,) * len(shape))


def vmem(count):
    return [pl.BlockSpec(memory_space=pltpu.VMEM)] * count


def gather_column(block):
    send = lambda v, *shift: lax.ppermute(v, "blk", blk_shift(*shift))
    half = block.shape[0] // 2
    below = send(block, 1, 0, 0)
    above = send(block, -1, 0, 0)
    across = send(block, 0, 1, 0)
    across_below = send(across, 1, 0, 0)
    far = send(above, -1, 0, 0)
    across_above = send(above, 0, 1, 0)
    across_far_a = send(across_below[:half], 1, 0, 0)
    across_far_b = send(far[half:], 0, 1, 0)
    own = [
        (block, 0, 0),
        (below, -1, 0),
        (above, 1, 0),
        (across, 0, 1),
        (across_below, -1, 1),
        (far, 2, 0),
        (across_above, 1, 1),
        (across_far_a, 2, 1),
        (across_far_b, 2, 1),
    ]
    pieces = [(v, dz, dx, 0) for v, dz, dx in own]
    pieces += [(send(v, 0, 0, 1), dz, dx, 1) for v, dz, dx in own]
    return pieces


def score_kernel(starts, tile, place_ref, *refs):
    n = len(starts)
    blocks, doc_ref = refs[:n], refs[n]
    score_ref, query_ref, stat_ref, pos_ref, pos_col = refs[n + 1 :]
    step = pl.program_id(0)
    dim = query_ref.shape[1]

    @pl.when(step == 0)
    def _():
        for k, block in enumerate(blocks):
            rows = block.shape[0]
            at = pl.multiple_of(place_ref[k], 16)
            query_ref[pl.ds(at, rows), :] = block[:, :dim]
            pos_col[pl.ds(at, rows), :] = block[:, dim:]
        lane = lax.broadcasted_iota(jnp.int32, (8, POS_LANES), 1)
        line = lax.broadcasted_iota(jnp.int32, (8, POS_LANES), 0)
        pick = jnp.where(lane == line, 1.0, 0.0).astype(jnp.bfloat16)
        parts = lax.dot_general(pick, pos_col[...], contract_last, preferred_element_type=jnp.float32)
        pos_ref[...] = (parts[0:1] * POS_BASE + parts[1:2]).astype(jnp.int32)
        stat_ref[...] = jnp.zeros_like(stat_ref)
        stat_ref[0:1] = jnp.full_like(stat_ref[0:1], -jnp.inf)

    scores = sharpness_scale * lax.dot_general(
        doc_ref[...], query_ref[...], contract_last, preferred_element_type=jnp.float32
    )
    score_ref[...] = scores
    top_before = stat_ref[0:1]
    top = jnp.maximum(top_before, jnp.max(scores, axis=0, keepdims=True))
    slot = place_ref[n] + step * tile + lax.broadcasted_iota(jnp.int32, scores.shape, 0)
    hit = jnp.where(slot == pos_ref[...], scores, 0.0)
    stat_ref[0:1] = top
    stat_ref[1:2] = stat_ref[1:2] * jnp.exp(top_before - top) + jnp.sum(
        jnp.exp(scores - top), axis=0, keepdims=True
    )
    stat_ref[2:3] = stat_ref[2:3] + jnp.sum(hit, axis=0, keepdims=True)


def column_scores(pieces, docs, row_places, first_passage, dim):
    shard_rows = docs.shape[0]
    cols = 512
    tile = 256
    places = jnp.concatenate([row_places, first_passage[None]])
    return pl.pallas_call(
        functools.partial(score_kernel, tuple(range(len(pieces))), tile),
        grid_spec=pltpu.PrefetchScalarGridSpec(
            num_scalar_prefetch=1,
            grid=(shard_rows // tile,),
            in_specs=[whole(v.shape) for v in pieces]
            + [pl.BlockSpec((tile, dim), lambda i, _: (i, 0))],
            out_specs=[
                pl.BlockSpec((tile, cols), lambda i, _: (i, 0)),
                whole((cols, dim)),
                whole((8, cols)),
                whole((1, cols)),
            ],
            scratch_shapes=[pltpu.VMEM((cols, POS_LANES), jnp.bfloat16)],
        ),
        out_shape=[
            jax.ShapeDtypeStruct((shard_rows, cols), jnp.float32),
            jax.ShapeDtypeStruct((cols, dim), jnp.bfloat16),
            jax.ShapeDtypeStruct((8, cols), jnp.float32),
            jax.ShapeDtypeStruct((1, cols), jnp.int32),
        ],
        compiler_params=pltpu.CompilerParams(vmem_limit_bytes=BIG_VMEM),
        cost_estimate=pl.CostEstimate(
            flops=2 * shard_rows * cols * dim,
            bytes_accessed=2 * (shard_rows + 2 * cols) * dim,
            transcendentals=shard_rows * cols,
        ),
        name="column_scores",
    )(places, *pieces, docs)


def weight_kernel(tile, rows, sub, first_ref, score_ref, stats_ref, pos_ref, doc_ref, weight_ref, grad_ref, loss_ref, total, acc):
    step = pl.program_id(0)
    cols = score_ref.shape[1]

    @pl.when(step == 0)
    def _():
        tops = stats_ref[:, 0, :]
        top = jnp.max(tops, axis=0, keepdims=True)
        summed = jnp.sum(stats_ref[:, 1, :] * jnp.exp(tops - top), axis=0, keepdims=True)
        total[...] = top + jnp.log(summed)
        loss_ref[...] = total[...] - jnp.sum(stats_ref[:, 2, :], axis=0, keepdims=True)
        acc[...] = jnp.zeros_like(acc)

    slot = first_ref[0] + step * tile + lax.broadcasted_iota(jnp.int32, score_ref.shape, 0)
    onehot = jnp.where(slot == pos_ref[...], 1.0, 0.0)
    weights = (jnp.exp(score_ref[...] - total[...]) - onehot).astype(jnp.bfloat16)
    weight_ref[...] = weights
    line = lax.broadcasted_iota(jnp.int32, (acc.shape[0], cols), 0)
    lane = lax.broadcasted_iota(jnp.int32, (acc.shape[0], cols), 1)
    pick = jnp.where(lane == line // sub * rows + line % sub, 1.0, 0.0).astype(jnp.bfloat16)
    picked = lax.dot_general(pick, weights, contract_last, preferred_element_type=jnp.float32).astype(jnp.bfloat16)
    acc[...] += jnp.dot(picked, doc_ref[...], preferred_element_type=jnp.float32)

    @pl.when(step == pl.num_programs(0) - 1)
    def _():
        grads = (sharpness_scale * acc[...]).astype(jnp.bfloat16)
        width = grad_ref.shape[2]
        for g in range(grad_ref.shape[0]):
            grad_ref[g] = grads[:, g * width : (g + 1) * width]


def column_weights(scores, stats, positives, docs, first_passage, rows, sub):
    shard_rows, cols = scores.shape
    dim = docs.shape[1]
    tile = 256
    lines = cols // rows * sub
    return pl.pallas_call(
        functools.partial(weight_kernel, tile, rows, sub),
        grid_spec=pltpu.PrefetchScalarGridSpec(
            num_scalar_prefetch=1,
            grid=(shard_rows // tile,),
            in_specs=[
                pl.BlockSpec((tile, cols), lambda i, _: (i, 0)),
                whole(stats.shape),
                whole((1, cols)),
                pl.BlockSpec((tile, dim), lambda i, _: (i, 0)),
            ],
            out_specs=[
                pl.BlockSpec((tile, cols), lambda i, _: (i, 0)),
                whole((N_GRP, lines, dim // N_GRP)),
                whole((1, cols)),
            ],
            scratch_shapes=[
                pltpu.VMEM((1, cols), jnp.float32),
                pltpu.VMEM((lines, dim), jnp.float32),
            ],
        ),
        out_shape=[
            jax.ShapeDtypeStruct((shard_rows, cols), jnp.bfloat16),
            jax.ShapeDtypeStruct((N_GRP, lines, dim // N_GRP), jnp.bfloat16),
            jax.ShapeDtypeStruct((1, cols), jnp.float32),
        ],
        compiler_params=pltpu.CompilerParams(vmem_limit_bytes=BIG_VMEM),
        cost_estimate=pl.CostEstimate(
            flops=2 * shard_rows * (cols + dim) * lines,
            bytes_accessed=2 * shard_rows * dim,
            transcendentals=shard_rows * cols,
        ),
        name="column_weights",
    )(first_passage[None], scores, stats, positives, docs)


def everyone(value, axis):
    size = N_BLK if axis == "blk" else N_GRP
    return lax.all_to_all(
        jnp.broadcast_to(value[None], (size, *value.shape)), axis, 0, 0, tiled=True
    )


def reduce_rows(partial):
    parts = partial.astype(jnp.bfloat16).reshape(N_GRP, -1, partial.shape[1])
    got = lax.all_to_all(parts, "grp", 0, 0, tiled=True)
    return jnp.sum(got.astype(jnp.float32), axis=0)


def shards(
    queries, stored_documents, positive, last_hidden, norm_gain, gate_weight, up_weight, down_weight
):
    blk_pos = lax.axis_index("blk")
    z, x, c = blk_pos // (X * C), blk_pos // C % X, blk_pos % C
    shard_rows, dim = stored_documents.shape
    own_rows = queries.shape[0]
    sub = last_hidden.shape[0]
    part = dim // N_GRP
    first_passage = blk_pos * shard_rows

    lane = lax.broadcasted_iota(jnp.int32, (own_rows, POS_LANES), 1)
    coded = jnp.where(
        lane == 0,
        (positive // POS_BASE)[:, None],
        jnp.where(lane == 1, (positive % POS_BASE)[:, None], 0),
    )
    block = jnp.concatenate([queries, coded.astype(jnp.bfloat16)], axis=1)
    pieces = gather_column(block)
    row_places = []
    seen = set()
    for _, dz, dx, dc in pieces:
        place = (((z + dz) % Z * X + (x + dx) % X) * C + (c + dc) % C) * own_rows
        row_places.append(place + (own_rows // 2 if (dz, dx, dc) in seen else 0))
        seen.add((dz, dx, dc))
    row_places = jnp.stack(row_places).astype(jnp.int32)
    scores, col_queries, stats, col_pos = column_scores(
        [v for v, *_ in pieces], stored_documents, row_places, first_passage, dim
    )

    hidden_f = last_hidden.astype(jnp.float32)
    inv_rms = lax.rsqrt(jnp.mean(hidden_f * hidden_f, axis=1, keepdims=True) + epsilon)
    normed = (hidden_f * inv_rms * norm_gain).astype(jnp.bfloat16)
    normed_parts = normed.reshape(sub, N_GRP, part).transpose(1, 0, 2)
    normed_cols = lax.all_to_all(
        jnp.broadcast_to(normed_parts[None], (N_BLK, N_GRP, sub, part)).reshape(-1, sub, part),
        ("blk", "grp"),
        0,
        0,
        tiled=True,
    ).reshape(-1, part)
    gate_part = jnp.dot(normed_cols, gate_weight, preferred_element_type=jnp.float32)
    up_part = jnp.dot(normed_cols, up_weight, preferred_element_type=jnp.float32)
    forward = reduce_rows(jnp.concatenate([gate_part, up_part], axis=1)).astype(jnp.bfloat16)
    hidden_units = gate_weight.shape[1]
    forward = everyone(forward, "grp").reshape(-1, 2 * hidden_units).astype(jnp.float32)
    gate_value, up_value = forward[:, :hidden_units], forward[:, hidden_units:]

    weights, sub_grads, loss_row = column_weights(
        scores, everyone(stats, "blk"), col_pos, stored_documents, first_passage, own_rows, sub
    )
    losses = lax.dynamic_slice_in_dim(loss_row[0], blk_pos * own_rows, own_rows)
    got = lax.all_to_all(
        sub_grads.reshape(N_GRP * N_BLK, sub, part), ("grp", "blk"), 0, 0, tiled=True
    )
    cot_rows = jnp.sum(got.reshape(N_GRP, N_BLK, sub, part).astype(jnp.float32), axis=1)
    cot_rows = cot_rows.astype(jnp.bfloat16)

    passage_part = (
        sharpness_scale * jnp.dot(weights, col_queries, preferred_element_type=jnp.float32)
    ).astype(jnp.bfloat16)
    passage_got = lax.all_to_all(
        passage_part.reshape(N_GRP, -1, dim), "grp", 0, 0, tiled=True
    )
    passage_grads = jnp.sum(passage_got.astype(jnp.float32), axis=0)

    cot_cols = everyone(cot_rows.reshape(-1, part), "blk").reshape(-1, part)
    act_part = lax.dot_general(
        cot_cols, down_weight, contract_last, preferred_element_type=jnp.float32
    )
    act_rows = reduce_rows(act_part).astype(jnp.bfloat16)
    act_grad = everyone(act_rows, "grp").reshape(-1, hidden_units).astype(jnp.float32)
    gate_sigmoid = jax.nn.sigmoid(gate_value)
    up_grad = (act_grad * gate_value * gate_sigmoid).astype(jnp.bfloat16)
    gate_grad = (
        act_grad * up_value * gate_sigmoid * (1.0 + gate_value * (1.0 - gate_sigmoid))
    ).astype(jnp.bfloat16)
    from_gate = lax.dot_general(
        gate_grad, gate_weight, contract_last, preferred_element_type=jnp.float32
    )
    from_up = lax.dot_general(up_grad, up_weight, contract_last, preferred_element_type=jnp.float32)
    normed_part = (from_gate + from_up).astype(jnp.bfloat16).reshape(N_BLK, N_GRP, sub, part)
    cot_sent = cot_cols.reshape(normed_part.shape)
    back = lax.all_to_all(
        jnp.concatenate([normed_part, cot_sent], axis=2).reshape(-1, 2 * sub, part),
        ("blk", "grp"),
        0,
        0,
        tiled=True,
    ).reshape(N_BLK, N_GRP, 2 * sub, part)
    normed_grad = jnp.sum(back[:, :, :sub].astype(jnp.float32), axis=0)
    normed_grad = normed_grad.transpose(1, 0, 2).reshape(sub, dim)
    cotangent = back[0, :, sub:].transpose(1, 0, 2).reshape(sub, dim).astype(jnp.float32)
    scaled = normed_grad * norm_gain
    hidden_grads = (
        cotangent
        + inv_rms * scaled
        - hidden_f
        * inv_rms
        * inv_rms
        * inv_rms
        * jnp.mean(hidden_f * scaled, axis=1, keepdims=True)
    )
    return (losses, passage_grads, hidden_grads)


def solution(mesh):
    return jax.shard_map(
        shards,
        mesh=mesh,
        in_specs=(
            P(("blk", "grp"), None),
            P("blk", None),
            P(("blk", "grp")),
            P(("blk", "grp"), None),
            P(),
            P("grp", "blk"),
            P("grp", "blk"),
            P("blk", "grp"),
        ),
        out_specs=(P(("blk", "grp")), P(("blk", "grp"), None), P(("blk", "grp"), None)),
        check_vma=False,
    )
```

time: 673 us -> 312 us (0.46)
  waiting for transfers between devices: 466 us -> 164 us
  blocking collectives: 126 us -> 0 us
  starting transfers between devices: 0.47 us -> 72.1 us
  matrix products: 53.1 us -> 13.7 us
  Pallas kernels: 0 us -> 18 us
  local copies, waits for them, and re-layouts: 3.76 us -> 20 us
  between operations: 16.8 us -> 1.02 us
  other arithmetic: 6.22 us -> 21.1 us
    all_gather x4 -> x0, waiting for transfers between devices: 230 us -> none  [the longest x1 94.2 us: shards(): lax.all_gather(up_weight, 'grp', axis=0, tiled=True)]
    unnamed x8 -> x0, waiting for transfers between devices: 169 us -> none
    all_to_all x0 -> x10, waiting for transfers between devices: none -> 161 us  [the longest x1 79.8 us: shards(): lax.all_to_all(passage_part.reshape(N_GRP, -1, dim), 'grp', 0, 0, tiled=T...]
    reduce_scatter x2 -> x0, waiting for transfers between devices: 67 us -> none  [the longest x1 67 us: shards(): lax.psum_scatter((sharpness_scale * jnp.dot(layer_parameters, stored_docu...]
    all_to_all x0 -> x10, starting transfers between devices: none -> 47.2 us  [the longest x4 17.1 us: everyone(): lax.all_to_all(jnp.broadcast_to(value[None], (size, *value.shape)), axis,...]
    all_gather x2 -> x0, blocking collectives: 44.5 us -> none  [the longest x1 23.2 us: shards(): lax.all_gather(cotangent, 'blk', axis=0, tiled=True)]
    dot_general x7 -> x6, matrix products: 53.1 us -> 13.7 us  [the longest x1 8.02 us: shards(): jnp.dot(weights, col_queries, preferred_element_type=jnp.float32)]
    psum x1 -> x0, blocking collectives: 34.8 us -> none  [shards(): lax.psum((summed * jnp.exp(highest - row_top), hit_logit), 'blk')]
  transfers between devices with their start and end apart: 7 -> 27, of which waited for: 5 -> 13; matrix products, arithmetic and copies ran while one was open for 4% -> 10% of each run, Pallas kernels for 0% -> 0%
where the time goes in v1:
time: 312 us; the launch traced here: 310 us
  waiting for transfers between devices  164 us (53%)
  starting transfers between devices  72.1 us (23%)
  other arithmetic  21.1 us (7%)
  local copies, waits for them, and re-layouts  20 us (6%)
  Pallas kernels  18 us (6%)
  matrix products  13.7 us (4%)
    all_to_all x1, waiting for transfers between devices, shards(): lax.all_to_all(passage_part.reshape(N_GRP, -1, dim), 'grp', 0, 0, tiled=T...  79.8 us
    all_to_all x4, waiting for transfers between devices, everyone(): lax.all_to_all(jnp.broadcast_to(value[None], (size, *value.shape)), axis,...  35.6 us
    ppermute x17, starting transfers between devices, gather_column(): send = lambda v, *shift: lax.ppermute(v, 'blk', blk_shift(*shift))  24.9 us
    all_to_all x2, waiting for transfers between devices, reduce_rows(): got = lax.all_to_all(parts, 'grp', 0, 0, tiled=True)  20.3 us
    all_to_all x4, starting transfers between devices, everyone(): lax.all_to_all(jnp.broadcast_to(value[None], (size, *value.shape)), axis,...  17.1 us
    pallas_call x1, Pallas kernels, column_scores(): pl.pallas_call(functools.partial(score_kernel, tuple(range(len(pieces))),...  11.2 us
    all_to_all x1, waiting for transfers between devices, shards(): lax.all_to_all(sub_grads.reshape(N_GRP * N_BLK, sub, part), ('grp', 'blk'...  9.98 us
    all_to_all x1, waiting for transfers between devices, shards(): lax.all_to_all(jnp.broadcast_to(normed_parts[None], (N_BLK, N_GRP, sub, p...  9.32 us
  transfers between devices with their start and end apart: 27, of which 13 were waited for; matrix products, arithmetic and copies ran while one was open for 10% of the time, Pallas kernels for 0%

profile of v1, /device:TPU:1, one launch (start us, length us, event | category | flops | bytes accessed | tf_op | source)
XLA Modules:
  0.0 310.2 jit_solution(4085160623217001872)
XLA Ops:
  2.5 3.7 %collective-permute-start.2 = (bf16[32,3712]{1,0:T(8,128)(2,1)S(1)}, bf16[32,3712]{1,0:T(8,128)(2,1)S(1)}, u32[]{:S(2)}, u32[]{:S(2)}) collective-permute-start(bf16[32,3712]{1,0:T(8,128)(2,1)S(1)} %pad_maximum_fusion.2.refs_0_), channel_id=1, source_target_pairs={{0,16},{8,24},{16,0},{24,8},{32,48},{40,56},{48,32},{56,40},{64,80... | collective-permute-start | bytes 712712 | tf_op jit(solution)/shard_map/ppermute | solution.py:37
  6.1 3.8 %collective-permute-start.1 = (bf16[32,3712]{1,0:T(8,128)(2,1)S(1)}, bf16[32,3712]{1,0:T(8,128)(2,1)S(1)}, u32[]{:S(2)}, u32[]{:S(2)}) collective-permute-start(bf16[32,3712]{1,0:T(8,128)(2,1)S(1)} %pad_maximum_fusion.2.refs_0_), channel_id=1, source_target_pairs={{0,96},{8,104},{16,112},{24,120},{32,0},{40,8},{48,16},{56,24},{64... | collective-permute-start | bytes 712712 | tf_op jit(solution)/shard_map/ppermute | solution.py:37
  14.0 3.4 %collective-permute-start.4 = (bf16[32,3712]{1,0:T(8,128)(2,1)S(1)}, bf16[32,3712]{1,0:T(8,128)(2,1)}, u32[]{:S(2)}, u32[]{:S(2)}) collective-permute-start(bf16[32,3712]{1,0:T(8,128)(2,1)S(1)} %collective-permute-done.1.refs_2_), channel_id=1, source_target_pairs={{0,96},{8,104},{16,112},{24,120},{32,0},{40,8},{48,16},{56,24},{64... | collective-permute-start | bytes 712712 | tf_op jit(solution)/shard_map/ppermute | solution.py:37
  22.7 2.5 collective-permute-start.9
  28.0 2.7 collective-permute-start.7
  34.7 6.4 %all-to-all-start.6 = ((bf16[128,2,448]{2,1,0:T(2,128)(2,1)}), bf16[128,2,448]{2,1,0:T(2,128)(2,1)S(1)}, u32[]{:S(2)}, u32[]{:S(2)}) async-start(bf16[128,2,448]{2,1,0:T(2,128)(2,1)} %bitcast.26), calls=%async_computation.6 | async-start | bytes 524288 | tf_op jit(solution)/shard_map/all_to_all | solution.py:255
  43.1 9.3 %all-to-all-done.6 = bf16[128,2,448]{2,1,0:T(2,128)(2,1)S(1)} async-done(((bf16[128,2,448]{2,1,0:T(2,128)(2,1)}), bf16[128,2,448]{2,1,0:T(2,128)(2,1)S(1)}, u32[]{:S(2)}, u32[]{:S(2)}) %all-to-all-start.6) | async-done | bytes 229408 | tf_op jit(solution)/shard_map/all_to_all | solution.py:255
  53.4 11.2 %column_scores.1 = (f32[1024,512]{1,0:T(8,128)}, bf16[512,3584]{1,0:T(8,128)(2,1)}, f32[8,512]{1,0:T(8,128)}, s32[1,512]{1,0:T(1,128)}) custom-call(s32[19]{0:T(128)} %concatenate.19.place_ref, bf16[32,3712]{1,0:T(8,128)(2,1)} %copy-done.5, bf16[32,3712]{1,0:T(8,128)(2,1)} %copy-done.11, bf16[32,3712]{1,0:T(8,128)(2,1)} %copy-done.10, ...), custom_call_target="tpu_custom_call" | custom-call | flops 3758096384 | bytes 14680064 | tf_op jit(solution)/shard_map/column_scores/pallas_call | solution.py:105
  66.1 3.8 %all-to-all-start = ((f32[16,8,512]{2,1,0:T(8,128)}), f32[16,8,512]{2,1,0:T(8,128)S(1)}, u32[]{:S(2)}, u32[]{:S(2)}) async-start(f32[16,8,512]{2,1,0:T(8,128)} %broadcast_in_dim.35), calls=%async_computation | async-start | bytes 524288 | tf_op jit(solution)/shard_map/all_to_all | solution.py:210
  70.4 8.2 %all-to-all-done.stats_ref = f32[16,8,512]{2,1,0:T(8,128)S(1)} async-done(((f32[16,8,512]{2,1,0:T(8,128)}), f32[16,8,512]{2,1,0:T(8,128)S(1)}, u32[]{:S(2)}, u32[]{:S(2)}) %all-to-all-start) | async-done | bytes 262176 | tf_op jit(solution)/shard_map/all_to_all | solution.py:210
  79.3 6.8 %column_weights.1 = (bf16[1024,512]{1,0:T(8,128)(2,1)}, bf16[8,32,448]{2,1,0:T(8,128)(2,1)}, f32[1,512]{1,0:T(1,128)}) custom-call(s32[1]{0:T(128)} %bitcast.first_ref, f32[1024,512]{1,0:T(8,128)} %get-tuple-element.10.score_ref, f32[16,8,512]{2,1,0:T(8,128)} %copy-done.3, s32[1,512]{1,0:T(1,128)} %get-tuple-element.12.pos_ref, bf16[1024,3584]{1,0:T(8,128)(2,1)} %doc_ref.1), custom_call_target="tpu_custom_call" | custom-call | flops 268435456 | bytes 7340032 | tf_op jit(solution)/shard_map/column_weights/pallas_call | solution.py:172
  87.9 4.4 %all-to-all-start.2 = ((bf16[128,2,448]{2,1,0:T(2,128)(2,1)}), bf16[128,2,448]{2,1,0:T(2,128)(2,1)S(1)}, u32[]{:S(2)}, u32[]{:S(2)}) async-start(bf16[128,2,448]{2,1,0:T(2,128)(2,1)} %reshape.80), calls=%async_computation.2 | async-start | bytes 524288 | tf_op jit(solution)/shard_map/all_to_all | solution.py:273
  93.6 10.0 %all-to-all-done.2 = bf16[128,2,448]{2,1,0:T(2,128)(2,1)S(1)} async-done(((bf16[128,2,448]{2,1,0:T(2,128)(2,1)}), bf16[128,2,448]{2,1,0:T(2,128)(2,1)S(1)}, u32[]{:S(2)}, u32[]{:S(2)}) %all-to-all-start.2) | async-done | bytes 229408 | tf_op jit(solution)/shard_map/all_to_all | solution.py:273
  104.6 4.1 %all-to-all-start.3 = ((bf16[16,16,448]{2,1,0:T(8,128)(2,1)}), bf16[16,16,448]{2,1,0:T(8,128)(2,1)S(1)}, u32[]{:S(2)}, u32[]{:S(2)}) async-start(bf16[16,16,448]{2,1,0:T(8,128)(2,1)} %broadcast_in_dim.37), calls=%async_computation.3 | async-start | bytes 524288 | tf_op jit(solution)/shard_map/all_to_all | solution.py:210
  108.7 2.4 pad_maximum_fusion
  111.1 6.2 %all-to-all-done.3 = bf16[16,16,448]{2,1,0:T(8,128)(2,1)S(1)} async-done(((bf16[16,16,448]{2,1,0:T(8,128)(2,1)}), bf16[16,16,448]{2,1,0:T(8,128)(2,1)S(1)}, u32[]{:S(2)}, u32[]{:S(2)}) %all-to-all-start.3) | async-done | bytes 229408 | tf_op jit(solution)/shard_map/all_to_all | solution.py:210
  118.1 3.7 %all-to-all-start.7 = ((bf16[8,32,2368]{2,1,0:T(8,128)(2,1)}), bf16[8,32,2368]{2,1,0:T(8,128)(2,1)S(1)}, u32[]{:S(2)}, u32[]{:S(2)}) async-start(bf16[8,32,2368]{2,1,0:T(8,128)(2,1)} %pad_maximum_fusion), calls=%async_computation.7 | async-start | bytes 2490368 | tf_op jit(solution)/shard_map/all_to_all | solution.py:217
  121.8 2.8 convolution_convert_fusion.2
  126.8 11.7 %all-to-all-done.7 = bf16[8,32,2368]{2,1,0:T(8,128)(2,1)S(1)} async-done(((bf16[8,32,2368]{2,1,0:T(8,128)(2,1)}), bf16[8,32,2368]{2,1,0:T(8,128)(2,1)S(1)}, u32[]{:S(2)}, u32[]{:S(2)}) %all-to-all-start.7) | async-done | bytes 1212448 | tf_op jit(solution)/shard_map/all_to_all | solution.py:217
  138.6 4.2 %all-to-all-start.4 = ((bf16[8,32,1184]{2,1,0:T(8,128)(2,1)}), bf16[8,32,1184]{2,1,0:T(8,128)(2,1)}, u32[]{:S(2)}, u32[]{:S(2)}) async-start(bf16[8,32,1184]{2,1,0:T(8,128)(2,1)} %bitcast.61), calls=%async_computation.4 | async-start | bytes 1310720 | tf_op jit(solution)/shard_map/all_to_all | solution.py:217
  143.6 8.5 %all-to-all-done.4 = bf16[8,32,1184]{2,1,0:T(8,128)(2,1)} async-done(((bf16[8,32,1184]{2,1,0:T(8,128)(2,1)}), bf16[8,32,1184]{2,1,0:T(8,128)(2,1)}, u32[]{:S(2)}, u32[]{:S(2)}) %all-to-all-start.4) | async-done | bytes 606240 | tf_op jit(solution)/shard_map/all_to_all | solution.py:217
  154.2 5.0 %all-to-all-start.8 = ((bf16[8,32,2368]{2,1,0:T(8,128)(2,1)}), bf16[8,32,2368]{2,1,0:T(8,128)(2,1)S(1)}, u32[]{:S(2)}, u32[]{:S(2)}) async-start(bf16[8,32,2368]{2,1,0:T(8,128)(2,1)} %broadcast_in_dim.40), calls=%async_computation.8 | async-start | bytes 2490368 | tf_op jit(solution)/shard_map/all_to_all | solution.py:210
  162.8 13.4 %all-to-all-done.8 = bf16[8,32,2368]{2,1,0:T(8,128)(2,1)S(1)} async-done(((bf16[8,32,2368]{2,1,0:T(8,128)(2,1)}), bf16[8,32,2368]{2,1,0:T(8,128)(2,1)S(1)}, u32[]{:S(2)}, u32[]{:S(2)}) %all-to-all-start.8) | async-done | bytes 1212448 | tf_op jit(solution)/shard_map/all_to_all | solution.py:210
  178.0 4.2 %all-to-all-start.5 = ((bf16[8,32,1184]{2,1,0:T(8,128)(2,1)}), bf16[8,32,1184]{2,1,0:T(8,128)(2,1)}, u32[]{:S(2)}, u32[]{:S(2)}) async-start(bf16[8,32,1184]{2,1,0:T(8,128)(2,1)} %broadcast_in_dim.38), calls=%async_computation.5 | async-start | bytes 1310720 | tf_op jit(solution)/shard_map/all_to_all | solution.py:210
  183.9 7.7 %all-to-all-done.5 = bf16[8,32,1184]{2,1,0:T(8,128)(2,1)} async-done(((bf16[8,32,1184]{2,1,0:T(8,128)(2,1)}), bf16[8,32,1184]{2,1,0:T(8,128)(2,1)}, u32[]{:S(2)}, u32[]{:S(2)}) %all-to-all-start.5) | async-done | bytes 606240 | tf_op jit(solution)/shard_map/all_to_all | solution.py:210
  191.7 2.6 fusion.4
  197.1 6.2 %all-to-all-start.9 = ((bf16[128,4,448]{2,1,0:T(4,128)(2,1)}), bf16[128,4,448]{2,1,0:T(4,128)(2,1)S(1)}, u32[]{:S(2)}, u32[]{:S(2)}) async-start(bf16[128,4,448]{2,1,0:T(4,128)(2,1)} %pad_maximum_fusion.1), calls=%async_computation.9 | async-start | bytes 1048576 | tf_op jit(solution)/shard_map/all_to_all | solution.py:304
  203.3 8.0 %multiply_convert_fusion = bf16[1024,3584]{1,0:T(8,128)(2,1)} fusion(bf16[1024,512]{1,0:T(8,128)(2,1)S(1)} %copy-done.8, bf16[512,3584]{1,0:T(8,128)(2,1)} %get-tuple-element.15), kind=kOutput, calls=%fused_computation.1 | convolution fusion | flops 3765436416 | bytes 12058624 | tf_op jit(solution)/shard_map/dot_general | solution.py:280
  211.4 5.9 %all-to-all-done.9 = bf16[128,4,448]{2,1,0:T(4,128)(2,1)S(1)} async-done(((bf16[128,4,448]{2,1,0:T(4,128)(2,1)}), bf16[128,4,448]{2,1,0:T(4,128)(2,1)S(1)}, u32[]{:S(2)}, u32[]{:S(2)}) %all-to-all-start.9) | async-done | bytes 458784 | tf_op jit(solution)/shard_map/all_to_all | solution.py:304
  217.2 5.1 %all-to-all-start.1 = ((bf16[8,128,3584]{2,1,0:T(8,128)(2,1)}), bf16[8,128,3584]{2,1,0:T(8,128)(2,1)}, u32[]{:S(2)}, u32[]{:S(2)}) async-start(bf16[8,128,3584]{2,1,0:T(8,128)(2,1)} %bitcast.60), calls=%async_computation.1 | async-start | bytes 14680064 | tf_op jit(solution)/shard_map/all_to_all | solution.py:282
  224.9 79.8 %all-to-all-done.1 = bf16[8,128,3584]{2,1,0:T(8,128)(2,1)} async-done(((bf16[8,128,3584]{2,1,0:T(8,128)(2,1)}), bf16[8,128,3584]{2,1,0:T(8,128)(2,1)}, u32[]{:S(2)}, u32[]{:S(2)}) %all-to-all-start.1) | async-done | bytes 7340064 | tf_op jit(solution)/shard_map/all_to_all | solution.py:282
  304.7 5.5 %convert_reduce_fusion = f32[128,3584]{1,0:T(8,128)} fusion(bf16[8,128,3584]{2,1,0:T(8,128)(2,1)} %all-to-all-done.1), kind=kLoop, calls=%fused_computation | loop fusion | flops 6881280 | bytes 9175040 | tf_op jit(solution)/shard_map/reduce_sum | solution.py:285
  (108 shorter events, 45.9 us)
Async XLA Ops:
  0.6 91.6 %copy-start = (bf16[448,1184]{1,0:T(8,128)(2,1)S(1)}, bf16[448,1184]{1,0:T(8,128)(2,1)}, u32[]{:S(2)}) copy-start(bf16[448,1184]{1,0:T(8,128)(2,1)} %param.13) | copy-start | bytes 3182596
  2.5 50.3 %copy-start.5 = (bf16[32,3712]{1,0:T(8,128)(2,1)}, bf16[32,3712]{1,0:T(8,128)(2,1)S(1)}, u32[]{:S(2)}) copy-start(bf16[32,3712]{1,0:T(8,128)(2,1)S(1)} %pad_maximum_fusion.2.refs_0_) | copy-start | bytes 712708
  2.5 8.7 %collective-permute-start.2 = (bf16[32,3712]{1,0:T(8,128)(2,1)S(1)}, bf16[32,3712]{1,0:T(8,128)(2,1)S(1)}, u32[]{:S(2)}, u32[]{:S(2)}) collective-permute-start(bf16[32,3712]{1,0:T(8,128)(2,1)S(1)} %pad_maximum_fusion.2.refs_0_), channel_id=1, source_target_pairs={{0,16},{8,24},{16,0},{24,8},{32,48},{40,56},{48,32},{56,40},{64,80... | collective-permute-start | bytes 712712 | tf_op jit(solution)/shard_map/ppermute | solution.py:37
  6.1 7.9 %collective-permute-start.1 = (bf16[32,3712]{1,0:T(8,128)(2,1)S(1)}, bf16[32,3712]{1,0:T(8,128)(2,1)S(1)}, u32[]{:S(2)}, u32[]{:S(2)}) collective-permute-start(bf16[32,3712]{1,0:T(8,128)(2,1)S(1)} %pad_maximum_fusion.2.refs_0_), channel_id=1, source_target_pairs={{0,96},{8,104},{16,112},{24,120},{32,0},{40,8},{48,16},{56,24},{64... | collective-permute-start | bytes 712712 | tf_op jit(solution)/shard_map/ppermute | solution.py:37
  9.9 9.7 %collective-permute-start = (bf16[32,3712]{1,0:T(8,128)(2,1)S(1)}, bf16[32,3712]{1,0:T(8,128)(2,1)S(1)}, u32[]{:S(2)}, u32[]{:S(2)}) collective-permute-start(bf16[32,3712]{1,0:T(8,128)(2,1)S(1)} %pad_maximum_fusion.2.refs_0_), channel_id=1, source_target_pairs={{0,32},{8,40},{16,48},{24,56},{32,64},{40,72},{48,80},{56,88},{64,... | collective-permute-start | bytes 712712 | tf_op jit(solution)/shard_map/ppermute | solution.py:37
  11.1 11.2 %collective-permute-start.3 = (bf16[32,3712]{1,0:T(8,128)(2,1)S(1)}, bf16[32,3712]{1,0:T(8,128)(2,1)}, u32[]{:S(2)}, u32[]{:S(2)}) collective-permute-start(bf16[32,3712]{1,0:T(8,128)(2,1)S(1)} %collective-permute-done.2.refs_3_), channel_id=1, source_target_pairs={{0,32},{8,40},{16,48},{24,56},{32,64},{40,72},{48,80},{56,88},{64,... | collective-permute-start | bytes 712712 | tf_op jit(solution)/shard_map/ppermute | solution.py:37
  14.0 38.4 %copy-start.10 = (bf16[32,3712]{1,0:T(8,128)(2,1)}, bf16[32,3712]{1,0:T(8,128)(2,1)S(1)}, u32[]{:S(2)}) copy-start(bf16[32,3712]{1,0:T(8,128)(2,1)S(1)} %collective-permute-done.1.refs_2_) | copy-start | bytes 712708
  14.0 8.7 %collective-permute-start.4 = (bf16[32,3712]{1,0:T(8,128)(2,1)S(1)}, bf16[32,3712]{1,0:T(8,128)(2,1)}, u32[]{:S(2)}, u32[]{:S(2)}) collective-permute-start(bf16[32,3712]{1,0:T(8,128)(2,1)S(1)} %collective-permute-done.1.refs_2_), channel_id=1, source_target_pairs={{0,96},{8,104},{16,112},{24,120},{32,0},{40,8},{48,16},{56,24},{64... | collective-permute-start | bytes 712712 | tf_op jit(solution)/shard_map/ppermute | solution.py:37
  17.4 10.4 %collective-permute-start.8 = (bf16[32,3712]{1,0:T(8,128)(2,1)S(1)}, bf16[32,3712]{1,0:T(8,128)(2,1)S(1)}, u32[]{:S(2)}, u32[]{:S(2)}) collective-permute-start(bf16[32,3712]{1,0:T(8,128)(2,1)S(1)} %pad_maximum_fusion.2.refs_0_), channel_id=1, source_target_pairs={{0,8},{8,0},{16,24},{24,16},{32,40},{40,32},{48,56},{56,48},{64,72... | collective-permute-start | bytes 712712 | tf_op jit(solution)/shard_map/ppermute | solution.py:37
  19.6 8.4 %collective-permute-start.11 = (bf16[32,3712]{1,0:T(8,128)(2,1)S(1)}, bf16[32,3712]{1,0:T(8,128)(2,1)S(1)}, u32[]{:S(2)}, u32[]{:S(2)}) collective-permute-start(bf16[32,3712]{1,0:T(8,128)(2,1)S(1)} %collective-permute-done.2.refs_3_), channel_id=1, source_target_pairs={{0,8},{8,0},{16,24},{24,16},{32,40},{40,32},{48,56},{56,48},{64,72... | collective-permute-start | bytes 712712 | tf_op jit(solution)/shard_map/ppermute | solution.py:37
  19.6 32.8 %copy-start.11 = (bf16[32,3712]{1,0:T(8,128)(2,1)}, bf16[32,3712]{1,0:T(8,128)(2,1)S(1)}, u32[]{:S(2)}) copy-start(bf16[32,3712]{1,0:T(8,128)(2,1)S(1)} %collective-permute-done.refs_1_) | copy-start | bytes 712708
  19.6 11.0 %collective-permute-start.10 = (bf16[32,3712]{1,0:T(8,128)(2,1)S(1)}, bf16[32,3712]{1,0:T(8,128)(2,1)S(1)}, u32[]{:S(2)}, u32[]{:S(2)}) collective-permute-start(bf16[32,3712]{1,0:T(8,128)(2,1)S(1)} %collective-permute-done.1.refs_2_), channel_id=1, source_target_pairs={{0,8},{8,0},{16,24},{24,16},{32,40},{40,32},{48,56},{56,48},{64,72... | collective-permute-start | bytes 712712 | tf_op jit(solution)/shard_map/ppermute | solution.py:37
  22.3 8.6 %collective-permute-start.5 = (bf16[32,3712]{1,0:T(8,128)(2,1)S(1)}, bf16[32,3712]{1,0:T(8,128)(2,1)}, u32[]{:S(2)}, u32[]{:S(2)}) collective-permute-start(bf16[32,3712]{1,0:T(8,128)(2,1)S(1)} %collective-permute-done.1.refs_2_), channel_id=1, source_target_pairs={{0,16},{8,24},{16,0},{24,8},{32,48},{40,56},{48,32},{56,40},{64,80... | collective-permute-start | bytes 712712 | tf_op jit(solution)/shard_map/ppermute | solution.py:37
  22.7 9.5 %collective-permute-start.9 = (bf16[32,3712]{1,0:T(8,128)(2,1)S(1)}, bf16[32,3712]{1,0:T(8,128)(2,1)S(1)}, u32[]{:S(2)}, u32[]{:S(2)}) collective-permute-start(bf16[32,3712]{1,0:T(8,128)(2,1)S(1)} %collective-permute-done.refs_1_), channel_id=1, source_target_pairs={{0,8},{8,0},{16,24},{24,16},{32,40},{40,32},{48,56},{56,48},{64,72... | collective-permute-start | bytes 712712 | tf_op jit(solution)/shard_map/ppermute | solution.py:37
  27.8 24.6 %copy-start.12 = (bf16[32,3712]{1,0:T(8,128)(2,1)}, bf16[32,3712]{1,0:T(8,128)(2,1)S(1)}, u32[]{:S(2)}) copy-start(bf16[32,3712]{1,0:T(8,128)(2,1)S(1)} %collective-permute-done.8.refs_9_) | copy-start | bytes 712708
  27.9 13.3 %collective-permute-start.6 = (bf16[16,3712]{1,0:T(8,128)(2,1)S(1)}, bf16[16,3712]{1,0:T(8,128)(2,1)}, u32[]{:S(2)}, u32[]{:S(2)}) collective-permute-start(bf16[16,3712]{1,0:T(8,128)(2,1)S(1)} %slice.24), channel_id=1, source_target_pairs={{0,32},{8,40},{16,48},{24,56},{32,64},{40,72},{48,80},{56,88},{64,... | collective-permute-start | bytes 356360 | tf_op jit(solution)/shard_map/ppermute | solution.py:37
  28.0 14.4 %collective-permute-start.7 = (bf16[16,3712]{1,0:T(8,128)(2,1)S(1)}, bf16[16,3712]{1,0:T(8,128)(2,1)}, u32[]{:S(2)}, u32[]{:S(2)}) collective-permute-start(bf16[16,3712]{1,0:T(8,128)(2,1)S(1)} %slice.25), channel_id=1, source_target_pairs={{0,16},{8,24},{16,0},{24,8},{32,48},{40,56},{48,32},{56,40},{64,80... | collective-permute-start | bytes 356360 | tf_op jit(solution)/shard_map/ppermute | solution.py:37
  30.6 22.1 %collective-permute-start.12 = (bf16[32,3712]{1,0:T(8,128)(2,1)}, bf16[32,3712]{1,0:T(8,128)(2,1)}, u32[]{:S(2)}, u32[]{:S(2)}) collective-permute-start(bf16[32,3712]{1,0:T(8,128)(2,1)} %collective-permute-done.3.refs_4_), channel_id=1, source_target_pairs={{0,8},{8,0},{16,24},{24,16},{32,40},{40,32},{48,56},{56,48},{64,72... | collective-permute-start | bytes 712712 | tf_op jit(solution)/shard_map/ppermute | solution.py:37
  30.9 21.8 %collective-permute-start.13 = (bf16[32,3712]{1,0:T(8,128)(2,1)}, bf16[32,3712]{1,0:T(8,128)(2,1)}, u32[]{:S(2)}, u32[]{:S(2)}) collective-permute-start(bf16[32,3712]{1,0:T(8,128)(2,1)} %collective-permute-done.4.refs_5_), channel_id=1, source_target_pairs={{0,8},{8,0},{16,24},{24,16},{32,40},{40,32},{48,56},{56,48},{64,72... | collective-permute-start | bytes 712712 | tf_op jit(solution)/shard_map/ppermute | solution.py:37
  32.2 20.5 %collective-permute-start.14 = (bf16[32,3712]{1,0:T(8,128)(2,1)}, bf16[32,3712]{1,0:T(8,128)(2,1)}, u32[]{:S(2)}, u32[]{:S(2)}) collective-permute-start(bf16[32,3712]{1,0:T(8,128)(2,1)} %collective-permute-done.5.refs_6_), channel_id=1, source_target_pairs={{0,8},{8,0},{16,24},{24,16},{32,40},{40,32},{48,56},{56,48},{64,72... | collective-permute-start | bytes 712712 | tf_op jit(solution)/shard_map/ppermute | solution.py:37
  34.7 17.7 %all-to-all-start.6 = ((bf16[128,2,448]{2,1,0:T(2,128)(2,1)}), bf16[128,2,448]{2,1,0:T(2,128)(2,1)S(1)}, u32[]{:S(2)}, u32[]{:S(2)}) async-start(bf16[128,2,448]{2,1,0:T(2,128)(2,1)} %bitcast.26), calls=%async_computation.6 | async-start | bytes 524288 | tf_op jit(solution)/shard_map/all_to_all | solution.py:255
  41.2 11.5 %collective-permute-start.15 = (bf16[16,3712]{1,0:T(8,128)(2,1)}, bf16[16,3712]{1,0:T(8,128)(2,1)S(1)}, u32[]{:S(2)}, u32[]{:S(2)}) collective-permute-start(bf16[16,3712]{1,0:T(8,128)(2,1)} %collective-permute-done.6.refs_7_), channel_id=1, source_target_pairs={{0,8},{8,0},{16,24},{24,16},{32,40},{40,32},{48,56},{56,48},{64,72... | collective-permute-start | bytes 356360 | tf_op jit(solution)/shard_map/ppermute | solution.py:37
  42.3 10.4 %collective-permute-start.16 = (bf16[16,3712]{1,0:T(8,128)(2,1)}, bf16[16,3712]{1,0:T(8,128)(2,1)S(1)}, u32[]{:S(2)}, u32[]{:S(2)}) collective-permute-start(bf16[16,3712]{1,0:T(8,128)(2,1)} %collective-permute-done.7.refs_8_), channel_id=1, source_target_pairs={{0,8},{8,0},{16,24},{24,16},{32,40},{40,32},{48,56},{56,48},{64,72... | collective-permute-start | bytes 356360 | tf_op jit(solution)/shard_map/ppermute | solution.py:37
  66.1 12.6 %all-to-all-start = ((f32[16,8,512]{2,1,0:T(8,128)}), f32[16,8,512]{2,1,0:T(8,128)S(1)}, u32[]{:S(2)}, u32[]{:S(2)}) async-start(f32[16,8,512]{2,1,0:T(8,128)} %broadcast_in_dim.35), calls=%async_computation | async-start | bytes 524288 | tf_op jit(solution)/shard_map/all_to_all | solution.py:210
  87.9 15.8 %all-to-all-start.2 = ((bf16[128,2,448]{2,1,0:T(2,128)(2,1)}), bf16[128,2,448]{2,1,0:T(2,128)(2,1)S(1)}, u32[]{:S(2)}, u32[]{:S(2)}) async-start(bf16[128,2,448]{2,1,0:T(2,128)(2,1)} %reshape.80), calls=%async_computation.2 | async-start | bytes 524288 | tf_op jit(solution)/shard_map/all_to_all | solution.py:273
  104.6 12.7 %all-to-all-start.3 = ((bf16[16,16,448]{2,1,0:T(8,128)(2,1)}), bf16[16,16,448]{2,1,0:T(8,128)(2,1)S(1)}, u32[]{:S(2)}, u32[]{:S(2)}) async-start(bf16[16,16,448]{2,1,0:T(8,128)(2,1)} %broadcast_in_dim.37), calls=%async_computation.3 | async-start | bytes 524288 | tf_op jit(solution)/shard_map/all_to_all | solution.py:210
  118.1 20.5 %all-to-all-start.7 = ((bf16[8,32,2368]{2,1,0:T(8,128)(2,1)}), bf16[8,32,2368]{2,1,0:T(8,128)(2,1)S(1)}, u32[]{:S(2)}, u32[]{:S(2)}) async-start(bf16[8,32,2368]{2,1,0:T(8,128)(2,1)} %pad_maximum_fusion), calls=%async_computation.7 | async-start | bytes 2490368 | tf_op jit(solution)/shard_map/all_to_all | solution.py:217
  138.6 13.6 %all-to-all-start.4 = ((bf16[8,32,1184]{2,1,0:T(8,128)(2,1)}), bf16[8,32,1184]{2,1,0:T(8,128)(2,1)}, u32[]{:S(2)}, u32[]{:S(2)}) async-start(bf16[8,32,1184]{2,1,0:T(8,128)(2,1)} %bitcast.61), calls=%async_computation.4 | async-start | bytes 1310720 | tf_op jit(solution)/shard_map/all_to_all | solution.py:217
  154.2 22.0 %all-to-all-start.8 = ((bf16[8,32,2368]{2,1,0:T(8,128)(2,1)}), bf16[8,32,2368]{2,1,0:T(8,128)(2,1)S(1)}, u32[]{:S(2)}, u32[]{:S(2)}) async-start(bf16[8,32,2368]{2,1,0:T(8,128)(2,1)} %broadcast_in_dim.40), calls=%async_computation.8 | async-start | bytes 2490368 | tf_op jit(solution)/shard_map/all_to_all | solution.py:210
  178.0 13.7 %all-to-all-start.5 = ((bf16[8,32,1184]{2,1,0:T(8,128)(2,1)}), bf16[8,32,1184]{2,1,0:T(8,128)(2,1)}, u32[]{:S(2)}, u32[]{:S(2)}) async-start(bf16[8,32,1184]{2,1,0:T(8,128)(2,1)} %broadcast_in_dim.38), calls=%async_computation.5 | async-start | bytes 1310720 | tf_op jit(solution)/shard_map/all_to_all | solution.py:210
  197.1 20.1 %all-to-all-start.9 = ((bf16[128,4,448]{2,1,0:T(4,128)(2,1)}), bf16[128,4,448]{2,1,0:T(4,128)(2,1)S(1)}, u32[]{:S(2)}, u32[]{:S(2)}) async-start(bf16[128,4,448]{2,1,0:T(4,128)(2,1)} %pad_maximum_fusion.1), calls=%async_computation.9 | async-start | bytes 1048576 | tf_op jit(solution)/shard_map/all_to_all | solution.py:304
  217.2 87.5 %all-to-all-start.1 = ((bf16[8,128,3584]{2,1,0:T(8,128)(2,1)}), bf16[8,128,3584]{2,1,0:T(8,128)(2,1)}, u32[]{:S(2)}, u32[]{:S(2)}) async-start(bf16[8,128,3584]{2,1,0:T(8,128)(2,1)} %bitcast.60), calls=%async_computation.1 | async-start | bytes 14680064 | tf_op jit(solution)/shard_map/all_to_all | solution.py:282
  (13 other events, 112.1 us)

commit v2 on v0

v2 whole, which is shorter than its diff:
```python
import functools

import jax
import jax.numpy as jnp
from jax import lax
from jax.experimental import pallas as pl
from jax.experimental.pallas import tpu as pltpu
from jax.sharding import PartitionSpec as P

sharpness_scale = 20.0
epsilon = 1e-06
contract_last = (((1,), (1,)), ((), ()))
Z, X, C = 4, 2, 2
N_BLK, N_GRP = 16, 8
POS_BASE = 128
TAIL = 128
ROWS = 32
SUB = 2
WIDE = 3 * SUB
LANES = 512
TILE = 256
f32, bf16 = jnp.float32, jnp.bfloat16
VMEM = pl.BlockSpec(memory_space=pltpu.VMEM)
SMEM = pl.BlockSpec(memory_space=pltpu.SMEM)


def local(kernel, name, out_shape, scratch=(), scalars=0, count=0, flops=0, moved=0, vmem=32):
    return pl.pallas_call(
        kernel,
        in_specs=[SMEM] * scalars + [VMEM] * count,
        out_specs=jax.tree.map(lambda _: VMEM, out_shape),
        out_shape=out_shape,
        scratch_shapes=list(scratch),
        compiler_params=pltpu.CompilerParams(vmem_limit_bytes=vmem * 1024 * 1024),
        cost_estimate=pl.CostEstimate(flops=flops, bytes_accessed=moved, transcendentals=0),
        name=name,
    )


def blk_shift(dz, dx, dc):
    pairs = []
    for s in range(N_BLK):
        z, x, c = s // (X * C), s // C % X, s % C
        pairs.append((s, ((z + dz) % Z * X + (x + dx) % X) * C + (c + dc) % C))
    return pairs


def send(v, *shift):
    return lax.ppermute(v, "blk", blk_shift(*shift))


def near_column(block):
    own = [block, send(block, 1, 0, 0), send(block, -1, 0, 0), send(block, 0, 1, 0)]
    return own + [send(v, 0, 0, 1) for v in own]


def far_column(below, above, across):
    across_below = send(across, 1, 0, 0)
    far = send(above, -1, 0, 0)
    across_above = send(above, 0, 1, 0)
    return across_below, far, across_above


def far_rest(across_below, far, across_above, half):
    own = [
        across_below,
        far,
        across_above,
        send(across_below[:half], 1, 0, 0),
        send(far[half:], 0, 1, 0),
    ]
    return own + [send(v, 0, 0, 1) for v in own]


def places_of(blk):
    z, x, c = blk // (X * C), blk // C % X, blk % C
    shifts = [(0, 0), (-1, 0), (1, 0), (0, 1)], [(-1, 1), (2, 0), (1, 1), (2, 1)]
    return [
        ((z + dz + Z) % Z * X + (x + dx) % X) * C + (c + dc) % C
        for batch in shifts
        for dc in range(C)
        for dz, dx in batch
    ]


def block_kernel(pos_ref, query_ref, out_ref):
    dim = query_ref.shape[1]
    out_ref[:, :dim] = query_ref[...]
    line = lax.broadcasted_iota(jnp.int32, (ROWS, TAIL), 0)
    lane = lax.broadcasted_iota(jnp.int32, (ROWS, TAIL), 1)
    index = jnp.zeros_like(line)
    for r in range(ROWS):
        index = jnp.where(line == r, pos_ref[r], index)
    coded = jnp.where(lane == 0, index // POS_BASE, jnp.where(lane == 1, index % POS_BASE, 0))
    out_ref[:, dim:] = coded.astype(f32).astype(bf16)


def split3(v):
    hi = v.astype(bf16)
    rest = v - hi.astype(f32)
    mid = rest.astype(bf16)
    return hi, mid, (rest - mid.astype(f32)).astype(bf16)


def exact_dot(v, onehot, dims):
    parts = [lax.dot_general(p, onehot, dims, preferred_element_type=f32) for p in split3(v)]
    return parts[0] + parts[1] + parts[2]


def batch_scores(first_slot, blocks, doc_ref, score_ref, query_ref, stat_ref, pos_ref, left_ref, tail_ref):
    half, dim = query_ref.shape
    at = 0
    for block in blocks:
        rows = block.shape[0]
        query_ref[at : at + rows, :] = block[:, :dim]
        tail_ref[at : at + rows, :] = block[:, dim:]
        at += rows
    lane = lax.broadcasted_iota(jnp.int32, (8, TAIL), 1)
    line = lax.broadcasted_iota(jnp.int32, (8, TAIL), 0)
    pick = jnp.where(lane == line, 1.0, 0.0).astype(bf16)
    parts = lax.dot_general(pick, tail_ref[...], contract_last, preferred_element_type=f32)
    positive = (parts[0:1] * POS_BASE + parts[1:2]).astype(jnp.int32) - first_slot
    pos_ref[...] = positive
    steps = doc_ref.shape[0] // TILE

    def multiply(t, top):
        at = pl.multiple_of(t * TILE, TILE)
        scores = sharpness_scale * lax.dot_general(
            doc_ref[pl.ds(at, TILE), :], query_ref[...], contract_last, preferred_element_type=f32
        )
        score_ref[pl.ds(at, TILE), :] = scores
        return jnp.maximum(top, jnp.max(scores, axis=0, keepdims=True))

    top = lax.fori_loop(0, steps, multiply, jnp.full((1, half), -jnp.inf, f32))
    wide = 2 * SUB
    lines = half // ROWS * wide
    line = lax.broadcasted_iota(jnp.int32, (lines, half), 0)
    lane = lax.broadcasted_iota(jnp.int32, (lines, half), 1)
    wanted = jnp.where(lane == line // wide * ROWS + line % SUB, 1.0, 0.0).astype(bf16)
    is_u = lax.broadcasted_iota(jnp.int32, (lines, TILE), 0) % wide < SUB

    def sums(t, carry):
        at = pl.multiple_of(t * TILE, TILE)
        scores = score_ref[pl.ds(at, TILE), :]
        hit = at + lax.broadcasted_iota(jnp.int32, scores.shape, 0) == positive
        exps = jnp.exp(scores - top)
        total = carry[0] + jnp.sum(exps, axis=0, keepdims=True)
        found = carry[1] + jnp.sum(jnp.where(hit, scores, 0.0), axis=0, keepdims=True)
        others = jnp.where(hit, 0.0, exps).astype(bf16)
        onehot = jnp.where(hit, 1.0, 0.0).astype(bf16)
        left_ref[:, pl.ds(at, TILE)] = jnp.where(
            is_u,
            lax.dot_general(wanted, others, contract_last, preferred_element_type=f32),
            lax.dot_general(wanted, onehot, contract_last, preferred_element_type=f32),
        ).astype(bf16)
        return total, found

    zero = jnp.zeros((1, half), f32)
    total, found = lax.fori_loop(0, steps, sums, (zero, zero))
    stat_ref[...] = jnp.concatenate([top, total, found, jnp.zeros((5, half), f32)], axis=0)


def first_kernel(blk_ref, *refs):
    blocks, refs = refs[:-10], refs[-10:]
    hidden_ref, gain_ref, doc_ref, normed_ref = refs[:4]
    hidden = hidden_ref[...].astype(f32)
    inv_rms = lax.rsqrt(jnp.mean(hidden * hidden, axis=1, keepdims=True) + epsilon)
    normed = hidden * inv_rms * gain_ref[...]
    normed_ref[...] = jnp.concatenate([normed, jnp.zeros((8 - SUB, hidden.shape[1]), f32)], axis=0).astype(bf16)
    batch_scores(blk_ref[0] * doc_ref.shape[0], blocks, doc_ref, *refs[4:])


def second_kernel(blk_ref, *refs):
    blocks, refs = refs[:-14], refs[-14:]
    stat_first, left_first, normed_ref, doc_ref, all_ref, sub_ref, order_ref = refs[:7]
    score_ref, query_ref, pos_ref, stat_ref, left_ref, tail_ref, acc = refs[7:]
    cols = order_ref.shape[0]
    lane = lax.broadcasted_iota(jnp.int32, (ROWS, cols), 1)
    line = lax.broadcasted_iota(jnp.int32, (ROWS, cols), 0)
    places = places_of(blk_ref[0])
    for k in range(N_BLK):
        order_ref[k * ROWS : (k + 1) * ROWS, :] = jnp.where(lane == places[k] * ROWS + line, 1.0, 0.0).astype(bf16)
    batch_scores(
        blk_ref[0] * doc_ref.shape[0], blocks, doc_ref, score_ref, query_ref, stat_ref, pos_ref, left_ref, tail_ref
    )
    stats = jnp.concatenate([stat_first[...], stat_ref[...]], axis=1)
    stats = exact_dot(stats, order_ref[...], (((1,), (0,)), ((), ())))
    parts = split3(stats)
    all_ref[...] = jnp.concatenate([p[:3].astype(f32) for p in parts] + [jnp.zeros((7, cols), f32)], axis=0).astype(bf16)
    four = 2 * SUB
    lines = N_BLK * WIDE
    line = lax.broadcasted_iota(jnp.int32, (lines, N_BLK * four), 0)
    lane = lax.broadcasted_iota(jnp.int32, (lines, N_BLK * four), 1)
    swap = jnp.zeros(line.shape, f32)
    for k in range(N_BLK):
        swap = jnp.where((lane // four == k) & (line == places[k] * WIDE + lane % four), 1.0, swap)
    left = jnp.concatenate([left_first[...], left_ref[...]], axis=0)
    left = jnp.dot(swap.astype(bf16), left, preferred_element_type=f32).astype(bf16)
    line = lax.broadcasted_iota(jnp.int32, (lines, 8), 0)
    lane = lax.broadcasted_iota(jnp.int32, (lines, 8), 1)
    spread = jnp.where((line % WIDE - four == lane) & (lane < SUB), 1.0, 0.0).astype(bf16)
    acc[...] = jnp.dot(spread, normed_ref[...], preferred_element_type=f32)
    acc[...] += jnp.dot(left, doc_ref[...], preferred_element_type=f32)
    line = lax.broadcasted_iota(jnp.int32, (lines, cols), 0)
    lane = lax.broadcasted_iota(jnp.int32, (lines, cols), 1)
    wanted = jnp.where((lane == line // WIDE * ROWS + line % WIDE) & (line % WIDE < SUB), 1.0, 0.0).astype(bf16)
    stat_rows = [
        lax.dot_general(wanted, p, contract_last, preferred_element_type=f32).astype(bf16) for p in parts
    ]
    width = doc_ref.shape[1] // N_GRP
    grads = acc[...].astype(bf16)
    tail = jnp.concatenate(stat_rows + [jnp.zeros((lines, LANES - width - 24), bf16)], axis=1)
    for g in range(N_GRP):
        sub_ref[g] = jnp.concatenate([grads[:, g * width : (g + 1) * width], tail], axis=1)


def cotangent_kernel(got_ref, stat_ref, cot_ref, width):
    rows = got_ref[:, :, : 2 * SUB, :].astype(f32)
    terms, hits, tail = rows[:, :, :SUB, :width], rows[:, :, SUB:, :width], rows[:, :, :SUB, width:]
    stat = lambda k: tail[..., k : k + 1] + tail[..., k + 8 : k + 9] + tail[..., k + 16 : k + 17]
    top = jnp.max(stat(0), axis=1, keepdims=True)
    total = jnp.sum(stat(1) * jnp.exp(stat(0) - top), axis=1, keepdims=True)
    log_total = top + jnp.log(total)
    found = jnp.sum(stat(2), axis=1, keepdims=True)
    scale = jnp.exp(stat(0) - log_total)
    grads = jnp.sum(scale * terms + (jnp.exp(found - log_total) - 1.0) * hits, axis=1)
    grads = sharpness_scale * grads
    grads = jnp.concatenate([grads[g] for g in range(N_GRP)], axis=0)
    grads = jnp.concatenate([grads, jnp.zeros((N_GRP * SUB, LANES - width), f32)], axis=1).astype(bf16)
    for b in range(N_BLK):
        cot_ref[b, : N_GRP * SUB] = grads
        cot_ref[b, N_GRP * SUB :] = stat_ref[...]


def weight_kernel(stats_ref, pos_a, pos_b, order_ref, first_ref, second_ref, query_a, query_b, loss_ref, grad_ref, total):
    step = pl.program_id(0)
    cols = order_ref.shape[1]
    half = cols // 2

    @pl.when(step == 0)
    def _():
        stats = stats_ref[:, N_GRP * SUB :, :].astype(f32)
        tops, totals, found = (stats[:, k] + stats[:, k + 3] + stats[:, k + 6] for k in range(3))
        top = jnp.max(tops, axis=0, keepdims=True)
        summed = jnp.sum(totals * jnp.exp(tops - top), axis=0, keepdims=True)
        log_total = top + jnp.log(summed)
        losses = log_total - jnp.sum(found, axis=0, keepdims=True)
        both = jnp.concatenate([log_total, losses, jnp.zeros((6, cols), f32)], axis=0)
        both = exact_dot(both, order_ref[...], contract_last)
        loss_ref[...] = both[1:2]
        total[...] = both[0:1]

    out = None
    for k, (score_ref, query_ref, pos_ref) in enumerate(
        ((first_ref, query_a, pos_a), (second_ref, query_b, pos_b))
    ):
        scores = score_ref[...]
        slot = step * scores.shape[0] + lax.broadcasted_iota(jnp.int32, scores.shape, 0)
        onehot = jnp.where(slot == pos_ref[...], 1.0, 0.0)
        weights = (jnp.exp(scores - total[:, k * half : (k + 1) * half]) - onehot).astype(bf16)
        term = jnp.dot(weights, query_ref[...], preferred_element_type=f32)
        out = term if out is None else out + term
    grad_ref[...] = (sharpness_scale * out).astype(bf16)


def passage_terms(stats, pos_a, pos_b, order, score_a, score_b, query_a, query_b):
    shard_rows, half = score_a.shape
    dim = query_a.shape[1]
    tile = 256
    fixed = lambda v: pl.BlockSpec(v.shape, lambda i: (0,) * v.ndim)
    return pl.pallas_call(
        weight_kernel,
        grid=(shard_rows // tile,),
        in_specs=[fixed(stats), fixed(pos_a), fixed(pos_b), fixed(order)]
        + [pl.BlockSpec((tile, half), lambda i: (i, 0))] * 2
        + [fixed(query_a), fixed(query_b)],
        out_specs=[
            pl.BlockSpec((1, 2 * half), lambda i: (0, 0)),
            pl.BlockSpec((tile, dim), lambda i: (i, 0)),
        ],
        out_shape=[
            jax.ShapeDtypeStruct((1, 2 * half), f32),
            jax.ShapeDtypeStruct((shard_rows, dim), bf16),
        ],
        scratch_shapes=[pltpu.VMEM((1, 2 * half), f32)],
        compiler_params=pltpu.CompilerParams(vmem_limit_bytes=32 * 1024 * 1024),
        cost_estimate=pl.CostEstimate(
            flops=4 * shard_rows * half * dim, bytes_accessed=4 * shard_rows * dim, transcendentals=0
        ),
        name="passage_terms",
    )(stats, pos_a, pos_b, order, score_a, score_b, query_a, query_b)


def act_kernel(blk_ref, cot_ref, got_ref, down_ref, gate_ref, up_ref, out_ref, normed):
    units, part = down_ref.shape
    for g in range(N_GRP):
        for b in range(N_BLK):
            at = (g * N_BLK + b) * SUB
            normed[at : at + SUB, :] = got_ref[g, b, 2 * SUB :, :part].astype(f32)
    rows = cot_ref[:, : N_GRP * SUB, :].reshape(-1, LANES)
    count = rows.shape[0]
    line = lax.broadcasted_iota(jnp.int32, (count, count), 0)
    lane = lax.broadcasted_iota(jnp.int32, (count, count), 1)
    per = N_BLK * SUB
    swap = jnp.where(lane == (line % per // SUB * N_GRP + line // per) * SUB + line % SUB, 1.0, 0.0).astype(bf16)
    rows = jnp.dot(swap, rows, preferred_element_type=f32).astype(bf16)[:, :part]
    values = [lax.dot_general(rows, down_ref[...], contract_last, preferred_element_type=f32).astype(bf16)]
    rows = normed[...].astype(bf16)
    values.append(jnp.dot(rows, gate_ref[...], preferred_element_type=f32).astype(bf16))
    values.append(jnp.dot(rows, up_ref[...], preferred_element_type=f32).astype(bf16))
    own = cot_ref[blk_ref[0]]
    width = part // N_GRP
    blank = jnp.zeros((per - N_GRP * SUB, width), bf16)
    for g in range(N_GRP):
        mine = own[g * SUB : (g + 1) * SUB].astype(f32)
        pieces = [mine[:, k * width : (k + 1) * width] for k in range(N_GRP)]
        pieces = jnp.concatenate(pieces, axis=0).astype(bf16)
        for k in range(3):
            out_ref[g, k * per : (k + 1) * per, :units] = values[k][g * per : (g + 1) * per]
        out_ref[g, :per, units : units + width] = jnp.concatenate([pieces, blank], axis=0)
        out_ref[g, per:, units : units + width] = jnp.zeros((2 * per, width), bf16)


def swiglu_kernel(got_ref, out_ref, cot_ref):
    per = got_ref.shape[1] // 3
    units = out_ref.shape[2]
    sums = jnp.sum(got_ref[:, :, :units].astype(f32), axis=0)
    act_grad, gate_value, up_value = sums[:per], sums[per : 2 * per], sums[2 * per :]
    gate_sigmoid = jax.nn.sigmoid(gate_value)
    up_grad = (act_grad * gate_value * gate_sigmoid).astype(bf16)
    gate_grad = (act_grad * up_value * gate_sigmoid * (1.0 + gate_value * (1.0 - gate_sigmoid))).astype(bf16)
    for g in range(N_GRP):
        out_ref[g, :per] = gate_grad
        out_ref[g, per:] = up_grad
    pieces = got_ref[:, : N_GRP * SUB, units:].astype(f32)
    cot_ref[...] = jnp.concatenate(
        [pieces[g, k * SUB : (k + 1) * SUB] for g in range(N_GRP) for k in range(N_GRP)], axis=1
    )


def backward_kernel(grad_ref, gate_ref, up_ref, out_ref):
    per = grad_ref.shape[1] // 2
    both = grad_ref[...]
    gate_grad = both[:, :per].reshape(N_GRP * per, -1)
    up_grad = both[:, per:].reshape(N_GRP * per, -1)
    total = lax.dot_general(gate_grad, gate_ref[...], contract_last, preferred_element_type=f32)
    total += lax.dot_general(up_grad, up_ref[...], contract_last, preferred_element_type=f32)
    for g in range(N_GRP):
        out_ref[g] = total[g * per : (g + 1) * per].astype(bf16)


def hidden_kernel(back_ref, cot_ref, hidden_ref, gain_ref, out_ref):
    sums = jnp.sum(back_ref[...].astype(f32), axis=1)
    normed_grad = jnp.concatenate([sums[g] for g in range(N_GRP)], axis=1)
    hidden = hidden_ref[...].astype(f32)
    inv_rms = lax.rsqrt(jnp.mean(hidden * hidden, axis=1, keepdims=True) + epsilon)
    scaled = normed_grad * gain_ref[...]
    mean = jnp.mean(hidden * scaled, axis=1, keepdims=True)
    out_ref[...] = cot_ref[...] + inv_rms * scaled - hidden * inv_rms * inv_rms * inv_rms * mean


def exchange(v, axis):
    return lax.all_to_all(v, axis, 0, 0, tiled=True)


def shards(
    queries, stored_documents, positive, last_hidden, norm_gain, gate_weight, up_weight, down_weight
):
    shape = jax.ShapeDtypeStruct
    blk = lax.axis_index("blk").astype(jnp.int32)[None]
    shard_rows, dim = stored_documents.shape
    part = dim // N_GRP
    units = gate_weight.shape[1]
    cols = N_BLK * ROWS
    half = cols // 2
    per = N_BLK * SUB
    gain = norm_gain[None]

    block = local(block_kernel, "block", shape((ROWS, dim + TAIL), bf16), scalars=1, count=1)(
        positive, queries
    )
    first = near_column(block)
    second = far_column(*first[1:4])

    product = 2 * shard_rows * half * dim
    normed, score_a, query_a, stat_a, pos_a, left_a = local(
        first_kernel,
        "first_scores",
        [
            shape((8, dim), bf16),
            shape((shard_rows, half), f32),
            shape((half, dim), bf16),
            shape((8, half), f32),
            shape((1, half), jnp.int32),
            shape((per, shard_rows), bf16),
        ],
        scratch=[pltpu.VMEM((half, TAIL), bf16)],
        scalars=1,
        count=len(first) + 3,
        flops=2 * product,
        moved=4 * shard_rows * dim,
    )(blk, *first, last_hidden, gain, stored_documents)
    second, left_a = lax.optimization_barrier((second, left_a))
    second = far_rest(*second, ROWS // 2)
    stats, sub_terms, order, score_b, query_b, pos_b = local(
        second_kernel,
        "second_scores",
        [
            shape((16, cols), bf16),
            shape((N_GRP, N_BLK * WIDE, LANES), bf16),
            shape((cols, cols), bf16),
            shape((shard_rows, half), f32),
            shape((half, dim), bf16),
            shape((1, half), jnp.int32),
        ],
        scratch=[
            pltpu.VMEM((8, half), f32),
            pltpu.VMEM((per, shard_rows), bf16),
            pltpu.VMEM((half, TAIL), bf16),
            pltpu.VMEM((N_BLK * WIDE, dim), f32),
        ],
        scalars=1,
        count=len(second) + 4,
        flops=2 * product,
        moved=4 * shard_rows * dim,
    )(blk, *second, stat_a, left_a, normed, stored_documents)

    got = exchange(sub_terms.reshape(N_GRP * N_BLK, WIDE, LANES), ("grp", "blk"))
    got = got.reshape(N_GRP, N_BLK, WIDE, LANES)
    cot = local(
        functools.partial(cotangent_kernel, width=part),
        "cotangents",
        shape((N_BLK, 2 * N_GRP * SUB, LANES), bf16),
        count=2,
    )(got, stats)
    cot = exchange(cot, "blk")

    loss_row, passage_part = passage_terms(cot, pos_a, pos_b, order, score_a, score_b, query_a, query_b)
    losses = loss_row[0, :ROWS]
    cot, passage_part = lax.optimization_barrier((cot, passage_part))
    passage_sum = lax.psum_scatter(passage_part, "grp", scatter_dimension=0, tiled=True)

    values = local(
        act_kernel,
        "act",
        shape((N_GRP, 3 * per, units + part // N_GRP), bf16),
        scratch=[pltpu.VMEM((N_GRP * per, part), f32)],
        scalars=1,
        count=5,
    )(blk, cot, got, down_weight, gate_weight, up_weight)
    grads, cotangent = local(
        swiglu_kernel,
        "swiglu",
        [shape((N_GRP, 2 * per, units), bf16), shape((SUB, dim), f32)],
        count=1,
    )(exchange(values, "grp"))
    normed_part = local(backward_kernel, "backward", shape((N_GRP, per, part), bf16), count=3)(
        exchange(grads, "grp"), gate_weight, up_weight
    )
    back = exchange(normed_part.reshape(N_GRP * N_BLK, SUB, part), ("grp", "blk"))
    passage_grads = passage_sum.astype(f32)
    hidden_grads = local(hidden_kernel, "hidden", shape((SUB, dim), f32), count=4)(
        back.reshape(N_GRP, N_BLK, SUB, part), cotangent, last_hidden, gain
    )
    return (losses, passage_grads, hidden_grads)


def solution(mesh):
    return jax.shard_map(
        shards,
        mesh=mesh,
        in_specs=(
            P(("blk", "grp"), None),
            P("blk", None),
            P(("blk", "grp")),
            P(("blk", "grp"), None),
            P(),
            P("grp", "blk"),
            P("grp", "blk"),
            P("blk", "grp"),
        ),
        out_specs=(P(("blk", "grp")), P(("blk", "grp"), None), P(("blk", "grp"), None)),
        check_vma=False,
    )
```

time: 673 us -> 234 us (0.35)
  waiting for transfers between devices: 466 us -> 20.8 us
  matrix products: 53.1 us -> 0 us
  starting transfers between devices: 0.47 us -> 27.3 us
  Pallas kernels: 0 us -> 20 us
  local copies, waits for them, and re-layouts: 3.76 us -> 18.6 us
    all_gather x4 -> x0, waiting for transfers between devices: 230 us -> none  [the longest x1 94.2 us: shards(): lax.all_gather(up_weight, 'grp', axis=0, tiled=True)]
    unnamed x8 -> x1, waiting for transfers between devices: 169 us -> 0.02 us
    all_to_all x0 -> x4, blocking collectives: none -> 130 us  [exchange(): return lax.all_to_all(v, axis, 0, 0, tiled=True)]
    reduce_scatter x2 -> x1, waiting for transfers between devices: 67 us -> 2.81 us  [shards(): lax.psum_scatter(passage_part, 'grp', scatter_dimension=0, tiled=True)]
    dot_general x7 -> x0, matrix products: 53.1 us -> none  [the longest x1 10.6 us: shards(): lax.dot_general(gate_grad, full_gate, contract_last, preferred_element_ty...]
    all_gather x2 -> x0, blocking collectives: 44.5 us -> none  [the longest x1 23.2 us: shards(): lax.all_gather(cotangent, 'blk', axis=0, tiled=True)]
    psum x1 -> x0, blocking collectives: 34.8 us -> none  [shards(): lax.psum((summed * jnp.exp(highest - row_top), hit_logit), 'blk')]
    pmax x1 -> x0, blocking collectives: 32.8 us -> none  [shards(): row_top = lax.pmax(highest, 'blk')]
  transfers between devices with their start and end apart: 7 -> 19, of which waited for: 5 -> 8; matrix products, arithmetic and copies ran while one was open for 4% -> 2% of each run, Pallas kernels for 0% -> 3%
where the time goes in v2:
time: 234 us
  blocking collectives  130 us (56%)
  starting transfers between devices  27.3 us (12%)
  waiting for transfers between devices  20.8 us (9%)
  Pallas kernels  20 us (9%)
  local copies, waits for them, and re-layouts  18.6 us (8%)
  between operations  14.3 us (6%)
  other arithmetic  2.59 us (1%)
    all_to_all x4, blocking collectives, exchange(): return lax.all_to_all(v, axis, 0, 0, tiled=True)  130 us
    ppermute x17, starting transfers between devices, send(): return lax.ppermute(v, 'blk', blk_shift(*shift))  23.4 us
    unnamed x39, local copies, waits for them, and re-layouts  15.2 us
    all_to_all x1, waiting for transfers between devices, exchange(): return lax.all_to_all(v, axis, 0, 0, tiled=True)  13.9 us
    pallas_call x1, Pallas kernels, shards(): local(second_kernel, 'second_scores', [shape((16, cols), bf16), shape((N_...  5.55 us
    pallas_call x1, Pallas kernels, passage_terms(): pl.pallas_call(weight_kernel, grid=(shard_rows // tile,), in_specs=[fixed...  5.15 us
  transfers between devices with their start and end apart: 19, of which 8 were waited for; matrix products, arithmetic and copies ran while one was open for 2% of the time, Pallas kernels for 3%

profile of v2, /device:TPU:1, one launch (start us, length us, event | category | flops | bytes accessed | tf_op | source)
XLA Modules:
  0.0 233.6 jit_solution(6430055768313306444)
XLA Ops:
  9.4 4.7 %collective-permute-start.2 = (bf16[32,3712]{1,0:T(8,128)(2,1)S(1)}, bf16[32,3712]{1,0:T(8,128)(2,1)S(1)}, u32[]{:S(2)}, u32[]{:S(2)}) collective-permute-start(bf16[32,3712]{1,0:T(8,128)(2,1)S(1)} %block.1.refs_0_), channel_id=1, source_target_pairs={{0,96},{8,104},{16,112},{24,120},{32,0},{40,8},{48,16},{56,24},{64... | collective-permute-start | bytes 712712 | tf_op jit(solution)/shard_map/ppermute | solution.py:49
  14.0 2.7 %collective-permute-start = (bf16[32,3712]{1,0:T(8,128)(2,1)S(1)}, bf16[32,3712]{1,0:T(8,128)(2,1)S(1)}, u32[]{:S(2)}, u32[]{:S(2)}) collective-permute-start(bf16[32,3712]{1,0:T(8,128)(2,1)S(1)} %block.1.refs_0_), channel_id=1, source_target_pairs={{0,16},{8,24},{16,0},{24,8},{32,48},{40,56},{48,32},{56,40},{64,80... | collective-permute-start | bytes 712712 | tf_op jit(solution)/shard_map/ppermute | solution.py:49
  16.8 1.2 collective-permute-start.6
  18.5 1.5 collective-permute-start.8
  20.0 1.8 collective-permute-done.refs_3_
  21.9 1.9 collective-permute-start.9
  24.0 2.2 collective-permute-start.7
  27.5 1.3 collective-permute-start.1
  29.5 3.1 %copy-done.10 = bf16[1024,3584]{1,0:T(8,128)(2,1)S(1)} copy-done((bf16[1024,3584]{1,0:T(8,128)(2,1)S(1)}, bf16[1024,3584]{1,0:T(8,128)(2,1)}, u32[]{:S(2)}) %copy-start.10) | copy-done | bytes 7340056
  32.6 3.8 %first_scores.1 = (bf16[8,3584]{1,0:T(8,128)(2,1)S(1)}, f32[1024,256]{1,0:T(8,128)S(1)}, bf16[256,3584]{1,0:T(8,128)(2,1)S(1)}, f32[8,256]{1,0:T(8,128)S(1)}, s3...) custom-call(s32[1]{0:T(128)} %bitcast.blk_ref, bf16[32,3712]{1,0:T(8,128)(2,1)S(1)} %block.1.refs_0_, ...), custom_call_target="tpu_custom_call" | custom-call | flops 3758096384 | bytes 14680064 | tf_op jit(solution)/shard_map/first_scores/pallas_call | solution.py:386
  36.4 1.0 copy-done.15
  37.6 2.7 %collective-permute-start.11 = (bf16[16,3712]{1,0:T(8,128)(2,1)S(1)}, bf16[16,3712]{1,0:T(8,128)(2,1)S(1)}, u32[]{:S(2)}, u32[]{:S(2)}) collective-permute-start(bf16[16,3712]{1,0:T(8,128)(2,1)S(1)} %slice.10), channel_id=1, source_target_pairs={{0,16},{8,24},{16,0},{24,8},{32,48},{40,56},{48,32},{56,40},{64,80... | collective-permute-start | bytes 356360 | tf_op jit(solution)/shard_map/ppermute | solution.py:49
  40.3 1.1 collective-permute-start.12
  42.4 2.5 %collective-permute-start.15 = (bf16[16,3712]{1,0:T(8,128)(2,1)S(1)}, bf16[16,3712]{1,0:T(8,128)(2,1)S(1)}, u32[]{:S(2)}, u32[]{:S(2)}) collective-permute-start(bf16[16,3712]{1,0:T(8,128)(2,1)S(1)} %collective-permute-done.10.refs_3_), channel_id=1, source_target_pairs={{0,8},{8,0},{16,24},{24,16},{32,40},{40,32},{48,56},{56,48},{64,72... | collective-permute-start | bytes 356360 | tf_op jit(solution)/shard_map/ppermute | solution.py:49
  46.3 5.6 %second_scores.1 = (bf16[16,512]{1,0:T(8,128)(2,1)S(1)}, bf16[8,96,512]{2,1,0:T(8,128)(2,1)S(1)}, bf16[512,512]{1,0:T(8,128)(2,1)S(1)}, f32[1024,256]{1,0:T(8,12...) custom-call(s32[1]{0:T(128)} %bitcast.blk_ref, bf16[32,3712]{1,0:T(8,128)(2,1)S(1)} %collective-permute-done.1.refs_0_, ...), custom_call_target="tpu_custom_call" | custom-call | flops 3758096384 | bytes 14680064 | tf_op jit(solution)/shard_map/second_scores/pallas_call | solution.py:405
  53.7 1.3 reshape.18
  54.9 28.2 %all_to_all.25 = bf16[128,6,512]{2,1,0:T(8,128)(2,1)S(1)} all-to-all(bf16[128,6,512]{2,1,0:T(8,128)(2,1)} %reshape.18), channel_id=1, replica_groups=mesh['blk'=16,'grp'=8] {'grp','blk'}, dimensions={0} | all-to-all | bytes 1572864 | tf_op jit(solution)/shard_map/all_to_all | solution.py:363
  83.2 1.1 cotangents.1
  84.3 15.2 %all_to_all.26.stats_ref.cot_ref = bf16[16,32,512]{2,1,0:T(8,128)(2,1)S(1)} all-to-all(bf16[16,32,512]{2,1,0:T(8,128)(2,1)S(1)} %cotangents.1), channel_id=1, replica_groups=mesh['blk'=16,'grp'=8] {'blk'}, dimensions={0} | all-to-all | bytes 1048576 | tf_op jit(solution)/shard_map/all_to_all | solution.py:363
  99.5 5.2 %passage_terms.1 = (f32[1,512]{1,0:T(1,128)S(1)}, bf16[1024,3584]{1,0:T(8,128)(2,1)S(1)}) custom-call(bf16[16,32,512]{2,1,0:T(8,128)(2,1)S(1)} %all_to_all.26.stats_ref.cot_ref, s32[1,256]{1,0:T(1,128)S(1)} %get-tuple-element.34.pos_a, s32[1,256]{1,0:T(1,128)S(1)} %get-tuple-element.35.pos_b, bf16[512,512]{1,0:T(8,128)(2,1)S(1)} %copy-done.18, ...), custom_call_target="tpu_custom_call" | custom-call | flops 3758096384 | bytes 14680064 | tf_op jit(solution)/shard_map/passage_terms/pallas_call | solution.py:271
  104.7 2.9 %copy-done = bf16[1024,3584]{1,0:T(8,128)(2,1)} copy-done((bf16[1024,3584]{1,0:T(8,128)(2,1)}, bf16[1024,3584]{1,0:T(8,128)(2,1)S(1)}, u32[]{:S(2)}) %copy-start) | copy-done | bytes 7340056
  107.6 1.9 copy.12.down_ref
  109.5 1.2 copy-done.2
  110.8 1.0 copy-done.5
  111.8 1.4 act.1
  113.2 50.0 %all_to_all.27.got_ref = bf16[8,96,1240]{2,1,0:T(8,128)(2,1)S(1)} all-to-all(bf16[8,96,1240]{2,1,0:T(8,128)(2,1)S(1)} %act.1), channel_id=1, replica_groups=mesh['blk'=16,'grp'=8] {'grp'}, dimensions={0} | all-to-all | bytes 3809280 | tf_op jit(solution)/shard_map/all_to_all | solution.py:363
  163.8 36.6 %all_to_all.28.grad_ref = bf16[8,64,1184]{2,1,0:T(8,128)(2,1)S(1)} all-to-all(bf16[8,64,1184]{2,1,0:T(8,128)(2,1)S(1)} %get-tuple-element.45), channel_id=1, replica_groups=mesh['blk'=16,'grp'=8] {'grp'}, dimensions={0} | all-to-all | bytes 2424832 | tf_op jit(solution)/shard_map/all_to_all | solution.py:363
  202.1 3.8 %all-to-all-start.4 = ((bf16[128,2,448]{2,1,0:T(2,128)(2,1)}), bf16[128,2,448]{2,1,0:T(2,128)(2,1)S(1)}, u32[]{:S(2)}, u32[]{:S(2)}) async-start(bf16[128,2,448]{2,1,0:T(2,128)(2,1)} %reshape.20), calls=%async_computation.5 | async-start | bytes 524288 | tf_op jit(solution)/shard_map/all_to_all | solution.py:363
  206.5 13.9 %all-to-all-done.4 = bf16[128,2,448]{2,1,0:T(2,128)(2,1)S(1)} async-done(((bf16[128,2,448]{2,1,0:T(2,128)(2,1)}), bf16[128,2,448]{2,1,0:T(2,128)(2,1)S(1)}, u32[]{:S(2)}, u32[]{:S(2)}) %all-to-all-start.4) | async-done | bytes 229408 | tf_op jit(solution)/shard_map/all_to_all | solution.py:363
  220.4 1.0 hidden.1
  221.3 2.8 %reduce-scatter.2.cloned.1.call-done = bf16[128,3584]{1,0:T(8,128)(2,1)} async-done(((bf16[1024,3584]{1,0:T(8,128)(2,1)}), bf16[128,3584]{1,0:T(8,128)(2,1)}) %reduce-scatter.2.cloned.1.call-update) | async-done | bytes 917520 | tf_op jit(solution)/shard_map/reduce_scatter | solution.py:441
  224.2 2.6 %convert_element_type.3 = f32[128,3584]{1,0:T(8,128)} convert(bf16[128,3584]{1,0:T(8,128)(2,1)} %reduce-scatter.2.cloned.1.call-done) | non-fusion elementwise | flops 458752 | bytes 2752512 | tf_op jit(solution)/shard_map/convert_element_type | solution.py:461
  (66 shorter events, 12.0 us)
Async XLA Ops:
  7.2 217.0 %reduce-scatter.2.cloned.1.call-start = ((), (), s32[]{:S(2)}) async-start(), calls=%async_computation.6 | async-start | bytes 8257536 | tf_op jit(solution)/shard_map/reduce_scatter | solution.py:441
  9.4 9.1 %collective-permute-start.2 = (bf16[32,3712]{1,0:T(8,128)(2,1)S(1)}, bf16[32,3712]{1,0:T(8,128)(2,1)S(1)}, u32[]{:S(2)}, u32[]{:S(2)}) collective-permute-start(bf16[32,3712]{1,0:T(8,128)(2,1)S(1)} %block.1.refs_0_), channel_id=1, source_target_pairs={{0,96},{8,104},{16,112},{24,120},{32,0},{40,8},{48,16},{56,24},{64... | collective-permute-start | bytes 712712 | tf_op jit(solution)/shard_map/ppermute | solution.py:49
  14.0 7.8 %collective-permute-start = (bf16[32,3712]{1,0:T(8,128)(2,1)S(1)}, bf16[32,3712]{1,0:T(8,128)(2,1)S(1)}, u32[]{:S(2)}, u32[]{:S(2)}) collective-permute-start(bf16[32,3712]{1,0:T(8,128)(2,1)S(1)} %block.1.refs_0_), channel_id=1, source_target_pairs={{0,16},{8,24},{16,0},{24,8},{32,48},{40,56},{48,32},{56,40},{64,80... | collective-permute-start | bytes 712712 | tf_op jit(solution)/shard_map/ppermute | solution.py:49
  16.8 7.2 %collective-permute-start.5 = (bf16[32,3712]{1,0:T(8,128)(2,1)S(1)}, bf16[32,3712]{1,0:T(8,128)(2,1)S(1)}, u32[]{:S(2)}, u32[]{:S(2)}) collective-permute-start(bf16[32,3712]{1,0:T(8,128)(2,1)S(1)} %block.1.refs_0_), channel_id=1, source_target_pairs={{0,32},{8,40},{16,48},{24,56},{32,64},{40,72},{48,80},{56,88},{64,... | collective-permute-start | bytes 712712 | tf_op jit(solution)/shard_map/ppermute | solution.py:49
  16.8 10.2 %collective-permute-start.6 = (bf16[32,3712]{1,0:T(8,128)(2,1)S(1)}, bf16[32,3712]{1,0:T(8,128)(2,1)S(1)}, u32[]{:S(2)}, u32[]{:S(2)}) collective-permute-start(bf16[32,3712]{1,0:T(8,128)(2,1)S(1)} %block.1.refs_0_), channel_id=1, source_target_pairs={{0,8},{8,0},{16,24},{24,16},{32,40},{40,32},{48,56},{56,48},{64,72... | collective-permute-start | bytes 712712 | tf_op jit(solution)/shard_map/ppermute | solution.py:49
  18.5 9.0 %collective-permute-start.8 = (bf16[32,3712]{1,0:T(8,128)(2,1)S(1)}, bf16[32,3712]{1,0:T(8,128)(2,1)S(1)}, u32[]{:S(2)}, u32[]{:S(2)}) collective-permute-start(bf16[32,3712]{1,0:T(8,128)(2,1)S(1)} %collective-permute-done.2.refs_2_), channel_id=1, source_target_pairs={{0,8},{8,0},{16,24},{24,16},{32,40},{40,32},{48,56},{56,48},{64,72... | collective-permute-start | bytes 712712 | tf_op jit(solution)/shard_map/ppermute | solution.py:49
  21.9 6.9 %collective-permute-start.9 = (bf16[32,3712]{1,0:T(8,128)(2,1)S(1)}, bf16[32,3712]{1,0:T(8,128)(2,1)S(1)}, u32[]{:S(2)}, u32[]{:S(2)}) collective-permute-start(bf16[32,3712]{1,0:T(8,128)(2,1)S(1)} %collective-permute-done.refs_3_), channel_id=1, source_target_pairs={{0,8},{8,0},{16,24},{24,16},{32,40},{40,32},{48,56},{56,48},{64,72... | collective-permute-start | bytes 712712 | tf_op jit(solution)/shard_map/ppermute | solution.py:49
  24.0 4.7 %collective-permute-start.7 = (bf16[32,3712]{1,0:T(8,128)(2,1)S(1)}, bf16[32,3712]{1,0:T(8,128)(2,1)S(1)}, u32[]{:S(2)}, u32[]{:S(2)}) collective-permute-start(bf16[32,3712]{1,0:T(8,128)(2,1)S(1)} %collective-permute-done.5.refs_1_), channel_id=1, source_target_pairs={{0,8},{8,0},{16,24},{24,16},{32,40},{40,32},{48,56},{56,48},{64,72... | collective-permute-start | bytes 712712 | tf_op jit(solution)/shard_map/ppermute | solution.py:49
  26.9 10.5 %collective-permute-start.3 = (bf16[32,3712]{1,0:T(8,128)(2,1)S(1)}, bf16[32,3712]{1,0:T(8,128)(2,1)S(1)}, u32[]{:S(2)}, u32[]{:S(2)}) collective-permute-start(bf16[32,3712]{1,0:T(8,128)(2,1)S(1)} %collective-permute-done.2.refs_2_), channel_id=1, source_target_pairs={{0,96},{8,104},{16,112},{24,120},{32,0},{40,8},{48,16},{56,24},{64... | collective-permute-start | bytes 712712 | tf_op jit(solution)/shard_map/ppermute | solution.py:49
  27.0 10.4 %collective-permute-start.4 = (bf16[32,3712]{1,0:T(8,128)(2,1)S(1)}, bf16[32,3712]{1,0:T(8,128)(2,1)S(1)}, u32[]{:S(2)}, u32[]{:S(2)}) collective-permute-start(bf16[32,3712]{1,0:T(8,128)(2,1)S(1)} %collective-permute-done.2.refs_2_), channel_id=1, source_target_pairs={{0,16},{8,24},{16,0},{24,8},{32,48},{40,56},{48,32},{56,40},{64,80... | collective-permute-start | bytes 712712 | tf_op jit(solution)/shard_map/ppermute | solution.py:49
  27.5 9.9 %collective-permute-start.1 = (bf16[32,3712]{1,0:T(8,128)(2,1)S(1)}, bf16[32,3712]{1,0:T(8,128)(2,1)S(1)}, u32[]{:S(2)}, u32[]{:S(2)}) collective-permute-start(bf16[32,3712]{1,0:T(8,128)(2,1)S(1)} %collective-permute-done.refs_3_), channel_id=1, source_target_pairs={{0,32},{8,40},{16,48},{24,56},{32,64},{40,72},{48,80},{56,88},{64,... | collective-permute-start | bytes 712712 | tf_op jit(solution)/shard_map/ppermute | solution.py:49
  29.5 3.1 %copy-start.10 = (bf16[1024,3584]{1,0:T(8,128)(2,1)S(1)}, bf16[1024,3584]{1,0:T(8,128)(2,1)}, u32[]{:S(2)}) copy-start(bf16[1024,3584]{1,0:T(8,128)(2,1)} %refs_13_.1) | copy-start | bytes 22020100
  37.4 14.5 %copy-start.11 = (bf16[256,3584]{1,0:T(8,128)(2,1)}, bf16[256,3584]{1,0:T(8,128)(2,1)S(1)}, u32[]{:S(2)}) copy-start(bf16[256,3584]{1,0:T(8,128)(2,1)S(1)} %get-tuple-element.39.query_a) | copy-start | bytes 5505028
  37.5 5.0 %collective-permute-start.10 = (bf16[16,3712]{1,0:T(8,128)(2,1)S(1)}, bf16[16,3712]{1,0:T(8,128)(2,1)S(1)}, u32[]{:S(2)}, u32[]{:S(2)}) collective-permute-start(bf16[16,3712]{1,0:T(8,128)(2,1)S(1)} %slice.9), channel_id=1, source_target_pairs={{0,32},{8,40},{16,48},{24,56},{32,64},{40,72},{48,80},{56,88},{64,... | collective-permute-start | bytes 356360 | tf_op jit(solution)/shard_map/ppermute | solution.py:49
  37.6 7.4 %collective-permute-start.11 = (bf16[16,3712]{1,0:T(8,128)(2,1)S(1)}, bf16[16,3712]{1,0:T(8,128)(2,1)S(1)}, u32[]{:S(2)}, u32[]{:S(2)}) collective-permute-start(bf16[16,3712]{1,0:T(8,128)(2,1)S(1)} %slice.10), channel_id=1, source_target_pairs={{0,16},{8,24},{16,0},{24,8},{32,48},{40,56},{48,32},{56,40},{64,80... | collective-permute-start | bytes 356360 | tf_op jit(solution)/shard_map/ppermute | solution.py:49
  40.3 6.0 %collective-permute-start.12 = (bf16[32,3712]{1,0:T(8,128)(2,1)S(1)}, bf16[32,3712]{1,0:T(8,128)(2,1)S(1)}, u32[]{:S(2)}, u32[]{:S(2)}) collective-permute-start(bf16[32,3712]{1,0:T(8,128)(2,1)S(1)} %collective-permute-done.1.refs_0_), channel_id=1, source_target_pairs={{0,8},{8,0},{16,24},{24,16},{32,40},{40,32},{48,56},{56,48},{64,72... | collective-permute-start | bytes 712712 | tf_op jit(solution)/shard_map/ppermute | solution.py:49
  41.5 4.9 %collective-permute-start.13 = (bf16[32,3712]{1,0:T(8,128)(2,1)S(1)}, bf16[32,3712]{1,0:T(8,128)(2,1)S(1)}, u32[]{:S(2)}, u32[]{:S(2)}) collective-permute-start(bf16[32,3712]{1,0:T(8,128)(2,1)S(1)} %collective-permute-done.3.refs_1_), channel_id=1, source_target_pairs={{0,8},{8,0},{16,24},{24,16},{32,40},{40,32},{48,56},{56,48},{64,72... | collective-permute-start | bytes 712712 | tf_op jit(solution)/shard_map/ppermute | solution.py:49
  41.5 4.9 %collective-permute-start.14 = (bf16[32,3712]{1,0:T(8,128)(2,1)S(1)}, bf16[32,3712]{1,0:T(8,128)(2,1)S(1)}, u32[]{:S(2)}, u32[]{:S(2)}) collective-permute-start(bf16[32,3712]{1,0:T(8,128)(2,1)S(1)} %collective-permute-done.4.refs_2_), channel_id=1, source_target_pairs={{0,8},{8,0},{16,24},{24,16},{32,40},{40,32},{48,56},{56,48},{64,72... | collective-permute-start | bytes 712712 | tf_op jit(solution)/shard_map/ppermute | solution.py:49
  42.4 3.5 %collective-permute-start.15 = (bf16[16,3712]{1,0:T(8,128)(2,1)S(1)}, bf16[16,3712]{1,0:T(8,128)(2,1)S(1)}, u32[]{:S(2)}, u32[]{:S(2)}) collective-permute-start(bf16[16,3712]{1,0:T(8,128)(2,1)S(1)} %collective-permute-done.10.refs_3_), channel_id=1, source_target_pairs={{0,8},{8,0},{16,24},{24,16},{32,40},{40,32},{48,56},{56,48},{64,72... | collective-permute-start | bytes 356360 | tf_op jit(solution)/shard_map/ppermute | solution.py:49
  44.9 1.4 collective-permute-start.16
  54.9 44.6 %copy-start.14 = (f32[1024,256]{1,0:T(8,128)S(1)}, f32[1024,256]{1,0:T(8,128)}, u32[]{:S(2)}) copy-start(f32[1024,256]{1,0:T(8,128)} %copy-done.13) | copy-start | bytes 3145732
  54.9 44.6 %copy-start.16 = (f32[1024,256]{1,0:T(8,128)S(1)}, f32[1024,256]{1,0:T(8,128)}, u32[]{:S(2)}) copy-start(f32[1024,256]{1,0:T(8,128)} %copy-done.15) | copy-start | bytes 3145732
  83.1 16.3 %copy-start.12 = (bf16[256,3584]{1,0:T(8,128)(2,1)S(1)}, bf16[256,3584]{1,0:T(8,128)(2,1)}, u32[]{:S(2)}) copy-start(bf16[256,3584]{1,0:T(8,128)(2,1)} %copy-done.11) | copy-start | bytes 5505028
  83.2 16.4 %copy-start.18 = (bf16[512,512]{1,0:T(8,128)(2,1)S(1)}, bf16[512,512]{1,0:T(8,128)(2,1)}, u32[]{:S(2)}) copy-start(bf16[512,512]{1,0:T(8,128)(2,1)} %copy-done.17) | copy-start | bytes 1572868
  99.5 5.2 %copy-start.4 = (bf16[16,32,512]{2,1,0:T(8,128)(2,1)}, bf16[16,32,512]{2,1,0:T(8,128)(2,1)S(1)}, u32[]{:S(2)}) copy-start(bf16[16,32,512]{2,1,0:T(8,128)(2,1)S(1)} %all_to_all.26.stats_ref.cot_ref) | copy-start | bytes 1572868
  104.7 2.9 %copy-start = (bf16[1024,3584]{1,0:T(8,128)(2,1)}, bf16[1024,3584]{1,0:T(8,128)(2,1)S(1)}, u32[]{:S(2)}) copy-start(bf16[1024,3584]{1,0:T(8,128)(2,1)S(1)} %get-tuple-element.43) | copy-start | bytes 22020100
  107.6 1.9 copy-start.1
  109.5 1.3 copy-start.2
  110.8 1.0 copy-start.5
  163.2 37.2 %copy-start.3 = (bf16[448,1184]{1,0:T(8,128)(2,1)S(1)}, bf16[448,1184]{1,0:T(8,128)(2,1)}, u32[]{:S(2)}) copy-start(bf16[448,1184]{1,0:T(8,128)(2,1)} %up_ref.3) | copy-start | bytes 3182596
  200.4 19.9 %copy-start.8 = (bf16[2,3584]{1,0:T(2,128)(2,1)S(1)}, bf16[2,3584]{1,0:T(2,128)(2,1)}, u32[]{:S(2)}) copy-start(bf16[2,3584]{1,0:T(2,128)(2,1)} %hidden_ref.1) | copy-start | bytes 43012
  202.1 18.2 %all-to-all-start.4 = ((bf16[128,2,448]{2,1,0:T(2,128)(2,1)}), bf16[128,2,448]{2,1,0:T(2,128)(2,1)S(1)}, u32[]{:S(2)}, u32[]{:S(2)}) async-start(bf16[128,2,448]{2,1,0:T(2,128)(2,1)} %reshape.20), calls=%async_computation.5 | async-start | bytes 524288 | tf_op jit(solution)/shard_map/all_to_all | solution.py:363
  (6 other events, 5.1 us)
Sparse Core Ops, SparseCore 0:
  107.7 116.3 reduce-scatter.1

commit v3 on v2

--- a/solution.py
+++ b/solution.py
@@ -18,6 +18,9 @@
 SUB = 2
 WIDE = 3 * SUB
 LANES = 512
+Y_FIRST = 2816
+GX, GY = 2, 4
+Y_GROUPS = [[x * GY + y for y in range(GY)] for x in range(GX)]
 TILE = 256
 f32, bf16 = jnp.float32, jnp.bfloat16
 VMEM = pl.BlockSpec(memory_space=pltpu.VMEM)
@@ -185,8 +188,8 @@
     )
     stats = jnp.concatenate([stat_first[...], stat_ref[...]], axis=1)
     stats = exact_dot(stats, order_ref[...], (((1,), (0,)), ((), ())))
+    all_ref[...] = stats
     parts = split3(stats)
-    all_ref[...] = jnp.concatenate([p[:3].astype(f32) for p in parts] + [jnp.zeros((7, cols), f32)], axis=0).astype(bf16)
     four = 2 * SUB
     lines = N_BLK * WIDE
     line = lax.broadcasted_iota(jnp.int32, (lines, N_BLK * four), 0)
@@ -214,7 +217,16 @@
         sub_ref[g] = jnp.concatenate([grads[:, g * width : (g + 1) * width], tail], axis=1)
 
 
-def cotangent_kernel(got_ref, stat_ref, cot_ref, width):
+def merge_kernel(*refs):
+    refs, out_ref = refs[:-1], refs[-1]
+    top = functools.reduce(jnp.maximum, [r[0:1] for r in refs])
+    total = sum(r[1:2] * jnp.exp(r[0:1] - top) for r in refs)
+    found = sum(r[2:3] for r in refs)
+    out_ref[...] = jnp.concatenate([top, total, found, jnp.zeros_like(out_ref[3:])], axis=0)
+
+
+def cotangent_kernel(got_ref, cot_ref):
+    width = cot_ref.shape[2]
     rows = got_ref[:, :, : 2 * SUB, :].astype(f32)
     terms, hits, tail = rows[:, :, :SUB, :width], rows[:, :, SUB:, :width], rows[:, :, :SUB, width:]
     stat = lambda k: tail[..., k : k + 1] + tail[..., k + 8 : k + 9] + tail[..., k + 16 : k + 17]
@@ -225,86 +237,120 @@
     scale = jnp.exp(stat(0) - log_total)
     grads = jnp.sum(scale * terms + (jnp.exp(found - log_total) - 1.0) * hits, axis=1)
     grads = sharpness_scale * grads
-    grads = jnp.concatenate([grads[g] for g in range(N_GRP)], axis=0)
-    grads = jnp.concatenate([grads, jnp.zeros((N_GRP * SUB, LANES - width), f32)], axis=1).astype(bf16)
+    grads = jnp.concatenate([grads[g] for g in range(N_GRP)], axis=0).astype(bf16)
     for b in range(N_BLK):
-        cot_ref[b, : N_GRP * SUB] = grads
-        cot_ref[b, N_GRP * SUB :] = stat_ref[...]
-
-
-def weight_kernel(stats_ref, pos_a, pos_b, order_ref, first_ref, second_ref, query_a, query_b, loss_ref, grad_ref, total):
+        cot_ref[b] = grads
+
+
+def weight_kernel(grp_ref, stats_ref, pos_a, pos_b, order_ref, first_ref, second_ref, query_a, query_b, *refs):
+    loss_ref, whole_ref, own_ref, other_ref, total = refs
     step = pl.program_id(0)
     cols = order_ref.shape[1]
     half = cols // 2
 
     @pl.when(step == 0)
     def _():
-        stats = stats_ref[:, N_GRP * SUB :, :].astype(f32)
-        tops, totals, found = (stats[:, k] + stats[:, k + 3] + stats[:, k + 6] for k in range(3))
-        top = jnp.max(tops, axis=0, keepdims=True)
-        summed = jnp.sum(totals * jnp.exp(tops - top), axis=0, keepdims=True)
-        log_total = top + jnp.log(summed)
-        losses = log_total - jnp.sum(found, axis=0, keepdims=True)
+        log_total = stats_ref[0:1] + jnp.log(stats_ref[1:2])
+        losses = log_total - stats_ref[2:3]
         both = jnp.concatenate([log_total, losses, jnp.zeros((6, cols), f32)], axis=0)
         both = exact_dot(both, order_ref[...], contract_last)
         loss_ref[...] = both[1:2]
         total[...] = both[0:1]
 
+    rows = first_ref.shape[2]
     out = None
     for k, (score_ref, query_ref, pos_ref) in enumerate(
         ((first_ref, query_a, pos_a), (second_ref, query_b, pos_b))
     ):
-        scores = score_ref[...]
-        slot = step * scores.shape[0] + lax.broadcasted_iota(jnp.int32, scores.shape, 0)
+        scores = score_ref[...].reshape(GX * rows, half)
+        line = lax.broadcasted_iota(jnp.int32, scores.shape, 0)
+        slot = (line // rows * GY + step) * rows + line % rows
         onehot = jnp.where(slot == pos_ref[...], 1.0, 0.0)
         weights = (jnp.exp(scores - total[:, k * half : (k + 1) * half]) - onehot).astype(bf16)
         term = jnp.dot(weights, query_ref[...], preferred_element_type=f32)
         out = term if out is None else out + term
-    grad_ref[...] = (sharpness_scale * out).astype(bf16)
-
-
-def passage_terms(stats, pos_a, pos_b, order, score_a, score_b, query_a, query_b):
+    out = sharpness_scale * out
+    first_x = grp_ref[0] // GY == 0
+    whole_ref[...] = out[:, :Y_FIRST].astype(bf16)
+    own_ref[...] = jnp.where(first_x, out[:rows, Y_FIRST:], out[rows:, Y_FIRST:]).astype(bf16)
+    other_ref[...] = jnp.where(first_x, out[rows:, Y_FIRST:], out[:rows, Y_FIRST:]).astype(bf16)
+
+
+def passage_terms(grp, stats, pos_a, pos_b, order, score_a, score_b, query_a, query_b):
     shard_rows, half = score_a.shape
     dim = query_a.shape[1]
-    tile = 256
-    fixed = lambda v: pl.BlockSpec(v.shape, lambda i: (0,) * v.ndim)
+    rows = shard_rows // N_GRP
+    shape = jax.ShapeDtypeStruct
+    fixed = lambda v: pl.BlockSpec(v.shape, lambda i: (0,) * len(v.shape))
+    scores = pl.BlockSpec((GX, 1, rows, half), lambda i: (0, i, 0, 0))
+    apart = pl.BlockSpec((rows, dim - Y_FIRST), lambda i: (i, 0))
+    loss = shape((1, 2 * half), f32)
     return pl.pallas_call(
         weight_kernel,
-        grid=(shard_rows // tile,),
-        in_specs=[fixed(stats), fixed(pos_a), fixed(pos_b), fixed(order)]
-        + [pl.BlockSpec((tile, half), lambda i: (i, 0))] * 2
+        grid=(GY,),
+        in_specs=[SMEM, fixed(stats), fixed(pos_a), fixed(pos_b), fixed(order), scores, scores]
         + [fixed(query_a), fixed(query_b)],
-        out_specs=[
-            pl.BlockSpec((1, 2 * half), lambda i: (0, 0)),
-            pl.BlockSpec((tile, dim), lambda i: (i, 0)),
-        ],
-        out_shape=[
-            jax.ShapeDtypeStruct((1, 2 * half), f32),
-            jax.ShapeDtypeStruct((shard_rows, dim), bf16),
-        ],
+        out_specs=[fixed(loss), pl.BlockSpec((GX * rows, Y_FIRST), lambda i: (i, 0)), apart, apart],
+        out_shape=[loss, shape((shard_rows, Y_FIRST), bf16)]
+        + [shape((GY * rows, dim - Y_FIRST), bf16)] * 2,
         scratch_shapes=[pltpu.VMEM((1, 2 * half), f32)],
-        compiler_params=pltpu.CompilerParams(vmem_limit_bytes=32 * 1024 * 1024),
+        compiler_params=pltpu.CompilerParams(vmem_limit_bytes=52 * 1024 * 1024),
         cost_estimate=pl.CostEstimate(
             flops=4 * shard_rows * half * dim, bytes_accessed=4 * shard_rows * dim, transcendentals=0
         ),
         name="passage_terms",
-    )(stats, pos_a, pos_b, order, score_a, score_b, query_a, query_b)
+    )(
+        grp,
+        stats,
+        pos_a,
+        pos_b,
+        order,
+        score_a.reshape(GX, GY, rows, half),
+        score_b.reshape(GX, GY, rows, half),
+        query_a,
+        query_b,
+    )
+
+
+def x_sum_kernel(own_ref, got_ref, out_ref):
+    out_ref[...] = (own_ref[...].astype(f32) + got_ref[...].astype(f32)).astype(bf16)
+
+
+def x_split_kernel(grp_ref, both_ref, own_ref, other_ref):
+    rows = own_ref.shape[0]
+    first_x = grp_ref[0] // GY == 0
+    above, below = both_ref[:rows].astype(f32), both_ref[rows:].astype(f32)
+    own_ref[...] = jnp.where(first_x, above, below).astype(bf16)
+    other_ref[...] = jnp.where(first_x, below, above).astype(bf16)
+
+
+def passage_kernel(own_ref, got_ref, rest_ref, out_ref):
+    out_ref[:, :Y_FIRST] = own_ref[...].astype(f32) + got_ref[...].astype(f32)
+    out_ref[:, Y_FIRST:] = rest_ref[...].astype(f32)
+
+
+def send_x(v):
+    return lax.ppermute(v, "grp", [(g, (g + GY) % N_GRP) for g in range(N_GRP)])
+
+
+def y_sum(v):
+    return lax.psum_scatter(v, "grp", scatter_dimension=0, axis_index_groups=Y_GROUPS, tiled=True)
 
 
 def act_kernel(blk_ref, cot_ref, got_ref, down_ref, gate_ref, up_ref, out_ref, normed):
-    units, part = down_ref.shape
+    part, units = down_ref.shape
     for g in range(N_GRP):
         for b in range(N_BLK):
             at = (g * N_BLK + b) * SUB
             normed[at : at + SUB, :] = got_ref[g, b, 2 * SUB :, :part].astype(f32)
-    rows = cot_ref[:, : N_GRP * SUB, :].reshape(-1, LANES)
+    rows = cot_ref[...].reshape(-1, part)
     count = rows.shape[0]
     line = lax.broadcasted_iota(jnp.int32, (count, count), 0)
     lane = lax.broadcasted_iota(jnp.int32, (count, count), 1)
     per = N_BLK * SUB
     swap = jnp.where(lane == (line % per // SUB * N_GRP + line // per) * SUB + line % SUB, 1.0, 0.0).astype(bf16)
-    rows = jnp.dot(swap, rows, preferred_element_type=f32).astype(bf16)[:, :part]
-    values = [lax.dot_general(rows, down_ref[...], contract_last, preferred_element_type=f32).astype(bf16)]
+    rows = jnp.dot(swap, rows, preferred_element_type=f32).astype(bf16)
+    values = [jnp.dot(rows, down_ref[...], preferred_element_type=f32).astype(bf16)]
     rows = normed[...].astype(bf16)
     values.append(jnp.dot(rows, gate_ref[...], preferred_element_type=f32).astype(bf16))
     values.append(jnp.dot(rows, up_ref[...], preferred_element_type=f32).astype(bf16))
@@ -368,6 +414,7 @@
 ):
     shape = jax.ShapeDtypeStruct
     blk = lax.axis_index("blk").astype(jnp.int32)[None]
+    grp = lax.axis_index("grp").astype(jnp.int32)[None]
     shard_rows, dim = stored_documents.shape
     part = dim // N_GRP
     units = gate_weight.shape[1]
@@ -406,7 +453,7 @@
         second_kernel,
         "second_scores",
         [
-            shape((16, cols), bf16),
+            shape((8, cols), f32),
             shape((N_GRP, N_BLK * WIDE, LANES), bf16),
             shape((cols, cols), bf16),
             shape((shard_rows, half), f32),
@@ -426,19 +473,20 @@
     )(blk, *second, stat_a, left_a, normed, stored_documents)
 
     got = exchange(sub_terms.reshape(N_GRP * N_BLK, WIDE, LANES), ("grp", "blk"))
+    for steps in ([(0, 1, 0), (0, 0, 1), (0, 1, 1)], [(1, 0, 0), (2, 0, 0), (3, 0, 0)]):
+        stats = local(merge_kernel, "merge", shape((8, cols), f32), count=4)(
+            stats, *[send(stats, *step) for step in steps]
+        )
+    loss_row, whole, own, other = passage_terms(
+        grp, stats, pos_a, pos_b, order, score_a, score_b, query_a, query_b
+    )
+    losses = loss_row[0, :ROWS]
     got = got.reshape(N_GRP, N_BLK, WIDE, LANES)
-    cot = local(
-        functools.partial(cotangent_kernel, width=part),
-        "cotangents",
-        shape((N_BLK, 2 * N_GRP * SUB, LANES), bf16),
-        count=2,
-    )(got, stats)
+    cot = local(cotangent_kernel, "cotangents", shape((N_BLK, N_GRP * SUB, part), bf16), count=1)(got)
+    cot, whole, other = lax.optimization_barrier((cot, whole, other))
+    other = send_x(other)
+    whole = y_sum(whole)
     cot = exchange(cot, "blk")
-
-    loss_row, passage_part = passage_terms(cot, pos_a, pos_b, order, score_a, score_b, query_a, query_b)
-    losses = loss_row[0, :ROWS]
-    cot, passage_part = lax.optimization_barrier((cot, passage_part))
-    passage_sum = lax.psum_scatter(passage_part, "grp", scatter_dimension=0, tiled=True)
 
     values = local(
         act_kernel,
@@ -447,18 +495,30 @@
         scratch=[pltpu.VMEM((N_GRP * per, part), f32)],
         scalars=1,
         count=5,
-    )(blk, cot, got, down_weight, gate_weight, up_weight)
+    )(blk, cot, got, down_weight.T, gate_weight, up_weight)
     grads, cotangent = local(
         swiglu_kernel,
         "swiglu",
         [shape((N_GRP, 2 * per, units), bf16), shape((SUB, dim), f32)],
         count=1,
     )(exchange(values, "grp"))
+    grads, other = lax.optimization_barrier((grads, other))
+    rest = local(x_sum_kernel, "x_sum", shape(own.shape, bf16), count=2)(own, other)
+    grads, rest = lax.optimization_barrier((grads, rest))
+    rest = y_sum(rest)
     normed_part = local(backward_kernel, "backward", shape((N_GRP, per, part), bf16), count=3)(
         exchange(grads, "grp"), gate_weight, up_weight
     )
+    normed_part, whole = lax.optimization_barrier((normed_part, whole))
+    own, other = local(
+        x_split_kernel, "x_split", [shape((shard_rows // N_GRP, Y_FIRST), bf16)] * 2, scalars=1, count=1
+    )(grp, whole)
+    normed_part, other = lax.optimization_barrier((normed_part, other))
+    other = send_x(other)
     back = exchange(normed_part.reshape(N_GRP * N_BLK, SUB, part), ("grp", "blk"))
-    passage_grads = passage_sum.astype(f32)
+    passage_grads = local(passage_kernel, "passages", shape((shard_rows // N_GRP, dim), f32), count=3)(
+        own, other, rest
+    )
     hidden_grads = local(hidden_kernel, "hidden", shape((SUB, dim), f32), count=4)(
         back.reshape(N_GRP, N_BLK, SUB, part), cotangent, last_hidden, gain
     )

time: 234 us -> 232 us (level)
  blocking collectives: 130 us -> 13.9 us
  waiting for transfers between devices: 20.8 us -> 96.9 us
  starting transfers between devices: 27.3 us -> 56.6 us
  Pallas kernels: 20 us -> 27.1 us
  local copies, waits for them, and re-layouts: 18.6 us -> 22.4 us
  other arithmetic: 2.59 us -> 0 us
    all_to_all x4 -> x1, blocking collectives: 130 us -> 13.9 us  [exchange(): return lax.all_to_all(v, axis, 0, 0, tiled=True)]
    all_to_all x1 -> x4, waiting for transfers between devices: 13.9 us -> 66.6 us  [exchange(): return lax.all_to_all(v, axis, 0, 0, tiled=True)]
    all_to_all x1 -> x4, starting transfers between devices: 3.83 us -> 25.3 us  [exchange(): return lax.all_to_all(v, axis, 0, 0, tiled=True)]
    ppermute x17 -> x23, waiting for transfers between devices: 4.06 us -> 21.2 us  [send(): return lax.ppermute(v, 'blk', blk_shift(*shift))]
    pallas_call x3 -> x8, Pallas kernels: 11.8 us -> 18.9 us  [the longest x1 8.96 us: passage_terms(): pl.pallas_call(weight_kernel, grid=(GY,), in_specs=[SMEM, fixed(stats), f...]
    ppermute x0 -> x2, waiting for transfers between devices: none -> 6.64 us  [send_x(): return lax.ppermute(v, 'grp', [(g, (g + GY) % N_GRP) for g in range(N_GRP)])]
    ppermute x17 -> x23, starting transfers between devices: 23.4 us -> 28.5 us  [send(): return lax.ppermute(v, 'blk', blk_shift(*shift))]
    unnamed x39 -> x40, local copies, waits for them, and re-layouts: 15.2 us -> 19 us
  transfers between devices with their start and end apart: 19 -> 31, of which waited for: 8 -> 12; matrix products, arithmetic and copies ran while one was open for 2% -> 1% of each run, Pallas kernels for 3% -> 8%
where the time goes in v3:
time: 232 us; the launch traced here: 231 us
  waiting for transfers between devices  96.9 us (42%)
  starting transfers between devices  56.6 us (24%)
  Pallas kernels  27.1 us (12%)
  local copies, waits for them, and re-layouts  22.4 us (10%)
  between operations  14.2 us (6%)
  blocking collectives  13.9 us (6%)
    all_to_all x4, waiting for transfers between devices, exchange(): return lax.all_to_all(v, axis, 0, 0, tiled=True)  66.6 us
    ppermute x23, starting transfers between devices, send(): return lax.ppermute(v, 'blk', blk_shift(*shift))  28.5 us
    all_to_all x4, starting transfers between devices, exchange(): return lax.all_to_all(v, axis, 0, 0, tiled=True)  25.3 us
    ppermute x23, waiting for transfers between devices, send(): return lax.ppermute(v, 'blk', blk_shift(*shift))  21.2 us
    unnamed x40, local copies, waits for them, and re-layouts  19 us
    all_to_all x1, blocking collectives, exchange(): return lax.all_to_all(v, axis, 0, 0, tiled=True)  13.9 us
    pallas_call x1, Pallas kernels, passage_terms(): pl.pallas_call(weight_kernel, grid=(GY,), in_specs=[SMEM, fixed(stats), f...  8.96 us
    ppermute x2, waiting for transfers between devices, send_x(): return lax.ppermute(v, 'grp', [(g, (g + GY) % N_GRP) for g in range(N_GRP)])  6.64 us
  transfers between devices with their start and end apart: 31, of which 12 were waited for; matrix products, arithmetic and copies ran while one was open for 1% of the time, Pallas kernels for 8%

profile of v3, /device:TPU:1, one launch (start us, length us, event | category | flops | bytes accessed | tf_op | source)
XLA Modules:
  0.0 231.1 jit_solution(13157698320423147615)
XLA Ops:
  9.3 2.5 %collective-permute-start.5 = (bf16[32,3712]{1,0:T(8,128)(2,1)S(1)}, bf16[32,3712]{1,0:T(8,128)(2,1)S(1)}, u32[]{:S(2)}, u32[]{:S(2)}) collective-permute-start(bf16[32,3712]{1,0:T(8,128)(2,1)S(1)} %block.1.refs_0_), channel_id=1, source_target_pairs={{0,32},{8,40},{16,48},{24,56},{32,64},{40,72},{48,80},{56,88},{64,... | collective-permute-start | bytes 712712 | tf_op jit(solution)/shard_map/ppermute | solution.py:52
  11.9 2.2 collective-permute-start.2
  14.1 2.7 %collective-permute-start = (bf16[32,3712]{1,0:T(8,128)(2,1)S(1)}, bf16[32,3712]{1,0:T(8,128)(2,1)S(1)}, u32[]{:S(2)}, u32[]{:S(2)}) collective-permute-start(bf16[32,3712]{1,0:T(8,128)(2,1)S(1)} %block.1.refs_0_), channel_id=1, source_target_pairs={{0,16},{8,24},{16,0},{24,8},{32,48},{40,56},{48,32},{56,40},{64,80... | collective-permute-start | bytes 712712 | tf_op jit(solution)/shard_map/ppermute | solution.py:52
  18.1 1.4 collective-permute-done.5.refs_1_
  21.9 1.9 collective-permute-start.9
  24.5 2.8 %collective-permute-start.4 = (bf16[32,3712]{1,0:T(8,128)(2,1)S(1)}, bf16[32,3712]{1,0:T(8,128)(2,1)S(1)}, u32[]{:S(2)}, u32[]{:S(2)}) collective-permute-start(bf16[32,3712]{1,0:T(8,128)(2,1)S(1)} %collective-permute-done.2.refs_2_), channel_id=1, source_target_pairs={{0,16},{8,24},{16,0},{24,8},{32,48},{40,56},{48,32},{56,40},{64,80... | collective-permute-start | bytes 712712 | tf_op jit(solution)/shard_map/ppermute | solution.py:52
  27.3 1.4 collective-permute-start.3
  29.5 3.1 %copy-done.15 = bf16[1024,3584]{1,0:T(8,128)(2,1)S(1)} copy-done((bf16[1024,3584]{1,0:T(8,128)(2,1)S(1)}, bf16[1024,3584]{1,0:T(8,128)(2,1)}, u32[]{:S(2)}) %copy-start.15) | copy-done | bytes 7340056
  32.6 3.8 %first_scores.1 = (bf16[8,3584]{1,0:T(8,128)(2,1)S(1)}, f32[1024,256]{1,0:T(8,128)S(1)}, bf16[256,3584]{1,0:T(8,128)(2,1)S(1)}, f32[8,256]{1,0:T(8,128)S(1)}, s3...) custom-call(s32[1]{0:T(128)} %bitcast.1.blk_ref, bf16[32,3712]{1,0:T(8,128)(2,1)S(1)} %block.1.refs_0_, ...), custom_call_target="tpu_custom_call" | custom-call | flops 3758096384 | bytes 14680064 | tf_op jit(solution)/shard_map/first_scores/pallas_call | solution.py:433
  40.8 3.2 %collective-permute-done.11.refs_4_ = bf16[16,3712]{1,0:T(8,128)(2,1)S(1)} collective-permute-done((bf16[16,3712]{1,0:T(8,128)(2,1)S(1)}, bf16[16,3712]{1,0:T(8,128)(2,1)S(1)}, u32[]{:S(2)}, u32[]{:S(2)}) %collective-permute-start.11) | collective-permute-done | bytes 118816 | tf_op jit(solution)/shard_map/ppermute | solution.py:52
  43.9 2.0 collective-permute-start.16
  47.3 5.7 %second_scores.1 = (f32[8,512]{1,0:T(8,128)S(1)}, bf16[8,96,512]{2,1,0:T(8,128)(2,1)S(1)}, bf16[512,512]{1,0:T(8,128)(2,1)S(1)}, f32[1024,256]{1,0:T(8,128)S(1)}...) custom-call(s32[1]{0:T(128)} %bitcast.1.blk_ref, bf16[32,3712]{1,0:T(8,128)(2,1)S(1)} %collective-permute-done.1.refs_0_, ...), custom_call_target="tpu_custom_call" | custom-call | flops 3758096384 | bytes 14680064 | tf_op jit(solution)/shard_map/second_scores/pallas_call | solution.py:452
  55.2 1.3 reshape.26
  56.5 7.8 %all-to-all-start = ((bf16[128,6,512]{2,1,0:T(8,128)(2,1)}), bf16[128,6,512]{2,1,0:T(8,128)(2,1)S(1)}, u32[]{:S(2)}, u32[]{:S(2)}) async-start(bf16[128,6,512]{2,1,0:T(8,128)(2,1)} %reshape.26), calls=%async_computation | async-start | bytes 2097152 | tf_op jit(solution)/shard_map/all_to_all | solution.py:409
  64.4 3.2 %collective-permute-start.19 = (f32[8,512]{1,0:T(8,128)S(1)}, f32[8,512]{1,0:T(8,128)S(1)}, u32[]{:S(2)}, u32[]{:S(2)}) collective-permute-start(f32[8,512]{1,0:T(8,128)S(1)} %get-tuple-element.45.refs_0_), channel_id=1, source_target_pairs={{0,24},{8,16},{16,8},{24,0},{32,56},{40,48},{48,40},{56,32},{64,88... | collective-permute-start | bytes 49160 | tf_op jit(solution)/shard_map/ppermute | solution.py:52
  68.4 11.2 %collective-permute-done.19.refs_3_ = f32[8,512]{1,0:T(8,128)S(1)} collective-permute-done((f32[8,512]{1,0:T(8,128)S(1)}, f32[8,512]{1,0:T(8,128)S(1)}, u32[]{:S(2)}, u32[]{:S(2)}) %collective-permute-start.19) | collective-permute-done | bytes 16416 | tf_op jit(solution)/shard_map/ppermute | solution.py:52
  79.6 3.2 %collective-permute-start.22 = (f32[8,512]{1,0:T(8,128)S(1)}, f32[8,512]{1,0:T(8,128)S(1)}, u32[]{:S(2)}, u32[]{:S(2)}) collective-permute-start(f32[8,512]{1,0:T(8,128)S(1)} %merge.2.refs_0_), channel_id=1, source_target_pairs={{0,96},{8,104},{16,112},{24,120},{32,0},{40,8},{48,16},{56,24},{64... | collective-permute-start | bytes 49160 | tf_op jit(solution)/shard_map/ppermute | solution.py:52
  83.6 3.2 %collective-permute-done.21.refs_2_ = f32[8,512]{1,0:T(8,128)S(1)} collective-permute-done((f32[8,512]{1,0:T(8,128)S(1)}, f32[8,512]{1,0:T(8,128)S(1)}, u32[]{:S(2)}, u32[]{:S(2)}) %collective-permute-start.21) | collective-permute-done | bytes 16416 | tf_op jit(solution)/shard_map/ppermute | solution.py:52
  86.9 9.0 %passage_terms.1 = (f32[1,512]{1,0:T(1,128)S(1)}, bf16[1024,2816]{1,0:T(8,128)(2,1)}, bf16[512,768]{1,0:T(8,128)(2,1)S(1)}, bf16[512,768]{1,0:T(8,128)(2,1)}) custom-call(s32[1]{0:T(128)} %bitcast.grp_ref, f32[8,512]{1,0:T(8,128)S(1)} %merge.3.stats_ref, s32[1,256]{1,0:T(1,128)S(1)} %get-tuple-element.46.pos_a, s32[1,256]{1,0:T(1,128)S(1)} %get-tuple-element.47.pos_b, ...), custom_call_target="tpu_custom_call" | custom-call | flops 3758096384 | bytes 14680064 | tf_op jit(solution)/shard_map/passage_terms/pallas_call | solution.py:288
  97.9 13.9 %all_to_all.25.cot_ref = bf16[16,16,448]{2,1,0:T(8,128)(2,1)S(1)} all-to-all(bf16[16,16,448]{2,1,0:T(8,128)(2,1)S(1)} %cotangents.1), channel_id=1, replica_groups=mesh['blk'=16,'grp'=8] {'blk'}, dimensions={0} | all-to-all | bytes 458752 | tf_op jit(solution)/shard_map/all_to_all | solution.py:409
  114.3 1.4 act.1
  117.1 5.0 %all-to-all-start.2 = ((bf16[8,96,1240]{2,1,0:T(8,128)(2,1)}), bf16[8,96,1240]{2,1,0:T(8,128)(2,1)S(1)}, u32[]{:S(2)}, u32[]{:S(2)}) async-start(bf16[8,96,1240]{2,1,0:T(8,128)(2,1)} %copy-done), calls=%async_computation.2 | async-start | bytes 3932160 | tf_op jit(solution)/shard_map/all_to_all | solution.py:409
  122.1 1.5 collective-permute-start.23
  123.5 30.6 %all-to-all-done.2.got_ref = bf16[8,96,1240]{2,1,0:T(8,128)(2,1)S(1)} async-done(((bf16[8,96,1240]{2,1,0:T(8,128)(2,1)}), bf16[8,96,1240]{2,1,0:T(8,128)(2,1)S(1)}, u32[]{:S(2)}, u32[]{:S(2)}) %all-to-all-start.2) | async-done | bytes 1904672 | tf_op jit(solution)/shard_map/all_to_all | solution.py:409
  154.7 6.6 %collective-permute-done.23.got_ref = bf16[512,768]{1,0:T(8,128)(2,1)} collective-permute-done((bf16[512,768]{1,0:T(8,128)(2,1)}, bf16[512,768]{1,0:T(8,128)(2,1)}, u32[]{:S(2)}, u32[]{:S(2)}) %collective-permute-start.23) | collective-permute-done | bytes 786464 | tf_op jit(solution)/shard_map/ppermute | solution.py:333
  163.6 4.0 %all-to-all-start.3 = ((bf16[8,64,1184]{2,1,0:T(8,128)(2,1)}), bf16[8,64,1184]{2,1,0:T(8,128)(2,1)S(1)}, u32[]{:S(2)}, u32[]{:S(2)}) async-start(bf16[8,64,1184]{2,1,0:T(8,128)(2,1)} %copy-done.6), calls=%async_computation.3 | async-start | bytes 2621440 | tf_op jit(solution)/shard_map/all_to_all | solution.py:409
  168.4 20.4 %all-to-all-done.3.grad_ref = bf16[8,64,1184]{2,1,0:T(8,128)(2,1)S(1)} async-done(((bf16[8,64,1184]{2,1,0:T(8,128)(2,1)}), bf16[8,64,1184]{2,1,0:T(8,128)(2,1)S(1)}, u32[]{:S(2)}, u32[]{:S(2)}) %all-to-all-start.3) | async-done | bytes 1212448 | tf_op jit(solution)/shard_map/all_to_all | solution.py:409
  190.9 1.7 reduce-scatter.3.cloned.1.call-done.both_ref
  192.6 1.4 copy-done.5
  196.5 8.4 %all-to-all-start.4 = ((bf16[128,2,448]{2,1,0:T(2,128)(2,1)}), bf16[128,2,448]{2,1,0:T(2,128)(2,1)S(1)}, u32[]{:S(2)}, u32[]{:S(2)}) async-start(bf16[128,2,448]{2,1,0:T(2,128)(2,1)} %reshape.28), calls=%async_computation.6 | async-start | bytes 524288 | tf_op jit(solution)/shard_map/all_to_all | solution.py:409
  205.4 15.6 %all-to-all-done.4 = bf16[128,2,448]{2,1,0:T(2,128)(2,1)S(1)} async-done(((bf16[128,2,448]{2,1,0:T(2,128)(2,1)}), bf16[128,2,448]{2,1,0:T(2,128)(2,1)S(1)}, u32[]{:S(2)}, u32[]{:S(2)}) %all-to-all-start.4) | async-done | bytes 229408 | tf_op jit(solution)/shard_map/all_to_all | solution.py:409
  222.9 1.4 passages.1
  (93 shorter events, 33.3 us)
Async XLA Ops:
  9.3 10.2 %collective-permute-start.5 = (bf16[32,3712]{1,0:T(8,128)(2,1)S(1)}, bf16[32,3712]{1,0:T(8,128)(2,1)S(1)}, u32[]{:S(2)}, u32[]{:S(2)}) collective-permute-start(bf16[32,3712]{1,0:T(8,128)(2,1)S(1)} %block.1.refs_0_), channel_id=1, source_target_pairs={{0,32},{8,40},{16,48},{24,56},{32,64},{40,72},{48,80},{56,88},{64,... | collective-permute-start | bytes 712712 | tf_op jit(solution)/shard_map/ppermute | solution.py:52
  11.9 8.9 %collective-permute-start.2 = (bf16[32,3712]{1,0:T(8,128)(2,1)S(1)}, bf16[32,3712]{1,0:T(8,128)(2,1)S(1)}, u32[]{:S(2)}, u32[]{:S(2)}) collective-permute-start(bf16[32,3712]{1,0:T(8,128)(2,1)S(1)} %block.1.refs_0_), channel_id=1, source_target_pairs={{0,96},{8,104},{16,112},{24,120},{32,0},{40,8},{48,16},{56,24},{64... | collective-permute-start | bytes 712712 | tf_op jit(solution)/shard_map/ppermute | solution.py:52
  14.1 7.8 %collective-permute-start = (bf16[32,3712]{1,0:T(8,128)(2,1)S(1)}, bf16[32,3712]{1,0:T(8,128)(2,1)S(1)}, u32[]{:S(2)}, u32[]{:S(2)}) collective-permute-start(bf16[32,3712]{1,0:T(8,128)(2,1)S(1)} %block.1.refs_0_), channel_id=1, source_target_pairs={{0,16},{8,24},{16,0},{24,8},{32,48},{40,56},{48,32},{56,40},{64,80... | collective-permute-start | bytes 712712 | tf_op jit(solution)/shard_map/ppermute | solution.py:52
  16.8 10.5 %collective-permute-start.6 = (bf16[32,3712]{1,0:T(8,128)(2,1)S(1)}, bf16[32,3712]{1,0:T(8,128)(2,1)S(1)}, u32[]{:S(2)}, u32[]{:S(2)}) collective-permute-start(bf16[32,3712]{1,0:T(8,128)(2,1)S(1)} %block.1.refs_0_), channel_id=1, source_target_pairs={{0,8},{8,0},{16,24},{24,16},{32,40},{40,32},{48,56},{56,48},{64,72... | collective-permute-start | bytes 712712 | tf_op jit(solution)/shard_map/ppermute | solution.py:52
  19.5 9.2 %collective-permute-start.7 = (bf16[32,3712]{1,0:T(8,128)(2,1)S(1)}, bf16[32,3712]{1,0:T(8,128)(2,1)S(1)}, u32[]{:S(2)}, u32[]{:S(2)}) collective-permute-start(bf16[32,3712]{1,0:T(8,128)(2,1)S(1)} %collective-permute-done.5.refs_1_), channel_id=1, source_target_pairs={{0,8},{8,0},{16,24},{24,16},{32,40},{40,32},{48,56},{56,48},{64,72... | collective-permute-start | bytes 712712 | tf_op jit(solution)/shard_map/ppermute | solution.py:52
  20.7 8.1 %collective-permute-start.8 = (bf16[32,3712]{1,0:T(8,128)(2,1)S(1)}, bf16[32,3712]{1,0:T(8,128)(2,1)S(1)}, u32[]{:S(2)}, u32[]{:S(2)}) collective-permute-start(bf16[32,3712]{1,0:T(8,128)(2,1)S(1)} %collective-permute-done.2.refs_2_), channel_id=1, source_target_pairs={{0,8},{8,0},{16,24},{24,16},{32,40},{40,32},{48,56},{56,48},{64,72... | collective-permute-start | bytes 712712 | tf_op jit(solution)/shard_map/ppermute | solution.py:52
  21.9 6.9 %collective-permute-start.9 = (bf16[32,3712]{1,0:T(8,128)(2,1)S(1)}, bf16[32,3712]{1,0:T(8,128)(2,1)S(1)}, u32[]{:S(2)}, u32[]{:S(2)}) collective-permute-start(bf16[32,3712]{1,0:T(8,128)(2,1)S(1)} %collective-permute-done.refs_3_), channel_id=1, source_target_pairs={{0,8},{8,0},{16,24},{24,16},{32,40},{40,32},{48,56},{56,48},{64,72... | collective-permute-start | bytes 712712 | tf_op jit(solution)/shard_map/ppermute | solution.py:52
  24.5 14.1 %collective-permute-start.4 = (bf16[32,3712]{1,0:T(8,128)(2,1)S(1)}, bf16[32,3712]{1,0:T(8,128)(2,1)S(1)}, u32[]{:S(2)}, u32[]{:S(2)}) collective-permute-start(bf16[32,3712]{1,0:T(8,128)(2,1)S(1)} %collective-permute-done.2.refs_2_), channel_id=1, source_target_pairs={{0,16},{8,24},{16,0},{24,8},{32,48},{40,56},{48,32},{56,40},{64,80... | collective-permute-start | bytes 712712 | tf_op jit(solution)/shard_map/ppermute | solution.py:52
  27.3 11.3 %collective-permute-start.3 = (bf16[32,3712]{1,0:T(8,128)(2,1)S(1)}, bf16[32,3712]{1,0:T(8,128)(2,1)S(1)}, u32[]{:S(2)}, u32[]{:S(2)}) collective-permute-start(bf16[32,3712]{1,0:T(8,128)(2,1)S(1)} %collective-permute-done.2.refs_2_), channel_id=1, source_target_pairs={{0,96},{8,104},{16,112},{24,120},{32,0},{40,8},{48,16},{56,24},{64... | collective-permute-start | bytes 712712 | tf_op jit(solution)/shard_map/ppermute | solution.py:52
  28.7 9.9 %collective-permute-start.1 = (bf16[32,3712]{1,0:T(8,128)(2,1)S(1)}, bf16[32,3712]{1,0:T(8,128)(2,1)S(1)}, u32[]{:S(2)}, u32[]{:S(2)}) collective-permute-start(bf16[32,3712]{1,0:T(8,128)(2,1)S(1)} %collective-permute-done.refs_3_), channel_id=1, source_target_pairs={{0,32},{8,40},{16,48},{24,56},{32,64},{40,72},{48,80},{56,88},{64,... | collective-permute-start | bytes 712712 | tf_op jit(solution)/shard_map/ppermute | solution.py:52
  38.7 5.3 %collective-permute-start.11 = (bf16[16,3712]{1,0:T(8,128)(2,1)S(1)}, bf16[16,3712]{1,0:T(8,128)(2,1)S(1)}, u32[]{:S(2)}, u32[]{:S(2)}) collective-permute-start(bf16[16,3712]{1,0:T(8,128)(2,1)S(1)} %slice.10), channel_id=1, source_target_pairs={{0,16},{8,24},{16,0},{24,8},{32,48},{40,56},{48,32},{56,40},{64,80... | collective-permute-start | bytes 356360 | tf_op jit(solution)/shard_map/ppermute | solution.py:52
  39.0 7.0 %collective-permute-start.10 = (bf16[16,3712]{1,0:T(8,128)(2,1)S(1)}, bf16[16,3712]{1,0:T(8,128)(2,1)S(1)}, u32[]{:S(2)}, u32[]{:S(2)}) collective-permute-start(bf16[16,3712]{1,0:T(8,128)(2,1)S(1)} %slice.9), channel_id=1, source_target_pairs={{0,32},{8,40},{16,48},{24,56},{32,64},{40,72},{48,80},{56,88},{64,... | collective-permute-start | bytes 356360 | tf_op jit(solution)/shard_map/ppermute | solution.py:52
  39.1 8.2 %collective-permute-start.14 = (bf16[32,3712]{1,0:T(8,128)(2,1)S(1)}, bf16[32,3712]{1,0:T(8,128)(2,1)S(1)}, u32[]{:S(2)}, u32[]{:S(2)}) collective-permute-start(bf16[32,3712]{1,0:T(8,128)(2,1)S(1)} %collective-permute-done.4.refs_2_), channel_id=1, source_target_pairs={{0,8},{8,0},{16,24},{24,16},{32,40},{40,32},{48,56},{56,48},{64,72... | collective-permute-start | bytes 712712 | tf_op jit(solution)/shard_map/ppermute | solution.py:52
  40.3 7.0 %collective-permute-start.12 = (bf16[32,3712]{1,0:T(8,128)(2,1)S(1)}, bf16[32,3712]{1,0:T(8,128)(2,1)S(1)}, u32[]{:S(2)}, u32[]{:S(2)}) collective-permute-start(bf16[32,3712]{1,0:T(8,128)(2,1)S(1)} %collective-permute-done.1.refs_0_), channel_id=1, source_target_pairs={{0,8},{8,0},{16,24},{24,16},{32,40},{40,32},{48,56},{56,48},{64,72... | collective-permute-start | bytes 712712 | tf_op jit(solution)/shard_map/ppermute | solution.py:52
  40.4 6.9 %collective-permute-start.13 = (bf16[32,3712]{1,0:T(8,128)(2,1)S(1)}, bf16[32,3712]{1,0:T(8,128)(2,1)S(1)}, u32[]{:S(2)}, u32[]{:S(2)}) collective-permute-start(bf16[32,3712]{1,0:T(8,128)(2,1)S(1)} %collective-permute-done.3.refs_1_), channel_id=1, source_target_pairs={{0,8},{8,0},{16,24},{24,16},{32,40},{40,32},{48,56},{56,48},{64,72... | collective-permute-start | bytes 712712 | tf_op jit(solution)/shard_map/ppermute | solution.py:52
  43.9 3.0 %collective-permute-start.16 = (bf16[16,3712]{1,0:T(8,128)(2,1)S(1)}, bf16[16,3712]{1,0:T(8,128)(2,1)S(1)}, u32[]{:S(2)}, u32[]{:S(2)}) collective-permute-start(bf16[16,3712]{1,0:T(8,128)(2,1)S(1)} %collective-permute-done.11.refs_4_), channel_id=1, source_target_pairs={{0,8},{8,0},{16,24},{24,16},{32,40},{40,32},{48,56},{56,48},{64,72... | collective-permute-start | bytes 356360 | tf_op jit(solution)/shard_map/ppermute | solution.py:52
  45.9 1.3 collective-permute-start.15
  56.5 40.2 %all-to-all-start = ((bf16[128,6,512]{2,1,0:T(8,128)(2,1)}), bf16[128,6,512]{2,1,0:T(8,128)(2,1)S(1)}, u32[]{:S(2)}, u32[]{:S(2)}) async-start(bf16[128,6,512]{2,1,0:T(8,128)(2,1)} %reshape.26), calls=%async_computation | async-start | bytes 2097152 | tf_op jit(solution)/shard_map/all_to_all | solution.py:409
  64.3 128.3 %reduce-scatter.3.cloned.1.call-start = ((), (), s32[]{:S(2)}) async-start(), calls=%async_computation.7 | async-start | bytes 7208960 | tf_op jit(solution)/shard_map/reduce_scatter | solution.py:337
  64.4 15.2 %collective-permute-start.19 = (f32[8,512]{1,0:T(8,128)S(1)}, f32[8,512]{1,0:T(8,128)S(1)}, u32[]{:S(2)}, u32[]{:S(2)}) collective-permute-start(f32[8,512]{1,0:T(8,128)S(1)} %get-tuple-element.45.refs_0_), channel_id=1, source_target_pairs={{0,24},{8,16},{16,8},{24,0},{32,56},{40,48},{48,40},{56,32},{64,88... | collective-permute-start | bytes 49160 | tf_op jit(solution)/shard_map/ppermute | solution.py:52
  67.6 12.0 %collective-permute-start.18 = (f32[8,512]{1,0:T(8,128)S(1)}, f32[8,512]{1,0:T(8,128)S(1)}, u32[]{:S(2)}, u32[]{:S(2)}) collective-permute-start(f32[8,512]{1,0:T(8,128)S(1)} %get-tuple-element.45.refs_0_), channel_id=1, source_target_pairs={{0,8},{8,0},{16,24},{24,16},{32,40},{40,32},{48,56},{56,48},{64,72... | collective-permute-start | bytes 49160 | tf_op jit(solution)/shard_map/ppermute | solution.py:52
  67.7 11.8 %collective-permute-start.17 = (f32[8,512]{1,0:T(8,128)S(1)}, f32[8,512]{1,0:T(8,128)S(1)}, u32[]{:S(2)}, u32[]{:S(2)}) collective-permute-start(f32[8,512]{1,0:T(8,128)S(1)} %get-tuple-element.45.refs_0_), channel_id=1, source_target_pairs={{0,16},{8,24},{16,0},{24,8},{32,48},{40,56},{48,32},{56,40},{64,80... | collective-permute-start | bytes 49160 | tf_op jit(solution)/shard_map/ppermute | solution.py:52
  79.6 4.0 %collective-permute-start.22 = (f32[8,512]{1,0:T(8,128)S(1)}, f32[8,512]{1,0:T(8,128)S(1)}, u32[]{:S(2)}, u32[]{:S(2)}) collective-permute-start(f32[8,512]{1,0:T(8,128)S(1)} %merge.2.refs_0_), channel_id=1, source_target_pairs={{0,96},{8,104},{16,112},{24,120},{32,0},{40,8},{48,16},{56,24},{64... | collective-permute-start | bytes 49160 | tf_op jit(solution)/shard_map/ppermute | solution.py:52
  82.7 4.1 %collective-permute-start.21 = (f32[8,512]{1,0:T(8,128)S(1)}, f32[8,512]{1,0:T(8,128)S(1)}, u32[]{:S(2)}, u32[]{:S(2)}) collective-permute-start(f32[8,512]{1,0:T(8,128)S(1)} %merge.2.refs_0_), channel_id=1, source_target_pairs={{0,64},{8,72},{16,80},{24,88},{32,96},{40,104},{48,112},{56,120},{... | collective-permute-start | bytes 49160 | tf_op jit(solution)/shard_map/ppermute | solution.py:52
  82.9 4.0 %collective-permute-start.20 = (f32[8,512]{1,0:T(8,128)S(1)}, f32[8,512]{1,0:T(8,128)S(1)}, u32[]{:S(2)}, u32[]{:S(2)}) collective-permute-start(f32[8,512]{1,0:T(8,128)S(1)} %merge.2.refs_0_), channel_id=1, source_target_pairs={{0,32},{8,40},{16,48},{24,56},{32,64},{40,72},{48,80},{56,88},{64,... | collective-permute-start | bytes 49160 | tf_op jit(solution)/shard_map/ppermute | solution.py:52
  117.1 37.1 %all-to-all-start.2 = ((bf16[8,96,1240]{2,1,0:T(8,128)(2,1)}), bf16[8,96,1240]{2,1,0:T(8,128)(2,1)S(1)}, u32[]{:S(2)}, u32[]{:S(2)}) async-start(bf16[8,96,1240]{2,1,0:T(8,128)(2,1)} %copy-done), calls=%async_computation.2 | async-start | bytes 3932160 | tf_op jit(solution)/shard_map/all_to_all | solution.py:409
  122.1 39.3 %collective-permute-start.23 = (bf16[512,768]{1,0:T(8,128)(2,1)}, bf16[512,768]{1,0:T(8,128)(2,1)}, u32[]{:S(2)}, u32[]{:S(2)}) collective-permute-start(bf16[512,768]{1,0:T(8,128)(2,1)} %get-tuple-element.59), channel_id=1, source_target_pairs={{0,4},{1,5},{2,6},{3,7},{4,0},{5,1},{6,2},{7,3},{8,12},{9,13},{10,... | collective-permute-start | bytes 2359304 | tf_op jit(solution)/shard_map/ppermute | solution.py:333
  163.6 25.2 %all-to-all-start.3 = ((bf16[8,64,1184]{2,1,0:T(8,128)(2,1)}), bf16[8,64,1184]{2,1,0:T(8,128)(2,1)S(1)}, u32[]{:S(2)}, u32[]{:S(2)}) async-start(bf16[8,64,1184]{2,1,0:T(8,128)(2,1)} %copy-done.6), calls=%async_computation.3 | async-start | bytes 2621440 | tf_op jit(solution)/shard_map/all_to_all | solution.py:409
  167.6 54.4 %reduce-scatter.5.cloned.1.call-start = ((), (), s32[]{:S(2)}) async-start(), calls=%async_computation.8 | async-start | bytes 983040 | tf_op jit(solution)/shard_map/reduce_scatter | solution.py:337
  194.0 27.0 %copy-start.13 = (bf16[2,3584]{1,0:T(2,128)(2,1)S(1)}, bf16[2,3584]{1,0:T(2,128)(2,1)}, u32[]{:S(2)}) copy-start(bf16[2,3584]{1,0:T(2,128)(2,1)} %hidden_ref.1) | copy-start | bytes 43012
  194.4 27.6 %collective-permute-start.24 = (bf16[128,2816]{1,0:T(8,128)(2,1)S(1)}, bf16[128,2816]{1,0:T(8,128)(2,1)S(1)}, u32[]{:S(2)}, u32[]{:S(2)}) collective-permute-start(bf16[128,2816]{1,0:T(8,128)(2,1)S(1)} %get-tuple-element.69), channel_id=1, source_target_pairs={{0,4},{1,5},{2,6},{3,7},{4,0},{5,1},{6,2},{7,3},{8,12},{9,13},{10,... | collective-permute-start | bytes 2162696 | tf_op jit(solution)/shard_map/ppermute | solution.py:333
  196.5 24.5 %all-to-all-start.4 = ((bf16[128,2,448]{2,1,0:T(2,128)(2,1)}), bf16[128,2,448]{2,1,0:T(2,128)(2,1)S(1)}, u32[]{:S(2)}, u32[]{:S(2)}) async-start(bf16[128,2,448]{2,1,0:T(2,128)(2,1)} %reshape.28), calls=%async_computation.6 | async-start | bytes 524288 | tf_op jit(solution)/shard_map/all_to_all | solution.py:409
  (19 other events, 46.8 us)
Sparse Core Ops, SparseCore 0:
  98.0 94.5 reduce-scatter.2
  195.0 21.1 reduce-scatter.4

commit v4 on v3

--- a/solution.py
+++ b/solution.py
@@ -18,7 +18,7 @@
 SUB = 2
 WIDE = 3 * SUB
 LANES = 512
-Y_FIRST = 2816
+Y_FIRST = 2688
 GX, GY = 2, 4
 Y_GROUPS = [[x * GY + y for y in range(GY)] for x in range(GX)]
 TILE = 256

time: 232 us -> 228 us (0.983)
  waiting for transfers between devices: 96.9 us -> 76.4 us
  blocking collectives: 13.9 us -> 33.7 us
    all_to_all x4 -> x3, waiting for transfers between devices: 66.6 us -> 45.7 us  [exchange(): return lax.all_to_all(v, axis, 0, 0, tiled=True)]
    all_to_all x1 -> x2, blocking collectives: 13.9 us -> 33.7 us  [exchange(): return lax.all_to_all(v, axis, 0, 0, tiled=True)]
    ppermute x2, waiting for transfers between devices: 6.64 us -> 9.45 us  [send_x(): return lax.ppermute(v, 'grp', [(g, (g + GY) % N_GRP) for g in range(N_GRP)])]
    all_to_all x4 -> x3, starting transfers between devices: 25.3 us -> 23.4 us  [exchange(): return lax.all_to_all(v, axis, 0, 0, tiled=True)]
  transfers between devices with their start and end apart: 31 -> 30, of which waited for: 12 -> 10; matrix products, arithmetic and copies ran while one was open for 1% -> 1% of each run, Pallas kernels for 8% -> 8%
where the time goes in v4:
time: 228 us; the launch traced here: 227 us
  waiting for transfers between devices  76.4 us (34%)
  starting transfers between devices  54.7 us (24%)
  blocking collectives  33.7 us (15%)
  Pallas kernels  27 us (12%)
  local copies, waits for them, and re-layouts  21.2 us (9%)
  between operations  14.3 us (6%)
    all_to_all x3, waiting for transfers between devices, exchange(): return lax.all_to_all(v, axis, 0, 0, tiled=True)  45.7 us
    all_to_all x2, blocking collectives, exchange(): return lax.all_to_all(v, axis, 0, 0, tiled=True)  33.7 us
    ppermute x23, starting transfers between devices, send(): return lax.ppermute(v, 'blk', blk_shift(*shift))  28.5 us
    all_to_all x3, starting transfers between devices, exchange(): return lax.all_to_all(v, axis, 0, 0, tiled=True)  23.4 us
    ppermute x23, waiting for transfers between devices, send(): return lax.ppermute(v, 'blk', blk_shift(*shift))  21.2 us
    unnamed x40, local copies, waits for them, and re-layouts  17.9 us
    ppermute x2, waiting for transfers between devices, send_x(): return lax.ppermute(v, 'grp', [(g, (g + GY) % N_GRP) for g in range(N_GRP)])  9.45 us
    pallas_call x1, Pallas kernels, passage_terms(): pl.pallas_call(weight_kernel, grid=(GY,), in_specs=[SMEM, fixed(stats), f...  8.93 us
  transfers between devices with their start and end apart: 30, of which 10 were waited for; matrix products, arithmetic and copies ran while one was open for 1% of the time, Pallas kernels for 8%

profile of v4, /device:TPU:1, one launch (start us, length us, event | category | flops | bytes accessed | tf_op | source)
XLA Modules:
  0.0 227.3 jit_solution(13127977363728311890)
XLA Ops:
  9.3 2.5 %collective-permute-start.5 = (bf16[32,3712]{1,0:T(8,128)(2,1)S(1)}, bf16[32,3712]{1,0:T(8,128)(2,1)S(1)}, u32[]{:S(2)}, u32[]{:S(2)}) collective-permute-start(bf16[32,3712]{1,0:T(8,128)(2,1)S(1)} %block.1.refs_0_), channel_id=1, source_target_pairs={{0,32},{8,40},{16,48},{24,56},{32,64},{40,72},{48,80},{56,88},{64,... | collective-permute-start | bytes 712712 | tf_op jit(solution)/shard_map/ppermute | solution.py:52
  11.9 2.2 collective-permute-start.2
  14.1 2.7 %collective-permute-start = (bf16[32,3712]{1,0:T(8,128)(2,1)S(1)}, bf16[32,3712]{1,0:T(8,128)(2,1)S(1)}, u32[]{:S(2)}, u32[]{:S(2)}) collective-permute-start(bf16[32,3712]{1,0:T(8,128)(2,1)S(1)} %block.1.refs_0_), channel_id=1, source_target_pairs={{0,16},{8,24},{16,0},{24,8},{32,48},{40,56},{48,32},{56,40},{64,80... | collective-permute-start | bytes 712712 | tf_op jit(solution)/shard_map/ppermute | solution.py:52
  18.1 1.4 collective-permute-done.5.refs_1_
  21.9 1.9 collective-permute-start.9
  24.5 2.8 %collective-permute-start.4 = (bf16[32,3712]{1,0:T(8,128)(2,1)S(1)}, bf16[32,3712]{1,0:T(8,128)(2,1)S(1)}, u32[]{:S(2)}, u32[]{:S(2)}) collective-permute-start(bf16[32,3712]{1,0:T(8,128)(2,1)S(1)} %collective-permute-done.2.refs_2_), channel_id=1, source_target_pairs={{0,16},{8,24},{16,0},{24,8},{32,48},{40,56},{48,32},{56,40},{64,80... | collective-permute-start | bytes 712712 | tf_op jit(solution)/shard_map/ppermute | solution.py:52
  27.3 1.4 collective-permute-start.3
  29.5 3.1 %copy-done.15 = bf16[1024,3584]{1,0:T(8,128)(2,1)S(1)} copy-done((bf16[1024,3584]{1,0:T(8,128)(2,1)S(1)}, bf16[1024,3584]{1,0:T(8,128)(2,1)}, u32[]{:S(2)}) %copy-start.15) | copy-done | bytes 7340056
  32.6 3.8 %first_scores.1 = (bf16[8,3584]{1,0:T(8,128)(2,1)S(1)}, f32[1024,256]{1,0:T(8,128)S(1)}, bf16[256,3584]{1,0:T(8,128)(2,1)S(1)}, f32[8,256]{1,0:T(8,128)S(1)}, s3...) custom-call(s32[1]{0:T(128)} %bitcast.1.blk_ref, bf16[32,3712]{1,0:T(8,128)(2,1)S(1)} %block.1.refs_0_, ...), custom_call_target="tpu_custom_call" | custom-call | flops 3758096384 | bytes 14680064 | tf_op jit(solution)/shard_map/first_scores/pallas_call | solution.py:433
  40.8 3.2 %collective-permute-done.11.refs_4_ = bf16[16,3712]{1,0:T(8,128)(2,1)S(1)} collective-permute-done((bf16[16,3712]{1,0:T(8,128)(2,1)S(1)}, bf16[16,3712]{1,0:T(8,128)(2,1)S(1)}, u32[]{:S(2)}, u32[]{:S(2)}) %collective-permute-start.11) | collective-permute-done | bytes 118816 | tf_op jit(solution)/shard_map/ppermute | solution.py:52
  44.0 2.0 collective-permute-start.16
  47.3 5.6 %second_scores.1 = (f32[8,512]{1,0:T(8,128)S(1)}, bf16[8,96,512]{2,1,0:T(8,128)(2,1)S(1)}, bf16[512,512]{1,0:T(8,128)(2,1)S(1)}, f32[1024,256]{1,0:T(8,128)S(1)}...) custom-call(s32[1]{0:T(128)} %bitcast.1.blk_ref, bf16[32,3712]{1,0:T(8,128)(2,1)S(1)} %collective-permute-done.1.refs_0_, ...), custom_call_target="tpu_custom_call" | custom-call | flops 3758096384 | bytes 14680064 | tf_op jit(solution)/shard_map/second_scores/pallas_call | solution.py:452
  53.8 1.3 copy-done.18
  56.4 7.9 %all-to-all-start = ((bf16[128,6,512]{2,1,0:T(8,128)(2,1)}), bf16[128,6,512]{2,1,0:T(8,128)(2,1)S(1)}, u32[]{:S(2)}, u32[]{:S(2)}) async-start(bf16[128,6,512]{2,1,0:T(8,128)(2,1)} %reshape.26), calls=%async_computation | async-start | bytes 2097152 | tf_op jit(solution)/shard_map/all_to_all | solution.py:409
  64.4 3.2 %collective-permute-start.19 = (f32[8,512]{1,0:T(8,128)S(1)}, f32[8,512]{1,0:T(8,128)S(1)}, u32[]{:S(2)}, u32[]{:S(2)}) collective-permute-start(f32[8,512]{1,0:T(8,128)S(1)} %get-tuple-element.45.refs_0_), channel_id=1, source_target_pairs={{0,24},{8,16},{16,8},{24,0},{32,56},{40,48},{48,40},{56,32},{64,88... | collective-permute-start | bytes 49160 | tf_op jit(solution)/shard_map/ppermute | solution.py:52
  68.4 11.2 %collective-permute-done.19.refs_3_ = f32[8,512]{1,0:T(8,128)S(1)} collective-permute-done((f32[8,512]{1,0:T(8,128)S(1)}, f32[8,512]{1,0:T(8,128)S(1)}, u32[]{:S(2)}, u32[]{:S(2)}) %collective-permute-start.19) | collective-permute-done | bytes 16416 | tf_op jit(solution)/shard_map/ppermute | solution.py:52
  79.6 3.2 %collective-permute-start.22 = (f32[8,512]{1,0:T(8,128)S(1)}, f32[8,512]{1,0:T(8,128)S(1)}, u32[]{:S(2)}, u32[]{:S(2)}) collective-permute-start(f32[8,512]{1,0:T(8,128)S(1)} %merge.2.refs_0_), channel_id=1, source_target_pairs={{0,96},{8,104},{16,112},{24,120},{32,0},{40,8},{48,16},{56,24},{64... | collective-permute-start | bytes 49160 | tf_op jit(solution)/shard_map/ppermute | solution.py:52
  83.6 3.2 %collective-permute-done.21.refs_2_ = f32[8,512]{1,0:T(8,128)S(1)} collective-permute-done((f32[8,512]{1,0:T(8,128)S(1)}, f32[8,512]{1,0:T(8,128)S(1)}, u32[]{:S(2)}, u32[]{:S(2)}) %collective-permute-start.21) | collective-permute-done | bytes 16416 | tf_op jit(solution)/shard_map/ppermute | solution.py:52
  86.9 8.9 %passage_terms.1 = (f32[1,512]{1,0:T(1,128)S(1)}, bf16[1024,2688]{1,0:T(8,128)(2,1)}, bf16[512,896]{1,0:T(8,128)(2,1)S(1)}, bf16[512,896]{1,0:T(8,128)(2,1)}) custom-call(s32[1]{0:T(128)} %bitcast.grp_ref, f32[8,512]{1,0:T(8,128)S(1)} %merge.3.stats_ref, s32[1,256]{1,0:T(1,128)S(1)} %get-tuple-element.46.pos_a, s32[1,256]{1,0:T(1,128)S(1)} %get-tuple-element.47.pos_b, ...), custom_call_target="tpu_custom_call" | custom-call | flops 3758096384 | bytes 14680064 | tf_op jit(solution)/shard_map/passage_terms/pallas_call | solution.py:288
  97.9 13.9 %all_to_all.25.cot_ref = bf16[16,16,448]{2,1,0:T(8,128)(2,1)S(1)} all-to-all(bf16[16,16,448]{2,1,0:T(8,128)(2,1)S(1)} %cotangents.1), channel_id=1, replica_groups=mesh['blk'=16,'grp'=8] {'blk'}, dimensions={0} | all-to-all | bytes 458752 | tf_op jit(solution)/shard_map/all_to_all | solution.py:409
  114.4 1.4 act.1
  117.1 5.0 %all-to-all-start.2 = ((bf16[8,96,1240]{2,1,0:T(8,128)(2,1)}), bf16[8,96,1240]{2,1,0:T(8,128)(2,1)S(1)}, u32[]{:S(2)}, u32[]{:S(2)}) async-start(bf16[8,96,1240]{2,1,0:T(8,128)(2,1)} %copy-done), calls=%async_computation.2 | async-start | bytes 3932160 | tf_op jit(solution)/shard_map/all_to_all | solution.py:409
  122.1 1.4 collective-permute-start.23
  123.5 30.6 %all-to-all-done.2.got_ref = bf16[8,96,1240]{2,1,0:T(8,128)(2,1)S(1)} async-done(((bf16[8,96,1240]{2,1,0:T(8,128)(2,1)}), bf16[8,96,1240]{2,1,0:T(8,128)(2,1)S(1)}, u32[]{:S(2)}, u32[]{:S(2)}) %all-to-all-start.2) | async-done | bytes 1904672 | tf_op jit(solution)/shard_map/all_to_all | solution.py:409
  154.7 9.4 %collective-permute-done.23.got_ref = bf16[512,896]{1,0:T(8,128)(2,1)} collective-permute-done((bf16[512,896]{1,0:T(8,128)(2,1)}, bf16[512,896]{1,0:T(8,128)(2,1)}, u32[]{:S(2)}, u32[]{:S(2)}) %collective-permute-start.23) | collective-permute-done | bytes 917536 | tf_op jit(solution)/shard_map/ppermute | solution.py:333
  164.2 1.4 x_sum.1
  166.6 19.8 %all_to_all.26.grad_ref = bf16[8,64,1184]{2,1,0:T(8,128)(2,1)S(1)} all-to-all(bf16[8,64,1184]{2,1,0:T(8,128)(2,1)} %copy-done.6), channel_id=1, replica_groups=mesh['blk'=16,'grp'=8] {'grp'}, dimensions={0} | all-to-all | bytes 2424832 | tf_op jit(solution)/shard_map/all_to_all | solution.py:409
  187.3 1.3 copy-done.5
  189.0 1.3 collective-permute-start.24
  191.1 10.5 %all-to-all-start.4 = ((bf16[128,2,448]{2,1,0:T(2,128)(2,1)}), bf16[128,2,448]{2,1,0:T(2,128)(2,1)S(1)}, u32[]{:S(2)}, u32[]{:S(2)}) async-start(bf16[128,2,448]{2,1,0:T(2,128)(2,1)} %reshape.28), calls=%async_computation.6 | async-start | bytes 524288 | tf_op jit(solution)/shard_map/all_to_all | solution.py:409
  202.1 15.0 %all-to-all-done.4 = bf16[128,2,448]{2,1,0:T(2,128)(2,1)S(1)} async-done(((bf16[128,2,448]{2,1,0:T(2,128)(2,1)}), bf16[128,2,448]{2,1,0:T(2,128)(2,1)S(1)}, u32[]{:S(2)}, u32[]{:S(2)}) %all-to-all-start.4) | async-done | bytes 229408 | tf_op jit(solution)/shard_map/all_to_all | solution.py:409
  219.0 1.4 passages.1
  (92 shorter events, 28.9 us)
Async XLA Ops:
  9.3 10.2 %collective-permute-start.5 = (bf16[32,3712]{1,0:T(8,128)(2,1)S(1)}, bf16[32,3712]{1,0:T(8,128)(2,1)S(1)}, u32[]{:S(2)}, u32[]{:S(2)}) collective-permute-start(bf16[32,3712]{1,0:T(8,128)(2,1)S(1)} %block.1.refs_0_), channel_id=1, source_target_pairs={{0,32},{8,40},{16,48},{24,56},{32,64},{40,72},{48,80},{56,88},{64,... | collective-permute-start | bytes 712712 | tf_op jit(solution)/shard_map/ppermute | solution.py:52
  11.9 8.9 %collective-permute-start.2 = (bf16[32,3712]{1,0:T(8,128)(2,1)S(1)}, bf16[32,3712]{1,0:T(8,128)(2,1)S(1)}, u32[]{:S(2)}, u32[]{:S(2)}) collective-permute-start(bf16[32,3712]{1,0:T(8,128)(2,1)S(1)} %block.1.refs_0_), channel_id=1, source_target_pairs={{0,96},{8,104},{16,112},{24,120},{32,0},{40,8},{48,16},{56,24},{64... | collective-permute-start | bytes 712712 | tf_op jit(solution)/shard_map/ppermute | solution.py:52
  14.1 7.8 %collective-permute-start = (bf16[32,3712]{1,0:T(8,128)(2,1)S(1)}, bf16[32,3712]{1,0:T(8,128)(2,1)S(1)}, u32[]{:S(2)}, u32[]{:S(2)}) collective-permute-start(bf16[32,3712]{1,0:T(8,128)(2,1)S(1)} %block.1.refs_0_), channel_id=1, source_target_pairs={{0,16},{8,24},{16,0},{24,8},{32,48},{40,56},{48,32},{56,40},{64,80... | collective-permute-start | bytes 712712 | tf_op jit(solution)/shard_map/ppermute | solution.py:52
  16.8 10.5 %collective-permute-start.6 = (bf16[32,3712]{1,0:T(8,128)(2,1)S(1)}, bf16[32,3712]{1,0:T(8,128)(2,1)S(1)}, u32[]{:S(2)}, u32[]{:S(2)}) collective-permute-start(bf16[32,3712]{1,0:T(8,128)(2,1)S(1)} %block.1.refs_0_), channel_id=1, source_target_pairs={{0,8},{8,0},{16,24},{24,16},{32,40},{40,32},{48,56},{56,48},{64,72... | collective-permute-start | bytes 712712 | tf_op jit(solution)/shard_map/ppermute | solution.py:52
  19.5 9.2 %collective-permute-start.7 = (bf16[32,3712]{1,0:T(8,128)(2,1)S(1)}, bf16[32,3712]{1,0:T(8,128)(2,1)S(1)}, u32[]{:S(2)}, u32[]{:S(2)}) collective-permute-start(bf16[32,3712]{1,0:T(8,128)(2,1)S(1)} %collective-permute-done.5.refs_1_), channel_id=1, source_target_pairs={{0,8},{8,0},{16,24},{24,16},{32,40},{40,32},{48,56},{56,48},{64,72... | collective-permute-start | bytes 712712 | tf_op jit(solution)/shard_map/ppermute | solution.py:52
  20.7 8.1 %collective-permute-start.8 = (bf16[32,3712]{1,0:T(8,128)(2,1)S(1)}, bf16[32,3712]{1,0:T(8,128)(2,1)S(1)}, u32[]{:S(2)}, u32[]{:S(2)}) collective-permute-start(bf16[32,3712]{1,0:T(8,128)(2,1)S(1)} %collective-permute-done.2.refs_2_), channel_id=1, source_target_pairs={{0,8},{8,0},{16,24},{24,16},{32,40},{40,32},{48,56},{56,48},{64,72... | collective-permute-start | bytes 712712 | tf_op jit(solution)/shard_map/ppermute | solution.py:52
  21.9 6.9 %collective-permute-start.9 = (bf16[32,3712]{1,0:T(8,128)(2,1)S(1)}, bf16[32,3712]{1,0:T(8,128)(2,1)S(1)}, u32[]{:S(2)}, u32[]{:S(2)}) collective-permute-start(bf16[32,3712]{1,0:T(8,128)(2,1)S(1)} %collective-permute-done.refs_3_), channel_id=1, source_target_pairs={{0,8},{8,0},{16,24},{24,16},{32,40},{40,32},{48,56},{56,48},{64,72... | collective-permute-start | bytes 712712 | tf_op jit(solution)/shard_map/ppermute | solution.py:52
  24.5 14.1 %collective-permute-start.4 = (bf16[32,3712]{1,0:T(8,128)(2,1)S(1)}, bf16[32,3712]{1,0:T(8,128)(2,1)S(1)}, u32[]{:S(2)}, u32[]{:S(2)}) collective-permute-start(bf16[32,3712]{1,0:T(8,128)(2,1)S(1)} %collective-permute-done.2.refs_2_), channel_id=1, source_target_pairs={{0,16},{8,24},{16,0},{24,8},{32,48},{40,56},{48,32},{56,40},{64,80... | collective-permute-start | bytes 712712 | tf_op jit(solution)/shard_map/ppermute | solution.py:52
  27.3 11.3 %collective-permute-start.3 = (bf16[32,3712]{1,0:T(8,128)(2,1)S(1)}, bf16[32,3712]{1,0:T(8,128)(2,1)S(1)}, u32[]{:S(2)}, u32[]{:S(2)}) collective-permute-start(bf16[32,3712]{1,0:T(8,128)(2,1)S(1)} %collective-permute-done.2.refs_2_), channel_id=1, source_target_pairs={{0,96},{8,104},{16,112},{24,120},{32,0},{40,8},{48,16},{56,24},{64... | collective-permute-start | bytes 712712 | tf_op jit(solution)/shard_map/ppermute | solution.py:52
  28.7 9.9 %collective-permute-start.1 = (bf16[32,3712]{1,0:T(8,128)(2,1)S(1)}, bf16[32,3712]{1,0:T(8,128)(2,1)S(1)}, u32[]{:S(2)}, u32[]{:S(2)}) collective-permute-start(bf16[32,3712]{1,0:T(8,128)(2,1)S(1)} %collective-permute-done.refs_3_), channel_id=1, source_target_pairs={{0,32},{8,40},{16,48},{24,56},{32,64},{40,72},{48,80},{56,88},{64,... | collective-permute-start | bytes 712712 | tf_op jit(solution)/shard_map/ppermute | solution.py:52
  38.7 5.3 %collective-permute-start.11 = (bf16[16,3712]{1,0:T(8,128)(2,1)S(1)}, bf16[16,3712]{1,0:T(8,128)(2,1)S(1)}, u32[]{:S(2)}, u32[]{:S(2)}) collective-permute-start(bf16[16,3712]{1,0:T(8,128)(2,1)S(1)} %slice.10), channel_id=1, source_target_pairs={{0,16},{8,24},{16,0},{24,8},{32,48},{40,56},{48,32},{56,40},{64,80... | collective-permute-start | bytes 356360 | tf_op jit(solution)/shard_map/ppermute | solution.py:52
  39.0 7.0 %collective-permute-start.10 = (bf16[16,3712]{1,0:T(8,128)(2,1)S(1)}, bf16[16,3712]{1,0:T(8,128)(2,1)S(1)}, u32[]{:S(2)}, u32[]{:S(2)}) collective-permute-start(bf16[16,3712]{1,0:T(8,128)(2,1)S(1)} %slice.9), channel_id=1, source_target_pairs={{0,32},{8,40},{16,48},{24,56},{32,64},{40,72},{48,80},{56,88},{64,... | collective-permute-start | bytes 356360 | tf_op jit(solution)/shard_map/ppermute | solution.py:52
  39.1 8.2 %collective-permute-start.14 = (bf16[32,3712]{1,0:T(8,128)(2,1)S(1)}, bf16[32,3712]{1,0:T(8,128)(2,1)S(1)}, u32[]{:S(2)}, u32[]{:S(2)}) collective-permute-start(bf16[32,3712]{1,0:T(8,128)(2,1)S(1)} %collective-permute-done.4.refs_2_), channel_id=1, source_target_pairs={{0,8},{8,0},{16,24},{24,16},{32,40},{40,32},{48,56},{56,48},{64,72... | collective-permute-start | bytes 712712 | tf_op jit(solution)/shard_map/ppermute | solution.py:52
  40.3 7.0 %collective-permute-start.12 = (bf16[32,3712]{1,0:T(8,128)(2,1)S(1)}, bf16[32,3712]{1,0:T(8,128)(2,1)S(1)}, u32[]{:S(2)}, u32[]{:S(2)}) collective-permute-start(bf16[32,3712]{1,0:T(8,128)(2,1)S(1)} %collective-permute-done.1.refs_0_), channel_id=1, source_target_pairs={{0,8},{8,0},{16,24},{24,16},{32,40},{40,32},{48,56},{56,48},{64,72... | collective-permute-start | bytes 712712 | tf_op jit(solution)/shard_map/ppermute | solution.py:52
  40.4 6.9 %collective-permute-start.13 = (bf16[32,3712]{1,0:T(8,128)(2,1)S(1)}, bf16[32,3712]{1,0:T(8,128)(2,1)S(1)}, u32[]{:S(2)}, u32[]{:S(2)}) collective-permute-start(bf16[32,3712]{1,0:T(8,128)(2,1)S(1)} %collective-permute-done.3.refs_1_), channel_id=1, source_target_pairs={{0,8},{8,0},{16,24},{24,16},{32,40},{40,32},{48,56},{56,48},{64,72... | collective-permute-start | bytes 712712 | tf_op jit(solution)/shard_map/ppermute | solution.py:52
  44.0 3.0 %collective-permute-start.16 = (bf16[16,3712]{1,0:T(8,128)(2,1)S(1)}, bf16[16,3712]{1,0:T(8,128)(2,1)S(1)}, u32[]{:S(2)}, u32[]{:S(2)}) collective-permute-start(bf16[16,3712]{1,0:T(8,128)(2,1)S(1)} %collective-permute-done.11.refs_4_), channel_id=1, source_target_pairs={{0,8},{8,0},{16,24},{24,16},{32,40},{40,32},{48,56},{56,48},{64,72... | collective-permute-start | bytes 356360 | tf_op jit(solution)/shard_map/ppermute | solution.py:52
  46.0 1.3 collective-permute-start.15
  56.4 40.4 %all-to-all-start = ((bf16[128,6,512]{2,1,0:T(8,128)(2,1)}), bf16[128,6,512]{2,1,0:T(8,128)(2,1)S(1)}, u32[]{:S(2)}, u32[]{:S(2)}) async-start(bf16[128,6,512]{2,1,0:T(8,128)(2,1)} %reshape.26), calls=%async_computation | async-start | bytes 2097152 | tf_op jit(solution)/shard_map/all_to_all | solution.py:409
  64.3 122.9 %reduce-scatter.3.cloned.1.call-start = ((), (), s32[]{:S(2)}) async-start(), calls=%async_computation.7 | async-start | bytes 6881280 | tf_op jit(solution)/shard_map/reduce_scatter | solution.py:337
  64.4 15.2 %collective-permute-start.19 = (f32[8,512]{1,0:T(8,128)S(1)}, f32[8,512]{1,0:T(8,128)S(1)}, u32[]{:S(2)}, u32[]{:S(2)}) collective-permute-start(f32[8,512]{1,0:T(8,128)S(1)} %get-tuple-element.45.refs_0_), channel_id=1, source_target_pairs={{0,24},{8,16},{16,8},{24,0},{32,56},{40,48},{48,40},{56,32},{64,88... | collective-permute-start | bytes 49160 | tf_op jit(solution)/shard_map/ppermute | solution.py:52
  67.6 12.0 %collective-permute-start.18 = (f32[8,512]{1,0:T(8,128)S(1)}, f32[8,512]{1,0:T(8,128)S(1)}, u32[]{:S(2)}, u32[]{:S(2)}) collective-permute-start(f32[8,512]{1,0:T(8,128)S(1)} %get-tuple-element.45.refs_0_), channel_id=1, source_target_pairs={{0,8},{8,0},{16,24},{24,16},{32,40},{40,32},{48,56},{56,48},{64,72... | collective-permute-start | bytes 49160 | tf_op jit(solution)/shard_map/ppermute | solution.py:52
  67.7 11.8 %collective-permute-start.17 = (f32[8,512]{1,0:T(8,128)S(1)}, f32[8,512]{1,0:T(8,128)S(1)}, u32[]{:S(2)}, u32[]{:S(2)}) collective-permute-start(f32[8,512]{1,0:T(8,128)S(1)} %get-tuple-element.45.refs_0_), channel_id=1, source_target_pairs={{0,16},{8,24},{16,0},{24,8},{32,48},{40,56},{48,32},{56,40},{64,80... | collective-permute-start | bytes 49160 | tf_op jit(solution)/shard_map/ppermute | solution.py:52
  79.6 4.0 %collective-permute-start.22 = (f32[8,512]{1,0:T(8,128)S(1)}, f32[8,512]{1,0:T(8,128)S(1)}, u32[]{:S(2)}, u32[]{:S(2)}) collective-permute-start(f32[8,512]{1,0:T(8,128)S(1)} %merge.2.refs_0_), channel_id=1, source_target_pairs={{0,96},{8,104},{16,112},{24,120},{32,0},{40,8},{48,16},{56,24},{64... | collective-permute-start | bytes 49160 | tf_op jit(solution)/shard_map/ppermute | solution.py:52
  82.7 4.1 %collective-permute-start.21 = (f32[8,512]{1,0:T(8,128)S(1)}, f32[8,512]{1,0:T(8,128)S(1)}, u32[]{:S(2)}, u32[]{:S(2)}) collective-permute-start(f32[8,512]{1,0:T(8,128)S(1)} %merge.2.refs_0_), channel_id=1, source_target_pairs={{0,64},{8,72},{16,80},{24,88},{32,96},{40,104},{48,112},{56,120},{... | collective-permute-start | bytes 49160 | tf_op jit(solution)/shard_map/ppermute | solution.py:52
  82.9 4.0 %collective-permute-start.20 = (f32[8,512]{1,0:T(8,128)S(1)}, f32[8,512]{1,0:T(8,128)S(1)}, u32[]{:S(2)}, u32[]{:S(2)}) collective-permute-start(f32[8,512]{1,0:T(8,128)S(1)} %merge.2.refs_0_), channel_id=1, source_target_pairs={{0,32},{8,40},{16,48},{24,56},{32,64},{40,72},{48,80},{56,88},{64,... | collective-permute-start | bytes 49160 | tf_op jit(solution)/shard_map/ppermute | solution.py:52
  117.1 37.1 %all-to-all-start.2 = ((bf16[8,96,1240]{2,1,0:T(8,128)(2,1)}), bf16[8,96,1240]{2,1,0:T(8,128)(2,1)S(1)}, u32[]{:S(2)}, u32[]{:S(2)}) async-start(bf16[8,96,1240]{2,1,0:T(8,128)(2,1)} %copy-done), calls=%async_computation.2 | async-start | bytes 3932160 | tf_op jit(solution)/shard_map/all_to_all | solution.py:409
  122.1 96.0 %reduce-scatter.5.cloned.1.call-start = ((), (), s32[]{:S(2)}) async-start(), calls=%async_computation.8 | async-start | bytes 1146880 | tf_op jit(solution)/shard_map/reduce_scatter | solution.py:337
  122.1 42.1 %collective-permute-start.23 = (bf16[512,896]{1,0:T(8,128)(2,1)}, bf16[512,896]{1,0:T(8,128)(2,1)}, u32[]{:S(2)}, u32[]{:S(2)}) collective-permute-start(bf16[512,896]{1,0:T(8,128)(2,1)} %get-tuple-element.59), channel_id=1, source_target_pairs={{0,4},{1,5},{2,6},{3,7},{4,0},{5,1},{6,2},{7,3},{8,12},{9,13},{10,... | collective-permute-start | bytes 2752520 | tf_op jit(solution)/shard_map/ppermute | solution.py:333
  166.5 19.8 %copy-start.3 = (bf16[448,1184]{1,0:T(8,128)(2,1)S(1)}, bf16[448,1184]{1,0:T(8,128)(2,1)}, u32[]{:S(2)}) copy-start(bf16[448,1184]{1,0:T(8,128)(2,1)} %up_ref.3) | copy-start | bytes 3182596
  188.6 28.5 %copy-start.13 = (bf16[2,3584]{1,0:T(2,128)(2,1)S(1)}, bf16[2,3584]{1,0:T(2,128)(2,1)}, u32[]{:S(2)}) copy-start(bf16[2,3584]{1,0:T(2,128)(2,1)} %hidden_ref.1) | copy-start | bytes 43012
  189.0 29.1 %collective-permute-start.24 = (bf16[128,2688]{1,0:T(8,128)(2,1)S(1)}, bf16[128,2688]{1,0:T(8,128)(2,1)S(1)}, u32[]{:S(2)}, u32[]{:S(2)}) collective-permute-start(bf16[128,2688]{1,0:T(8,128)(2,1)S(1)} %get-tuple-element.69), channel_id=1, source_target_pairs={{0,4},{1,5},{2,6},{3,7},{4,0},{5,1},{6,2},{7,3},{8,12},{9,13},{10,... | collective-permute-start | bytes 2064392 | tf_op jit(solution)/shard_map/ppermute | solution.py:333
  191.1 26.0 %all-to-all-start.4 = ((bf16[128,2,448]{2,1,0:T(2,128)(2,1)}), bf16[128,2,448]{2,1,0:T(2,128)(2,1)S(1)}, u32[]{:S(2)}, u32[]{:S(2)}) async-start(bf16[128,2,448]{2,1,0:T(2,128)(2,1)} %reshape.28), calls=%async_computation.6 | async-start | bytes 524288 | tf_op jit(solution)/shard_map/all_to_all | solution.py:409
  (18 other events, 51.3 us)
Sparse Core Ops, SparseCore 0:
  98.1 78.3 reduce-scatter.2
  178.9 33.8 reduce-scatter.4

commit v5 on v4

--- a/solution.py
+++ b/solution.py
@@ -294,7 +294,7 @@
         out_shape=[loss, shape((shard_rows, Y_FIRST), bf16)]
         + [shape((GY * rows, dim - Y_FIRST), bf16)] * 2,
         scratch_shapes=[pltpu.VMEM((1, 2 * half), f32)],
-        compiler_params=pltpu.CompilerParams(vmem_limit_bytes=52 * 1024 * 1024),
+        compiler_params=pltpu.CompilerParams(vmem_limit_bytes=28 * 1024 * 1024),
         cost_estimate=pl.CostEstimate(
             flops=4 * shard_rows * half * dim, bytes_accessed=4 * shard_rows * dim, transcendentals=0
         ),

time: 228 us -> 232 us (1.018)
  local copies, waits for them, and re-layouts: 21.2 us -> 28.7 us
  Pallas kernels: 27 us -> 23.5 us
    unnamed x40 -> x52, local copies, waits for them, and re-layouts: 17.9 us -> 25.3 us
    pallas_call x1, Pallas kernels: 8.93 us -> 5.4 us  [passage_terms(): pl.pallas_call(weight_kernel, grid=(GY,), in_specs=[SMEM, fixed(stats), f...]
  transfers between devices with their start and end apart: 30 -> 30, of which waited for: 10 -> 10; matrix products, arithmetic and copies ran while one was open for 1% -> 1% of each run, Pallas kernels for 8% -> 6%
where the time goes in v5:
time: 232 us; the launch traced here: 231 us
  waiting for transfers between devices  76.4 us (33%)
  starting transfers between devices  54.6 us (24%)
  blocking collectives  33.7 us (15%)
  local copies, waits for them, and re-layouts  28.7 us (12%)
  Pallas kernels  23.5 us (10%)
  between operations  14.3 us (6%)
    all_to_all x3, waiting for transfers between devices, exchange(): return lax.all_to_all(v, axis, 0, 0, tiled=True)  45.7 us
    all_to_all x2, blocking collectives, exchange(): return lax.all_to_all(v, axis, 0, 0, tiled=True)  33.7 us
    ppermute x23, starting transfers between devices, send(): return lax.ppermute(v, 'blk', blk_shift(*shift))  28.5 us
    unnamed x52, local copies, waits for them, and re-layouts  25.3 us
    all_to_all x3, starting transfers between devices, exchange(): return lax.all_to_all(v, axis, 0, 0, tiled=True)  23.4 us
    ppermute x23, waiting for transfers between devices, send(): return lax.ppermute(v, 'blk', blk_shift(*shift))  21.2 us
    ppermute x2, waiting for transfers between devices, send_x(): return lax.ppermute(v, 'grp', [(g, (g + GY) % N_GRP) for g in range(N_GRP)])  9.45 us
    pallas_call x1, Pallas kernels, shards(): local(second_kernel, 'second_scores', [shape((8, cols), f32), shape((N_GR...  5.56 us
  transfers between devices with their start and end apart: 30, of which 10 were waited for; matrix products, arithmetic and copies ran while one was open for 1% of the time, Pallas kernels for 6%

profile of v5, /device:TPU:1, one launch (start us, length us, event | category | flops | bytes accessed | tf_op | source)
XLA Modules:
  0.0 231.2 jit_solution(14816786984162971015)
XLA Ops:
  9.3 2.5 %collective-permute-start.5 = (bf16[32,3712]{1,0:T(8,128)(2,1)S(1)}, bf16[32,3712]{1,0:T(8,128)(2,1)S(1)}, u32[]{:S(2)}, u32[]{:S(2)}) collective-permute-start(bf16[32,3712]{1,0:T(8,128)(2,1)S(1)} %block.1.refs_0_), channel_id=1, source_target_pairs={{0,32},{8,40},{16,48},{24,56},{32,64},{40,72},{48,80},{56,88},{64,... | collective-permute-start | bytes 712712 | tf_op jit(solution)/shard_map/ppermute | solution.py:52
  11.9 2.2 collective-permute-start.2
  14.1 2.7 %collective-permute-start = (bf16[32,3712]{1,0:T(8,128)(2,1)S(1)}, bf16[32,3712]{1,0:T(8,128)(2,1)S(1)}, u32[]{:S(2)}, u32[]{:S(2)}) collective-permute-start(bf16[32,3712]{1,0:T(8,128)(2,1)S(1)} %block.1.refs_0_), channel_id=1, source_target_pairs={{0,16},{8,24},{16,0},{24,8},{32,48},{40,56},{48,32},{56,40},{64,80... | collective-permute-start | bytes 712712 | tf_op jit(solution)/shard_map/ppermute | solution.py:52
  18.1 1.4 collective-permute-done.5.refs_1_
  21.9 1.9 collective-permute-start.9
  24.5 2.8 %collective-permute-start.4 = (bf16[32,3712]{1,0:T(8,128)(2,1)S(1)}, bf16[32,3712]{1,0:T(8,128)(2,1)S(1)}, u32[]{:S(2)}, u32[]{:S(2)}) collective-permute-start(bf16[32,3712]{1,0:T(8,128)(2,1)S(1)} %collective-permute-done.2.refs_2_), channel_id=1, source_target_pairs={{0,16},{8,24},{16,0},{24,8},{32,48},{40,56},{48,32},{56,40},{64,80... | collective-permute-start | bytes 712712 | tf_op jit(solution)/shard_map/ppermute | solution.py:52
  27.3 1.4 collective-permute-start.3
  29.5 3.1 %copy-done.16 = bf16[1024,3584]{1,0:T(8,128)(2,1)S(1)} copy-done((bf16[1024,3584]{1,0:T(8,128)(2,1)S(1)}, bf16[1024,3584]{1,0:T(8,128)(2,1)}, u32[]{:S(2)}) %copy-start.16) | copy-done | bytes 7340056
  32.6 3.8 %first_scores.1 = (bf16[8,3584]{1,0:T(8,128)(2,1)S(1)}, f32[1024,256]{1,0:T(8,128)S(1)}, bf16[256,3584]{1,0:T(8,128)(2,1)S(1)}, f32[8,256]{1,0:T(8,128)S(1)}, s3...) custom-call(s32[1]{0:T(128)} %bitcast.1.blk_ref, bf16[32,3712]{1,0:T(8,128)(2,1)S(1)} %block.1.refs_0_, ...), custom_call_target="tpu_custom_call" | custom-call | flops 3758096384 | bytes 14680064 | tf_op jit(solution)/shard_map/first_scores/pallas_call | solution.py:433
  40.8 3.2 %collective-permute-done.11.refs_4_ = bf16[16,3712]{1,0:T(8,128)(2,1)S(1)} collective-permute-done((bf16[16,3712]{1,0:T(8,128)(2,1)S(1)}, bf16[16,3712]{1,0:T(8,128)(2,1)S(1)}, u32[]{:S(2)}, u32[]{:S(2)}) %collective-permute-start.11) | collective-permute-done | bytes 118816 | tf_op jit(solution)/shard_map/ppermute | solution.py:52
  44.0 2.0 collective-permute-start.16
  47.3 5.6 %second_scores.1 = (f32[8,512]{1,0:T(8,128)S(1)}, bf16[8,96,512]{2,1,0:T(8,128)(2,1)S(1)}, bf16[512,512]{1,0:T(8,128)(2,1)S(1)}, f32[1024,256]{1,0:T(8,128)S(1)}...) custom-call(s32[1]{0:T(128)} %bitcast.1.blk_ref, bf16[32,3712]{1,0:T(8,128)(2,1)S(1)} %collective-permute-done.1.refs_0_, ...), custom_call_target="tpu_custom_call" | custom-call | flops 3758096384 | bytes 14680064 | tf_op jit(solution)/shard_map/second_scores/pallas_call | solution.py:452
  56.4 7.9 %all-to-all-start = ((bf16[128,6,512]{2,1,0:T(8,128)(2,1)}), bf16[128,6,512]{2,1,0:T(8,128)(2,1)S(1)}, u32[]{:S(2)}, u32[]{:S(2)}) async-start(bf16[128,6,512]{2,1,0:T(8,128)(2,1)} %reshape.26), calls=%async_computation | async-start | bytes 2097152 | tf_op jit(solution)/shard_map/all_to_all | solution.py:409
  64.3 3.2 %collective-permute-start.19 = (f32[8,512]{1,0:T(8,128)S(1)}, f32[8,512]{1,0:T(8,128)S(1)}, u32[]{:S(2)}, u32[]{:S(2)}) collective-permute-start(f32[8,512]{1,0:T(8,128)S(1)} %get-tuple-element.45.refs_0_), channel_id=1, source_target_pairs={{0,24},{8,16},{16,8},{24,0},{32,56},{40,48},{48,40},{56,32},{64,88... | collective-permute-start | bytes 49160 | tf_op jit(solution)/shard_map/ppermute | solution.py:52
  68.3 11.2 %collective-permute-done.19.refs_3_ = f32[8,512]{1,0:T(8,128)S(1)} collective-permute-done((f32[8,512]{1,0:T(8,128)S(1)}, f32[8,512]{1,0:T(8,128)S(1)}, u32[]{:S(2)}, u32[]{:S(2)}) %collective-permute-start.19) | collective-permute-done | bytes 16416 | tf_op jit(solution)/shard_map/ppermute | solution.py:52
  79.6 3.2 %collective-permute-start.22 = (f32[8,512]{1,0:T(8,128)S(1)}, f32[8,512]{1,0:T(8,128)S(1)}, u32[]{:S(2)}, u32[]{:S(2)}) collective-permute-start(f32[8,512]{1,0:T(8,128)S(1)} %merge.2.refs_0_), channel_id=1, source_target_pairs={{0,96},{8,104},{16,112},{24,120},{32,0},{40,8},{48,16},{56,24},{64... | collective-permute-start | bytes 49160 | tf_op jit(solution)/shard_map/ppermute | solution.py:52
  83.6 3.2 %collective-permute-done.21.refs_2_ = f32[8,512]{1,0:T(8,128)S(1)} collective-permute-done((f32[8,512]{1,0:T(8,128)S(1)}, f32[8,512]{1,0:T(8,128)S(1)}, u32[]{:S(2)}, u32[]{:S(2)}) %collective-permute-start.21) | collective-permute-done | bytes 16416 | tf_op jit(solution)/shard_map/ppermute | solution.py:52
  88.1 1.5 copy-done.23
  89.6 1.5 copy-done.25
  91.1 5.4 %passage_terms.1 = (f32[1,512]{1,0:T(1,128)S(1)}, bf16[1024,2688]{1,0:T(8,128)(2,1)S(1)}, bf16[512,896]{1,0:T(8,128)(2,1)S(1)}, bf16[512,896]{1,0:T(8,128)(2,1)S(1)}) custom-call(s32[1]{0:T(128)} %bitcast.grp_ref, f32[8,512]{1,0:T(8,128)S(1)} %merge.3.stats_ref, s32[1,256]{1,0:T(1,128)S(1)} %get-tuple-element.46.pos_a, ...), custom_call_target="tpu_custom_call" | custom-call | flops 3758096384 | bytes 14680064 | tf_op jit(solution)/shard_map/passage_terms/pallas_call | solution.py:288
  96.5 2.4 %copy-done.1 = bf16[1024,2688]{1,0:T(8,128)(2,1)} copy-done((bf16[1024,2688]{1,0:T(8,128)(2,1)}, bf16[1024,2688]{1,0:T(8,128)(2,1)S(1)}, u32[]{:S(2)}) %copy-start.1) | copy-done | bytes 5505048
  101.9 13.9 %all_to_all.25.cot_ref = bf16[16,16,448]{2,1,0:T(8,128)(2,1)S(1)} all-to-all(bf16[16,16,448]{2,1,0:T(8,128)(2,1)S(1)} %cotangents.1), channel_id=1, replica_groups=mesh['blk'=16,'grp'=8] {'blk'}, dimensions={0} | all-to-all | bytes 458752 | tf_op jit(solution)/shard_map/all_to_all | solution.py:409
  118.3 1.4 act.1
  121.1 5.0 %all-to-all-start.2 = ((bf16[8,96,1240]{2,1,0:T(8,128)(2,1)}), bf16[8,96,1240]{2,1,0:T(8,128)(2,1)S(1)}, u32[]{:S(2)}, u32[]{:S(2)}) async-start(bf16[8,96,1240]{2,1,0:T(8,128)(2,1)} %copy-done), calls=%async_computation.2 | async-start | bytes 3932160 | tf_op jit(solution)/shard_map/all_to_all | solution.py:409
  126.1 1.4 collective-permute-start.23
  127.5 30.6 %all-to-all-done.2.got_ref = bf16[8,96,1240]{2,1,0:T(8,128)(2,1)S(1)} async-done(((bf16[8,96,1240]{2,1,0:T(8,128)(2,1)}), bf16[8,96,1240]{2,1,0:T(8,128)(2,1)S(1)}, u32[]{:S(2)}, u32[]{:S(2)}) %all-to-all-start.2) | async-done | bytes 1904672 | tf_op jit(solution)/shard_map/all_to_all | solution.py:409
  158.7 9.4 %collective-permute-done.23.got_ref = bf16[512,896]{1,0:T(8,128)(2,1)} collective-permute-done((bf16[512,896]{1,0:T(8,128)(2,1)}, bf16[512,896]{1,0:T(8,128)(2,1)}, u32[]{:S(2)}, u32[]{:S(2)}) %collective-permute-start.23) | collective-permute-done | bytes 917536 | tf_op jit(solution)/shard_map/ppermute | solution.py:333
  168.2 1.4 x_sum.1
  170.6 19.8 %all_to_all.26.grad_ref = bf16[8,64,1184]{2,1,0:T(8,128)(2,1)S(1)} all-to-all(bf16[8,64,1184]{2,1,0:T(8,128)(2,1)} %copy-done.7), channel_id=1, replica_groups=mesh['blk'=16,'grp'=8] {'grp'}, dimensions={0} | all-to-all | bytes 2424832 | tf_op jit(solution)/shard_map/all_to_all | solution.py:409
  195.0 10.5 %all-to-all-start.4 = ((bf16[128,2,448]{2,1,0:T(2,128)(2,1)}), bf16[128,2,448]{2,1,0:T(2,128)(2,1)S(1)}, u32[]{:S(2)}, u32[]{:S(2)}) async-start(bf16[128,2,448]{2,1,0:T(2,128)(2,1)} %reshape.28), calls=%async_computation.6 | async-start | bytes 524288 | tf_op jit(solution)/shard_map/all_to_all | solution.py:409
  206.0 15.0 %all-to-all-done.4 = bf16[128,2,448]{2,1,0:T(2,128)(2,1)S(1)} async-done(((bf16[128,2,448]{2,1,0:T(2,128)(2,1)}), bf16[128,2,448]{2,1,0:T(2,128)(2,1)S(1)}, u32[]{:S(2)}, u32[]{:S(2)}) %all-to-all-start.4) | async-done | bytes 229408 | tf_op jit(solution)/shard_map/all_to_all | solution.py:409
  223.0 1.4 passages.1
  (104 shorter events, 34.9 us)
Async XLA Ops:
  9.3 10.2 %collective-permute-start.5 = (bf16[32,3712]{1,0:T(8,128)(2,1)S(1)}, bf16[32,3712]{1,0:T(8,128)(2,1)S(1)}, u32[]{:S(2)}, u32[]{:S(2)}) collective-permute-start(bf16[32,3712]{1,0:T(8,128)(2,1)S(1)} %block.1.refs_0_), channel_id=1, source_target_pairs={{0,32},{8,40},{16,48},{24,56},{32,64},{40,72},{48,80},{56,88},{64,... | collective-permute-start | bytes 712712 | tf_op jit(solution)/shard_map/ppermute | solution.py:52
  11.9 8.9 %collective-permute-start.2 = (bf16[32,3712]{1,0:T(8,128)(2,1)S(1)}, bf16[32,3712]{1,0:T(8,128)(2,1)S(1)}, u32[]{:S(2)}, u32[]{:S(2)}) collective-permute-start(bf16[32,3712]{1,0:T(8,128)(2,1)S(1)} %block.1.refs_0_), channel_id=1, source_target_pairs={{0,96},{8,104},{16,112},{24,120},{32,0},{40,8},{48,16},{56,24},{64... | collective-permute-start | bytes 712712 | tf_op jit(solution)/shard_map/ppermute | solution.py:52
  14.1 7.8 %collective-permute-start = (bf16[32,3712]{1,0:T(8,128)(2,1)S(1)}, bf16[32,3712]{1,0:T(8,128)(2,1)S(1)}, u32[]{:S(2)}, u32[]{:S(2)}) collective-permute-start(bf16[32,3712]{1,0:T(8,128)(2,1)S(1)} %block.1.refs_0_), channel_id=1, source_target_pairs={{0,16},{8,24},{16,0},{24,8},{32,48},{40,56},{48,32},{56,40},{64,80... | collective-permute-start | bytes 712712 | tf_op jit(solution)/shard_map/ppermute | solution.py:52
  16.8 10.5 %collective-permute-start.6 = (bf16[32,3712]{1,0:T(8,128)(2,1)S(1)}, bf16[32,3712]{1,0:T(8,128)(2,1)S(1)}, u32[]{:S(2)}, u32[]{:S(2)}) collective-permute-start(bf16[32,3712]{1,0:T(8,128)(2,1)S(1)} %block.1.refs_0_), channel_id=1, source_target_pairs={{0,8},{8,0},{16,24},{24,16},{32,40},{40,32},{48,56},{56,48},{64,72... | collective-permute-start | bytes 712712 | tf_op jit(solution)/shard_map/ppermute | solution.py:52
  19.5 9.2 %collective-permute-start.7 = (bf16[32,3712]{1,0:T(8,128)(2,1)S(1)}, bf16[32,3712]{1,0:T(8,128)(2,1)S(1)}, u32[]{:S(2)}, u32[]{:S(2)}) collective-permute-start(bf16[32,3712]{1,0:T(8,128)(2,1)S(1)} %collective-permute-done.5.refs_1_), channel_id=1, source_target_pairs={{0,8},{8,0},{16,24},{24,16},{32,40},{40,32},{48,56},{56,48},{64,72... | collective-permute-start | bytes 712712 | tf_op jit(solution)/shard_map/ppermute | solution.py:52
  20.7 8.1 %collective-permute-start.8 = (bf16[32,3712]{1,0:T(8,128)(2,1)S(1)}, bf16[32,3712]{1,0:T(8,128)(2,1)S(1)}, u32[]{:S(2)}, u32[]{:S(2)}) collective-permute-start(bf16[32,3712]{1,0:T(8,128)(2,1)S(1)} %collective-permute-done.2.refs_2_), channel_id=1, source_target_pairs={{0,8},{8,0},{16,24},{24,16},{32,40},{40,32},{48,56},{56,48},{64,72... | collective-permute-start | bytes 712712 | tf_op jit(solution)/shard_map/ppermute | solution.py:52
  21.9 6.9 %collective-permute-start.9 = (bf16[32,3712]{1,0:T(8,128)(2,1)S(1)}, bf16[32,3712]{1,0:T(8,128)(2,1)S(1)}, u32[]{:S(2)}, u32[]{:S(2)}) collective-permute-start(bf16[32,3712]{1,0:T(8,128)(2,1)S(1)} %collective-permute-done.refs_3_), channel_id=1, source_target_pairs={{0,8},{8,0},{16,24},{24,16},{32,40},{40,32},{48,56},{56,48},{64,72... | collective-permute-start | bytes 712712 | tf_op jit(solution)/shard_map/ppermute | solution.py:52
  24.5 14.1 %collective-permute-start.4 = (bf16[32,3712]{1,0:T(8,128)(2,1)S(1)}, bf16[32,3712]{1,0:T(8,128)(2,1)S(1)}, u32[]{:S(2)}, u32[]{:S(2)}) collective-permute-start(bf16[32,3712]{1,0:T(8,128)(2,1)S(1)} %collective-permute-done.2.refs_2_), channel_id=1, source_target_pairs={{0,16},{8,24},{16,0},{24,8},{32,48},{40,56},{48,32},{56,40},{64,80... | collective-permute-start | bytes 712712 | tf_op jit(solution)/shard_map/ppermute | solution.py:52
  27.3 11.3 %collective-permute-start.3 = (bf16[32,3712]{1,0:T(8,128)(2,1)S(1)}, bf16[32,3712]{1,0:T(8,128)(2,1)S(1)}, u32[]{:S(2)}, u32[]{:S(2)}) collective-permute-start(bf16[32,3712]{1,0:T(8,128)(2,1)S(1)} %collective-permute-done.2.refs_2_), channel_id=1, source_target_pairs={{0,96},{8,104},{16,112},{24,120},{32,0},{40,8},{48,16},{56,24},{64... | collective-permute-start | bytes 712712 | tf_op jit(solution)/shard_map/ppermute | solution.py:52
  28.7 9.9 %collective-permute-start.1 = (bf16[32,3712]{1,0:T(8,128)(2,1)S(1)}, bf16[32,3712]{1,0:T(8,128)(2,1)S(1)}, u32[]{:S(2)}, u32[]{:S(2)}) collective-permute-start(bf16[32,3712]{1,0:T(8,128)(2,1)S(1)} %collective-permute-done.refs_3_), channel_id=1, source_target_pairs={{0,32},{8,40},{16,48},{24,56},{32,64},{40,72},{48,80},{56,88},{64,... | collective-permute-start | bytes 712712 | tf_op jit(solution)/shard_map/ppermute | solution.py:52
  38.7 5.3 %collective-permute-start.11 = (bf16[16,3712]{1,0:T(8,128)(2,1)S(1)}, bf16[16,3712]{1,0:T(8,128)(2,1)S(1)}, u32[]{:S(2)}, u32[]{:S(2)}) collective-permute-start(bf16[16,3712]{1,0:T(8,128)(2,1)S(1)} %slice.10), channel_id=1, source_target_pairs={{0,16},{8,24},{16,0},{24,8},{32,48},{40,56},{48,32},{56,40},{64,80... | collective-permute-start | bytes 356360 | tf_op jit(solution)/shard_map/ppermute | solution.py:52
  39.0 7.0 %collective-permute-start.10 = (bf16[16,3712]{1,0:T(8,128)(2,1)S(1)}, bf16[16,3712]{1,0:T(8,128)(2,1)S(1)}, u32[]{:S(2)}, u32[]{:S(2)}) collective-permute-start(bf16[16,3712]{1,0:T(8,128)(2,1)S(1)} %slice.9), channel_id=1, source_target_pairs={{0,32},{8,40},{16,48},{24,56},{32,64},{40,72},{48,80},{56,88},{64,... | collective-permute-start | bytes 356360 | tf_op jit(solution)/shard_map/ppermute | solution.py:52
  39.1 8.2 %collective-permute-start.14 = (bf16[32,3712]{1,0:T(8,128)(2,1)S(1)}, bf16[32,3712]{1,0:T(8,128)(2,1)S(1)}, u32[]{:S(2)}, u32[]{:S(2)}) collective-permute-start(bf16[32,3712]{1,0:T(8,128)(2,1)S(1)} %collective-permute-done.4.refs_2_), channel_id=1, source_target_pairs={{0,8},{8,0},{16,24},{24,16},{32,40},{40,32},{48,56},{56,48},{64,72... | collective-permute-start | bytes 712712 | tf_op jit(solution)/shard_map/ppermute | solution.py:52
  40.3 7.0 %collective-permute-start.12 = (bf16[32,3712]{1,0:T(8,128)(2,1)S(1)}, bf16[32,3712]{1,0:T(8,128)(2,1)S(1)}, u32[]{:S(2)}, u32[]{:S(2)}) collective-permute-start(bf16[32,3712]{1,0:T(8,128)(2,1)S(1)} %collective-permute-done.1.refs_0_), channel_id=1, source_target_pairs={{0,8},{8,0},{16,24},{24,16},{32,40},{40,32},{48,56},{56,48},{64,72... | collective-permute-start | bytes 712712 | tf_op jit(solution)/shard_map/ppermute | solution.py:52
  40.4 6.9 %collective-permute-start.13 = (bf16[32,3712]{1,0:T(8,128)(2,1)S(1)}, bf16[32,3712]{1,0:T(8,128)(2,1)S(1)}, u32[]{:S(2)}, u32[]{:S(2)}) collective-permute-start(bf16[32,3712]{1,0:T(8,128)(2,1)S(1)} %collective-permute-done.3.refs_1_), channel_id=1, source_target_pairs={{0,8},{8,0},{16,24},{24,16},{32,40},{40,32},{48,56},{56,48},{64,72... | collective-permute-start | bytes 712712 | tf_op jit(solution)/shard_map/ppermute | solution.py:52
  44.0 3.0 %collective-permute-start.16 = (bf16[16,3712]{1,0:T(8,128)(2,1)S(1)}, bf16[16,3712]{1,0:T(8,128)(2,1)S(1)}, u32[]{:S(2)}, u32[]{:S(2)}) collective-permute-start(bf16[16,3712]{1,0:T(8,128)(2,1)S(1)} %collective-permute-done.11.refs_4_), channel_id=1, source_target_pairs={{0,8},{8,0},{16,24},{24,16},{32,40},{40,32},{48,56},{56,48},{64,72... | collective-permute-start | bytes 356360 | tf_op jit(solution)/shard_map/ppermute | solution.py:52
  46.0 1.3 collective-permute-start.15
  55.1 31.7 %copy-start.19 = (f32[1024,256]{1,0:T(8,128)S(1)}, f32[1024,256]{1,0:T(8,128)}, u32[]{:S(2)}) copy-start(f32[1024,256]{1,0:T(8,128)} %copy-done.18) | copy-start | bytes 3145732
  56.4 44.4 %all-to-all-start = ((bf16[128,6,512]{2,1,0:T(8,128)(2,1)}), bf16[128,6,512]{2,1,0:T(8,128)(2,1)S(1)}, u32[]{:S(2)}, u32[]{:S(2)}) async-start(bf16[128,6,512]{2,1,0:T(8,128)(2,1)} %reshape.26), calls=%async_computation | async-start | bytes 2097152 | tf_op jit(solution)/shard_map/all_to_all | solution.py:409
  64.3 127.0 %reduce-scatter.3.cloned.1.call-start = ((), (), s32[]{:S(2)}) async-start(), calls=%async_computation.7 | async-start | bytes 6881280 | tf_op jit(solution)/shard_map/reduce_scatter | solution.py:337
  64.3 15.2 %collective-permute-start.19 = (f32[8,512]{1,0:T(8,128)S(1)}, f32[8,512]{1,0:T(8,128)S(1)}, u32[]{:S(2)}, u32[]{:S(2)}) collective-permute-start(f32[8,512]{1,0:T(8,128)S(1)} %get-tuple-element.45.refs_0_), channel_id=1, source_target_pairs={{0,24},{8,16},{16,8},{24,0},{32,56},{40,48},{48,40},{56,32},{64,88... | collective-permute-start | bytes 49160 | tf_op jit(solution)/shard_map/ppermute | solution.py:52
  67.6 12.0 %collective-permute-start.18 = (f32[8,512]{1,0:T(8,128)S(1)}, f32[8,512]{1,0:T(8,128)S(1)}, u32[]{:S(2)}, u32[]{:S(2)}) collective-permute-start(f32[8,512]{1,0:T(8,128)S(1)} %get-tuple-element.45.refs_0_), channel_id=1, source_target_pairs={{0,8},{8,0},{16,24},{24,16},{32,40},{40,32},{48,56},{56,48},{64,72... | collective-permute-start | bytes 49160 | tf_op jit(solution)/shard_map/ppermute | solution.py:52
  67.7 11.8 %collective-permute-start.17 = (f32[8,512]{1,0:T(8,128)S(1)}, f32[8,512]{1,0:T(8,128)S(1)}, u32[]{:S(2)}, u32[]{:S(2)}) collective-permute-start(f32[8,512]{1,0:T(8,128)S(1)} %get-tuple-element.45.refs_0_), channel_id=1, source_target_pairs={{0,16},{8,24},{16,0},{24,8},{32,48},{40,56},{48,32},{56,40},{64,80... | collective-permute-start | bytes 49160 | tf_op jit(solution)/shard_map/ppermute | solution.py:52
  79.6 4.0 %collective-permute-start.22 = (f32[8,512]{1,0:T(8,128)S(1)}, f32[8,512]{1,0:T(8,128)S(1)}, u32[]{:S(2)}, u32[]{:S(2)}) collective-permute-start(f32[8,512]{1,0:T(8,128)S(1)} %merge.2.refs_0_), channel_id=1, source_target_pairs={{0,96},{8,104},{16,112},{24,120},{32,0},{40,8},{48,16},{56,24},{64... | collective-permute-start | bytes 49160 | tf_op jit(solution)/shard_map/ppermute | solution.py:52
  82.7 4.1 %collective-permute-start.21 = (f32[8,512]{1,0:T(8,128)S(1)}, f32[8,512]{1,0:T(8,128)S(1)}, u32[]{:S(2)}, u32[]{:S(2)}) collective-permute-start(f32[8,512]{1,0:T(8,128)S(1)} %merge.2.refs_0_), channel_id=1, source_target_pairs={{0,64},{8,72},{16,80},{24,88},{32,96},{40,104},{48,112},{56,120},{... | collective-permute-start | bytes 49160 | tf_op jit(solution)/shard_map/ppermute | solution.py:52
  82.8 4.0 %collective-permute-start.20 = (f32[8,512]{1,0:T(8,128)S(1)}, f32[8,512]{1,0:T(8,128)S(1)}, u32[]{:S(2)}, u32[]{:S(2)}) collective-permute-start(f32[8,512]{1,0:T(8,128)S(1)} %merge.2.refs_0_), channel_id=1, source_target_pairs={{0,32},{8,40},{16,48},{24,56},{32,64},{40,72},{48,80},{56,88},{64,... | collective-permute-start | bytes 49160 | tf_op jit(solution)/shard_map/ppermute | solution.py:52
  121.1 37.1 %all-to-all-start.2 = ((bf16[8,96,1240]{2,1,0:T(8,128)(2,1)}), bf16[8,96,1240]{2,1,0:T(8,128)(2,1)S(1)}, u32[]{:S(2)}, u32[]{:S(2)}) async-start(bf16[8,96,1240]{2,1,0:T(8,128)(2,1)} %copy-done), calls=%async_computation.2 | async-start | bytes 3932160 | tf_op jit(solution)/shard_map/all_to_all | solution.py:409
  126.0 96.0 %reduce-scatter.5.cloned.1.call-start = ((), (), s32[]{:S(2)}) async-start(), calls=%async_computation.8 | async-start | bytes 1146880 | tf_op jit(solution)/shard_map/reduce_scatter | solution.py:337
  126.1 42.1 %collective-permute-start.23 = (bf16[512,896]{1,0:T(8,128)(2,1)}, bf16[512,896]{1,0:T(8,128)(2,1)}, u32[]{:S(2)}, u32[]{:S(2)}) collective-permute-start(bf16[512,896]{1,0:T(8,128)(2,1)} %copy-done.17), channel_id=1, source_target_pairs={{0,4},{1,5},{2,6},{3,7},{4,0},{5,1},{6,2},{7,3},{8,12},{9,13},{10,... | collective-permute-start | bytes 2752520 | tf_op jit(solution)/shard_map/ppermute | solution.py:333
  192.6 28.5 %copy-start.14 = (bf16[2,3584]{1,0:T(2,128)(2,1)S(1)}, bf16[2,3584]{1,0:T(2,128)(2,1)}, u32[]{:S(2)}) copy-start(bf16[2,3584]{1,0:T(2,128)(2,1)} %hidden_ref.1) | copy-start | bytes 43012
  193.0 29.1 %collective-permute-start.24 = (bf16[128,2688]{1,0:T(8,128)(2,1)S(1)}, bf16[128,2688]{1,0:T(8,128)(2,1)S(1)}, u32[]{:S(2)}, u32[]{:S(2)}) collective-permute-start(bf16[128,2688]{1,0:T(8,128)(2,1)S(1)} %get-tuple-element.69), channel_id=1, source_target_pairs={{0,4},{1,5},{2,6},{3,7},{4,0},{5,1},{6,2},{7,3},{8,12},{9,13},{10,... | collective-permute-start | bytes 2064392 | tf_op jit(solution)/shard_map/ppermute | solution.py:333
  195.0 26.1 %all-to-all-start.4 = ((bf16[128,2,448]{2,1,0:T(2,128)(2,1)}), bf16[128,2,448]{2,1,0:T(2,128)(2,1)S(1)}, u32[]{:S(2)}, u32[]{:S(2)}) async-start(bf16[128,2,448]{2,1,0:T(2,128)(2,1)} %reshape.28), calls=%async_computation.6 | async-start | bytes 524288 | tf_op jit(solution)/shard_map/all_to_all | solution.py:409
  (24 other events, 78.6 us)
Sparse Core Ops, SparseCore 0:
  102.0 78.3 reduce-scatter.2
  182.8 33.5 reduce-scatter.4

commit v6 on v4

--- a/solution.py
+++ b/solution.py
@@ -18,7 +18,7 @@
 SUB = 2
 WIDE = 3 * SUB
 LANES = 512
-Y_FIRST = 2688
+Y_FIRST = 2560
 GX, GY = 2, 4
 Y_GROUPS = [[x * GY + y for y in range(GY)] for x in range(GX)]
 TILE = 256

time: 228 us -> 228 us (level)
    all_to_all x3, waiting for transfers between devices: 45.7 us -> 42 us  [exchange(): return lax.all_to_all(v, axis, 0, 0, tiled=True)]
    ppermute x2, waiting for transfers between devices: 9.45 us -> 12.3 us  [send_x(): return lax.ppermute(v, 'grp', [(g, (g + GY) % N_GRP) for g in range(N_GRP)])]
where the time goes in v6:
time: 228 us; the launch traced here: 227 us
  waiting for transfers between devices  75.6 us (33%)
  starting transfers between devices  55.6 us (24%)
  blocking collectives  33.6 us (15%)
  Pallas kernels  26.9 us (12%)
  local copies, waits for them, and re-layouts  21.2 us (9%)
  between operations  14.3 us (6%)
    all_to_all x3, waiting for transfers between devices, exchange(): return lax.all_to_all(v, axis, 0, 0, tiled=True)  42 us
    all_to_all x2, blocking collectives, exchange(): return lax.all_to_all(v, axis, 0, 0, tiled=True)  33.6 us
    ppermute x23, starting transfers between devices, send(): return lax.ppermute(v, 'blk', blk_shift(*shift))  28.5 us
    all_to_all x3, starting transfers between devices, exchange(): return lax.all_to_all(v, axis, 0, 0, tiled=True)  24.7 us
    ppermute x23, waiting for transfers between devices, send(): return lax.ppermute(v, 'blk', blk_shift(*shift))  21.2 us
    unnamed x40, local copies, waits for them, and re-layouts  17.8 us
    ppermute x2, waiting for transfers between devices, send_x(): return lax.ppermute(v, 'grp', [(g, (g + GY) % N_GRP) for g in range(N_GRP)])  12.3 us
    pallas_call x1, Pallas kernels, passage_terms(): pl.pallas_call(weight_kernel, grid=(GY,), in_specs=[SMEM, fixed(stats), f...  8.81 us
  transfers between devices with their start and end apart: 30, of which 10 were waited for; matrix products, arithmetic and copies ran while one was open for 1% of the time, Pallas kernels for 8%

profile of v6, /device:TPU:1, one launch (start us, length us, event | category | flops | bytes accessed | tf_op | source)
XLA Modules:
  0.0 227.2 jit_solution(5545886178684170220)
XLA Ops:
  9.3 2.5 %collective-permute-start.5 = (bf16[32,3712]{1,0:T(8,128)(2,1)S(1)}, bf16[32,3712]{1,0:T(8,128)(2,1)S(1)}, u32[]{:S(2)}, u32[]{:S(2)}) collective-permute-start(bf16[32,3712]{1,0:T(8,128)(2,1)S(1)} %block.1.refs_0_), channel_id=1, source_target_pairs={{0,32},{8,40},{16,48},{24,56},{32,64},{40,72},{48,80},{56,88},{64,... | collective-permute-start | bytes 712712 | tf_op jit(solution)/shard_map/ppermute | solution.py:52
  11.9 2.2 collective-permute-start.2
  14.1 2.7 %collective-permute-start = (bf16[32,3712]{1,0:T(8,128)(2,1)S(1)}, bf16[32,3712]{1,0:T(8,128)(2,1)S(1)}, u32[]{:S(2)}, u32[]{:S(2)}) collective-permute-start(bf16[32,3712]{1,0:T(8,128)(2,1)S(1)} %block.1.refs_0_), channel_id=1, source_target_pairs={{0,16},{8,24},{16,0},{24,8},{32,48},{40,56},{48,32},{56,40},{64,80... | collective-permute-start | bytes 712712 | tf_op jit(solution)/shard_map/ppermute | solution.py:52
  18.1 1.4 collective-permute-done.5.refs_1_
  21.9 1.9 collective-permute-start.9
  24.5 2.8 %collective-permute-start.4 = (bf16[32,3712]{1,0:T(8,128)(2,1)S(1)}, bf16[32,3712]{1,0:T(8,128)(2,1)S(1)}, u32[]{:S(2)}, u32[]{:S(2)}) collective-permute-start(bf16[32,3712]{1,0:T(8,128)(2,1)S(1)} %collective-permute-done.2.refs_2_), channel_id=1, source_target_pairs={{0,16},{8,24},{16,0},{24,8},{32,48},{40,56},{48,32},{56,40},{64,80... | collective-permute-start | bytes 712712 | tf_op jit(solution)/shard_map/ppermute | solution.py:52
  27.3 1.4 collective-permute-start.3
  29.5 3.1 %copy-done.15 = bf16[1024,3584]{1,0:T(8,128)(2,1)S(1)} copy-done((bf16[1024,3584]{1,0:T(8,128)(2,1)S(1)}, bf16[1024,3584]{1,0:T(8,128)(2,1)}, u32[]{:S(2)}) %copy-start.15) | copy-done | bytes 7340056
  32.6 3.8 %first_scores.1 = (bf16[8,3584]{1,0:T(8,128)(2,1)S(1)}, f32[1024,256]{1,0:T(8,128)S(1)}, bf16[256,3584]{1,0:T(8,128)(2,1)S(1)}, f32[8,256]{1,0:T(8,128)S(1)}, s3...) custom-call(s32[1]{0:T(128)} %bitcast.1.blk_ref, bf16[32,3712]{1,0:T(8,128)(2,1)S(1)} %block.1.refs_0_, ...), custom_call_target="tpu_custom_call" | custom-call | flops 3758096384 | bytes 14680064 | tf_op jit(solution)/shard_map/first_scores/pallas_call | solution.py:433
  40.8 3.2 %collective-permute-done.11.refs_4_ = bf16[16,3712]{1,0:T(8,128)(2,1)S(1)} collective-permute-done((bf16[16,3712]{1,0:T(8,128)(2,1)S(1)}, bf16[16,3712]{1,0:T(8,128)(2,1)S(1)}, u32[]{:S(2)}, u32[]{:S(2)}) %collective-permute-start.11) | collective-permute-done | bytes 118816 | tf_op jit(solution)/shard_map/ppermute | solution.py:52
  44.0 2.0 collective-permute-start.16
  47.3 5.6 %second_scores.1 = (f32[8,512]{1,0:T(8,128)S(1)}, bf16[8,96,512]{2,1,0:T(8,128)(2,1)S(1)}, bf16[512,512]{1,0:T(8,128)(2,1)S(1)}, f32[1024,256]{1,0:T(8,128)S(1)}...) custom-call(s32[1]{0:T(128)} %bitcast.1.blk_ref, bf16[32,3712]{1,0:T(8,128)(2,1)S(1)} %collective-permute-done.1.refs_0_, ...), custom_call_target="tpu_custom_call" | custom-call | flops 3758096384 | bytes 14680064 | tf_op jit(solution)/shard_map/second_scores/pallas_call | solution.py:452
  55.1 1.3 reshape.26
  56.4 7.9 %all-to-all-start = ((bf16[128,6,512]{2,1,0:T(8,128)(2,1)}), bf16[128,6,512]{2,1,0:T(8,128)(2,1)S(1)}, u32[]{:S(2)}, u32[]{:S(2)}) async-start(bf16[128,6,512]{2,1,0:T(8,128)(2,1)} %reshape.26), calls=%async_computation | async-start | bytes 2097152 | tf_op jit(solution)/shard_map/all_to_all | solution.py:409
  64.4 3.2 %collective-permute-start.19 = (f32[8,512]{1,0:T(8,128)S(1)}, f32[8,512]{1,0:T(8,128)S(1)}, u32[]{:S(2)}, u32[]{:S(2)}) collective-permute-start(f32[8,512]{1,0:T(8,128)S(1)} %get-tuple-element.45.refs_0_), channel_id=1, source_target_pairs={{0,24},{8,16},{16,8},{24,0},{32,56},{40,48},{48,40},{56,32},{64,88... | collective-permute-start | bytes 49160 | tf_op jit(solution)/shard_map/ppermute | solution.py:52
  68.4 11.2 %collective-permute-done.19.refs_3_ = f32[8,512]{1,0:T(8,128)S(1)} collective-permute-done((f32[8,512]{1,0:T(8,128)S(1)}, f32[8,512]{1,0:T(8,128)S(1)}, u32[]{:S(2)}, u32[]{:S(2)}) %collective-permute-start.19) | collective-permute-done | bytes 16416 | tf_op jit(solution)/shard_map/ppermute | solution.py:52
  79.6 3.2 %collective-permute-start.22 = (f32[8,512]{1,0:T(8,128)S(1)}, f32[8,512]{1,0:T(8,128)S(1)}, u32[]{:S(2)}, u32[]{:S(2)}) collective-permute-start(f32[8,512]{1,0:T(8,128)S(1)} %merge.2.refs_0_), channel_id=1, source_target_pairs={{0,96},{8,104},{16,112},{24,120},{32,0},{40,8},{48,16},{56,24},{64... | collective-permute-start | bytes 49160 | tf_op jit(solution)/shard_map/ppermute | solution.py:52
  83.6 3.2 %collective-permute-done.21.refs_2_ = f32[8,512]{1,0:T(8,128)S(1)} collective-permute-done((f32[8,512]{1,0:T(8,128)S(1)}, f32[8,512]{1,0:T(8,128)S(1)}, u32[]{:S(2)}, u32[]{:S(2)}) %collective-permute-start.21) | collective-permute-done | bytes 16416 | tf_op jit(solution)/shard_map/ppermute | solution.py:52
  86.9 8.8 %passage_terms.1 = (f32[1,512]{1,0:T(1,128)S(1)}, bf16[1024,2560]{1,0:T(8,128)(2,1)}, bf16[512,1024]{1,0:T(8,128)(2,1)S(1)}, bf16[512,1024]{1,0:T(8,128)(2,1)}) custom-call(s32[1]{0:T(128)} %bitcast.grp_ref, f32[8,512]{1,0:T(8,128)S(1)} %merge.3.stats_ref, s32[1,256]{1,0:T(1,128)S(1)} %get-tuple-element.46.pos_a, s32[1,256]{1,0:T(1,128)S(1)} %get-tuple-element.47.pos_b, ...), custom_call_target="tpu_custom_call" | custom-call | flops 3758096384 | bytes 14680064 | tf_op jit(solution)/shard_map/passage_terms/pallas_call | solution.py:288
  97.8 13.9 %all_to_all.25.cot_ref = bf16[16,16,448]{2,1,0:T(8,128)(2,1)S(1)} all-to-all(bf16[16,16,448]{2,1,0:T(8,128)(2,1)S(1)} %cotangents.1), channel_id=1, replica_groups=mesh['blk'=16,'grp'=8] {'blk'}, dimensions={0} | all-to-all | bytes 458752 | tf_op jit(solution)/shard_map/all_to_all | solution.py:409
  114.2 1.4 act.1
  115.7 1.3 copy-done
  116.9 5.0 %all-to-all-start.2 = ((bf16[8,96,1240]{2,1,0:T(8,128)(2,1)}), bf16[8,96,1240]{2,1,0:T(8,128)(2,1)S(1)}, u32[]{:S(2)}, u32[]{:S(2)}) async-start(bf16[8,96,1240]{2,1,0:T(8,128)(2,1)} %copy-done), calls=%async_computation.2 | async-start | bytes 3932160 | tf_op jit(solution)/shard_map/all_to_all | solution.py:409
  122.0 1.4 collective-permute-start.23
  123.4 30.6 %all-to-all-done.2.got_ref = bf16[8,96,1240]{2,1,0:T(8,128)(2,1)S(1)} async-done(((bf16[8,96,1240]{2,1,0:T(8,128)(2,1)}), bf16[8,96,1240]{2,1,0:T(8,128)(2,1)S(1)}, u32[]{:S(2)}, u32[]{:S(2)}) %all-to-all-start.2) | async-done | bytes 1904672 | tf_op jit(solution)/shard_map/all_to_all | solution.py:409
  154.6 12.2 %collective-permute-done.23.got_ref = bf16[512,1024]{1,0:T(8,128)(2,1)} collective-permute-done((bf16[512,1024]{1,0:T(8,128)(2,1)}, bf16[512,1024]{1,0:T(8,128)(2,1)}, u32[]{:S(2)}, u32[]{:S(2)}) %collective-permute-start.23) | collective-permute-done | bytes 1048608 | tf_op jit(solution)/shard_map/ppermute | solution.py:333
  166.8 1.5 x_sum.1
  169.3 19.7 %all_to_all.26.grad_ref = bf16[8,64,1184]{2,1,0:T(8,128)(2,1)S(1)} all-to-all(bf16[8,64,1184]{2,1,0:T(8,128)(2,1)} %copy-done.6), channel_id=1, replica_groups=mesh['blk'=16,'grp'=8] {'grp'}, dimensions={0} | all-to-all | bytes 2424832 | tf_op jit(solution)/shard_map/all_to_all | solution.py:409
  190.0 1.3 copy-done.5
  193.3 11.8 %all-to-all-start.4 = ((bf16[128,2,448]{2,1,0:T(2,128)(2,1)}), bf16[128,2,448]{2,1,0:T(2,128)(2,1)S(1)}, u32[]{:S(2)}, u32[]{:S(2)}) async-start(bf16[128,2,448]{2,1,0:T(2,128)(2,1)} %reshape.28), calls=%async_computation.6 | async-start | bytes 524288 | tf_op jit(solution)/shard_map/all_to_all | solution.py:409
  205.6 11.4 %all-to-all-done.4 = bf16[128,2,448]{2,1,0:T(2,128)(2,1)S(1)} async-done(((bf16[128,2,448]{2,1,0:T(2,128)(2,1)}), bf16[128,2,448]{2,1,0:T(2,128)(2,1)S(1)}, u32[]{:S(2)}, u32[]{:S(2)}) %all-to-all-start.4) | async-done | bytes 229408 | tf_op jit(solution)/shard_map/all_to_all | solution.py:409
  219.0 1.4 passages.1
  (92 shorter events, 28.5 us)
Async XLA Ops:
  9.3 10.2 %collective-permute-start.5 = (bf16[32,3712]{1,0:T(8,128)(2,1)S(1)}, bf16[32,3712]{1,0:T(8,128)(2,1)S(1)}, u32[]{:S(2)}, u32[]{:S(2)}) collective-permute-start(bf16[32,3712]{1,0:T(8,128)(2,1)S(1)} %block.1.refs_0_), channel_id=1, source_target_pairs={{0,32},{8,40},{16,48},{24,56},{32,64},{40,72},{48,80},{56,88},{64,... | collective-permute-start | bytes 712712 | tf_op jit(solution)/shard_map/ppermute | solution.py:52
  11.9 8.9 %collective-permute-start.2 = (bf16[32,3712]{1,0:T(8,128)(2,1)S(1)}, bf16[32,3712]{1,0:T(8,128)(2,1)S(1)}, u32[]{:S(2)}, u32[]{:S(2)}) collective-permute-start(bf16[32,3712]{1,0:T(8,128)(2,1)S(1)} %block.1.refs_0_), channel_id=1, source_target_pairs={{0,96},{8,104},{16,112},{24,120},{32,0},{40,8},{48,16},{56,24},{64... | collective-permute-start | bytes 712712 | tf_op jit(solution)/shard_map/ppermute | solution.py:52
  14.1 7.8 %collective-permute-start = (bf16[32,3712]{1,0:T(8,128)(2,1)S(1)}, bf16[32,3712]{1,0:T(8,128)(2,1)S(1)}, u32[]{:S(2)}, u32[]{:S(2)}) collective-permute-start(bf16[32,3712]{1,0:T(8,128)(2,1)S(1)} %block.1.refs_0_), channel_id=1, source_target_pairs={{0,16},{8,24},{16,0},{24,8},{32,48},{40,56},{48,32},{56,40},{64,80... | collective-permute-start | bytes 712712 | tf_op jit(solution)/shard_map/ppermute | solution.py:52
  16.8 10.5 %collective-permute-start.6 = (bf16[32,3712]{1,0:T(8,128)(2,1)S(1)}, bf16[32,3712]{1,0:T(8,128)(2,1)S(1)}, u32[]{:S(2)}, u32[]{:S(2)}) collective-permute-start(bf16[32,3712]{1,0:T(8,128)(2,1)S(1)} %block.1.refs_0_), channel_id=1, source_target_pairs={{0,8},{8,0},{16,24},{24,16},{32,40},{40,32},{48,56},{56,48},{64,72... | collective-permute-start | bytes 712712 | tf_op jit(solution)/shard_map/ppermute | solution.py:52
  19.5 9.2 %collective-permute-start.7 = (bf16[32,3712]{1,0:T(8,128)(2,1)S(1)}, bf16[32,3712]{1,0:T(8,128)(2,1)S(1)}, u32[]{:S(2)}, u32[]{:S(2)}) collective-permute-start(bf16[32,3712]{1,0:T(8,128)(2,1)S(1)} %collective-permute-done.5.refs_1_), channel_id=1, source_target_pairs={{0,8},{8,0},{16,24},{24,16},{32,40},{40,32},{48,56},{56,48},{64,72... | collective-permute-start | bytes 712712 | tf_op jit(solution)/shard_map/ppermute | solution.py:52
  20.7 8.1 %collective-permute-start.8 = (bf16[32,3712]{1,0:T(8,128)(2,1)S(1)}, bf16[32,3712]{1,0:T(8,128)(2,1)S(1)}, u32[]{:S(2)}, u32[]{:S(2)}) collective-permute-start(bf16[32,3712]{1,0:T(8,128)(2,1)S(1)} %collective-permute-done.2.refs_2_), channel_id=1, source_target_pairs={{0,8},{8,0},{16,24},{24,16},{32,40},{40,32},{48,56},{56,48},{64,72... | collective-permute-start | bytes 712712 | tf_op jit(solution)/shard_map/ppermute | solution.py:52
  21.9 6.9 %collective-permute-start.9 = (bf16[32,3712]{1,0:T(8,128)(2,1)S(1)}, bf16[32,3712]{1,0:T(8,128)(2,1)S(1)}, u32[]{:S(2)}, u32[]{:S(2)}) collective-permute-start(bf16[32,3712]{1,0:T(8,128)(2,1)S(1)} %collective-permute-done.refs_3_), channel_id=1, source_target_pairs={{0,8},{8,0},{16,24},{24,16},{32,40},{40,32},{48,56},{56,48},{64,72... | collective-permute-start | bytes 712712 | tf_op jit(solution)/shard_map/ppermute | solution.py:52
  24.5 14.1 %collective-permute-start.4 = (bf16[32,3712]{1,0:T(8,128)(2,1)S(1)}, bf16[32,3712]{1,0:T(8,128)(2,1)S(1)}, u32[]{:S(2)}, u32[]{:S(2)}) collective-permute-start(bf16[32,3712]{1,0:T(8,128)(2,1)S(1)} %collective-permute-done.2.refs_2_), channel_id=1, source_target_pairs={{0,16},{8,24},{16,0},{24,8},{32,48},{40,56},{48,32},{56,40},{64,80... | collective-permute-start | bytes 712712 | tf_op jit(solution)/shard_map/ppermute | solution.py:52
  27.3 11.3 %collective-permute-start.3 = (bf16[32,3712]{1,0:T(8,128)(2,1)S(1)}, bf16[32,3712]{1,0:T(8,128)(2,1)S(1)}, u32[]{:S(2)}, u32[]{:S(2)}) collective-permute-start(bf16[32,3712]{1,0:T(8,128)(2,1)S(1)} %collective-permute-done.2.refs_2_), channel_id=1, source_target_pairs={{0,96},{8,104},{16,112},{24,120},{32,0},{40,8},{48,16},{56,24},{64... | collective-permute-start | bytes 712712 | tf_op jit(solution)/shard_map/ppermute | solution.py:52
  28.7 9.9 %collective-permute-start.1 = (bf16[32,3712]{1,0:T(8,128)(2,1)S(1)}, bf16[32,3712]{1,0:T(8,128)(2,1)S(1)}, u32[]{:S(2)}, u32[]{:S(2)}) collective-permute-start(bf16[32,3712]{1,0:T(8,128)(2,1)S(1)} %collective-permute-done.refs_3_), channel_id=1, source_target_pairs={{0,32},{8,40},{16,48},{24,56},{32,64},{40,72},{48,80},{56,88},{64,... | collective-permute-start | bytes 712712 | tf_op jit(solution)/shard_map/ppermute | solution.py:52
  38.7 5.3 %collective-permute-start.11 = (bf16[16,3712]{1,0:T(8,128)(2,1)S(1)}, bf16[16,3712]{1,0:T(8,128)(2,1)S(1)}, u32[]{:S(2)}, u32[]{:S(2)}) collective-permute-start(bf16[16,3712]{1,0:T(8,128)(2,1)S(1)} %slice.10), channel_id=1, source_target_pairs={{0,16},{8,24},{16,0},{24,8},{32,48},{40,56},{48,32},{56,40},{64,80... | collective-permute-start | bytes 356360 | tf_op jit(solution)/shard_map/ppermute | solution.py:52
  39.0 7.0 %collective-permute-start.10 = (bf16[16,3712]{1,0:T(8,128)(2,1)S(1)}, bf16[16,3712]{1,0:T(8,128)(2,1)S(1)}, u32[]{:S(2)}, u32[]{:S(2)}) collective-permute-start(bf16[16,3712]{1,0:T(8,128)(2,1)S(1)} %slice.9), channel_id=1, source_target_pairs={{0,32},{8,40},{16,48},{24,56},{32,64},{40,72},{48,80},{56,88},{64,... | collective-permute-start | bytes 356360 | tf_op jit(solution)/shard_map/ppermute | solution.py:52
  39.1 8.2 %collective-permute-start.14 = (bf16[32,3712]{1,0:T(8,128)(2,1)S(1)}, bf16[32,3712]{1,0:T(8,128)(2,1)S(1)}, u32[]{:S(2)}, u32[]{:S(2)}) collective-permute-start(bf16[32,3712]{1,0:T(8,128)(2,1)S(1)} %collective-permute-done.4.refs_2_), channel_id=1, source_target_pairs={{0,8},{8,0},{16,24},{24,16},{32,40},{40,32},{48,56},{56,48},{64,72... | collective-permute-start | bytes 712712 | tf_op jit(solution)/shard_map/ppermute | solution.py:52
  40.3 7.0 %collective-permute-start.12 = (bf16[32,3712]{1,0:T(8,128)(2,1)S(1)}, bf16[32,3712]{1,0:T(8,128)(2,1)S(1)}, u32[]{:S(2)}, u32[]{:S(2)}) collective-permute-start(bf16[32,3712]{1,0:T(8,128)(2,1)S(1)} %collective-permute-done.1.refs_0_), channel_id=1, source_target_pairs={{0,8},{8,0},{16,24},{24,16},{32,40},{40,32},{48,56},{56,48},{64,72... | collective-permute-start | bytes 712712 | tf_op jit(solution)/shard_map/ppermute | solution.py:52
  40.4 6.9 %collective-permute-start.13 = (bf16[32,3712]{1,0:T(8,128)(2,1)S(1)}, bf16[32,3712]{1,0:T(8,128)(2,1)S(1)}, u32[]{:S(2)}, u32[]{:S(2)}) collective-permute-start(bf16[32,3712]{1,0:T(8,128)(2,1)S(1)} %collective-permute-done.3.refs_1_), channel_id=1, source_target_pairs={{0,8},{8,0},{16,24},{24,16},{32,40},{40,32},{48,56},{56,48},{64,72... | collective-permute-start | bytes 712712 | tf_op jit(solution)/shard_map/ppermute | solution.py:52
  44.0 3.0 %collective-permute-start.16 = (bf16[16,3712]{1,0:T(8,128)(2,1)S(1)}, bf16[16,3712]{1,0:T(8,128)(2,1)S(1)}, u32[]{:S(2)}, u32[]{:S(2)}) collective-permute-start(bf16[16,3712]{1,0:T(8,128)(2,1)S(1)} %collective-permute-done.11.refs_4_), channel_id=1, source_target_pairs={{0,8},{8,0},{16,24},{24,16},{32,40},{40,32},{48,56},{56,48},{64,72... | collective-permute-start | bytes 356360 | tf_op jit(solution)/shard_map/ppermute | solution.py:52
  46.0 1.3 collective-permute-start.15
  56.4 40.3 %all-to-all-start = ((bf16[128,6,512]{2,1,0:T(8,128)(2,1)}), bf16[128,6,512]{2,1,0:T(8,128)(2,1)S(1)}, u32[]{:S(2)}, u32[]{:S(2)}) async-start(bf16[128,6,512]{2,1,0:T(8,128)(2,1)} %reshape.26), calls=%async_computation | async-start | bytes 2097152 | tf_op jit(solution)/shard_map/all_to_all | solution.py:409
  64.3 125.6 %reduce-scatter.3.cloned.1.call-start = ((), (), s32[]{:S(2)}) async-start(), calls=%async_computation.7 | async-start | bytes 6553600 | tf_op jit(solution)/shard_map/reduce_scatter | solution.py:337
  64.4 15.2 %collective-permute-start.19 = (f32[8,512]{1,0:T(8,128)S(1)}, f32[8,512]{1,0:T(8,128)S(1)}, u32[]{:S(2)}, u32[]{:S(2)}) collective-permute-start(f32[8,512]{1,0:T(8,128)S(1)} %get-tuple-element.45.refs_0_), channel_id=1, source_target_pairs={{0,24},{8,16},{16,8},{24,0},{32,56},{40,48},{48,40},{56,32},{64,88... | collective-permute-start | bytes 49160 | tf_op jit(solution)/shard_map/ppermute | solution.py:52
  67.6 12.0 %collective-permute-start.18 = (f32[8,512]{1,0:T(8,128)S(1)}, f32[8,512]{1,0:T(8,128)S(1)}, u32[]{:S(2)}, u32[]{:S(2)}) collective-permute-start(f32[8,512]{1,0:T(8,128)S(1)} %get-tuple-element.45.refs_0_), channel_id=1, source_target_pairs={{0,8},{8,0},{16,24},{24,16},{32,40},{40,32},{48,56},{56,48},{64,72... | collective-permute-start | bytes 49160 | tf_op jit(solution)/shard_map/ppermute | solution.py:52
  67.7 11.8 %collective-permute-start.17 = (f32[8,512]{1,0:T(8,128)S(1)}, f32[8,512]{1,0:T(8,128)S(1)}, u32[]{:S(2)}, u32[]{:S(2)}) collective-permute-start(f32[8,512]{1,0:T(8,128)S(1)} %get-tuple-element.45.refs_0_), channel_id=1, source_target_pairs={{0,16},{8,24},{16,0},{24,8},{32,48},{40,56},{48,32},{56,40},{64,80... | collective-permute-start | bytes 49160 | tf_op jit(solution)/shard_map/ppermute | solution.py:52
  79.6 4.0 %collective-permute-start.22 = (f32[8,512]{1,0:T(8,128)S(1)}, f32[8,512]{1,0:T(8,128)S(1)}, u32[]{:S(2)}, u32[]{:S(2)}) collective-permute-start(f32[8,512]{1,0:T(8,128)S(1)} %merge.2.refs_0_), channel_id=1, source_target_pairs={{0,96},{8,104},{16,112},{24,120},{32,0},{40,8},{48,16},{56,24},{64... | collective-permute-start | bytes 49160 | tf_op jit(solution)/shard_map/ppermute | solution.py:52
  82.7 4.1 %collective-permute-start.21 = (f32[8,512]{1,0:T(8,128)S(1)}, f32[8,512]{1,0:T(8,128)S(1)}, u32[]{:S(2)}, u32[]{:S(2)}) collective-permute-start(f32[8,512]{1,0:T(8,128)S(1)} %merge.2.refs_0_), channel_id=1, source_target_pairs={{0,64},{8,72},{16,80},{24,88},{32,96},{40,104},{48,112},{56,120},{... | collective-permute-start | bytes 49160 | tf_op jit(solution)/shard_map/ppermute | solution.py:52
  82.8 4.0 %collective-permute-start.20 = (f32[8,512]{1,0:T(8,128)S(1)}, f32[8,512]{1,0:T(8,128)S(1)}, u32[]{:S(2)}, u32[]{:S(2)}) collective-permute-start(f32[8,512]{1,0:T(8,128)S(1)} %merge.2.refs_0_), channel_id=1, source_target_pairs={{0,32},{8,40},{16,48},{24,56},{32,64},{40,72},{48,80},{56,88},{64,... | collective-permute-start | bytes 49160 | tf_op jit(solution)/shard_map/ppermute | solution.py:52
  116.9 37.1 %all-to-all-start.2 = ((bf16[8,96,1240]{2,1,0:T(8,128)(2,1)}), bf16[8,96,1240]{2,1,0:T(8,128)(2,1)S(1)}, u32[]{:S(2)}, u32[]{:S(2)}) async-start(bf16[8,96,1240]{2,1,0:T(8,128)(2,1)} %copy-done), calls=%async_computation.2 | async-start | bytes 3932160 | tf_op jit(solution)/shard_map/all_to_all | solution.py:409
  121.9 96.1 %reduce-scatter.5.cloned.1.call-start = ((), (), s32[]{:S(2)}) async-start(), calls=%async_computation.8 | async-start | bytes 1310720 | tf_op jit(solution)/shard_map/reduce_scatter | solution.py:337
  122.0 44.9 %collective-permute-start.23 = (bf16[512,1024]{1,0:T(8,128)(2,1)}, bf16[512,1024]{1,0:T(8,128)(2,1)}, u32[]{:S(2)}, u32[]{:S(2)}) collective-permute-start(bf16[512,1024]{1,0:T(8,128)(2,1)} %get-tuple-element.59), channel_id=1, source_target_pairs={{0,4},{1,5},{2,6},{3,7},{4,0},{5,1},{6,2},{7,3},{8,12},{9,13},{10,... | collective-permute-start | bytes 3145736 | tf_op jit(solution)/shard_map/ppermute | solution.py:333
  169.3 19.8 %copy-start.3 = (bf16[448,1184]{1,0:T(8,128)(2,1)S(1)}, bf16[448,1184]{1,0:T(8,128)(2,1)}, u32[]{:S(2)}) copy-start(bf16[448,1184]{1,0:T(8,128)(2,1)} %up_ref.3) | copy-start | bytes 3182596
  191.3 25.8 %copy-start.13 = (bf16[2,3584]{1,0:T(2,128)(2,1)S(1)}, bf16[2,3584]{1,0:T(2,128)(2,1)}, u32[]{:S(2)}) copy-start(bf16[2,3584]{1,0:T(2,128)(2,1)} %hidden_ref.1) | copy-start | bytes 43012
  191.6 26.4 %collective-permute-start.24 = (bf16[128,2560]{1,0:T(8,128)(2,1)S(1)}, bf16[128,2560]{1,0:T(8,128)(2,1)S(1)}, u32[]{:S(2)}, u32[]{:S(2)}) collective-permute-start(bf16[128,2560]{1,0:T(8,128)(2,1)S(1)} %get-tuple-element.69), channel_id=1, source_target_pairs={{0,4},{1,5},{2,6},{3,7},{4,0},{5,1},{6,2},{7,3},{8,12},{9,13},{10,... | collective-permute-start | bytes 1966088 | tf_op jit(solution)/shard_map/ppermute | solution.py:333
  193.3 23.7 %all-to-all-start.4 = ((bf16[128,2,448]{2,1,0:T(2,128)(2,1)}), bf16[128,2,448]{2,1,0:T(2,128)(2,1)S(1)}, u32[]{:S(2)}, u32[]{:S(2)}) async-start(bf16[128,2,448]{2,1,0:T(2,128)(2,1)} %reshape.28), calls=%async_computation.6 | async-start | bytes 524288 | tf_op jit(solution)/shard_map/all_to_all | solution.py:409
  (18 other events, 56.8 us)
Sparse Core Ops, SparseCore 0:
  97.9 76.2 reduce-scatter.2
  176.6 25.4 reduce-scatter.4
